TPU v7x, 32 devices: a whole 2x2x4 slice. The times are simulated.
32 devices in a mesh: fsdp: 16 (over z, x, core), seq: 2 (over y).
Axes of the slice: x: 2, y: 2, z: 4, core: 2. Of those that a mesh axis runs over, the one named last changes fastest.
Arguments:
- tokens: bfloat16 [16, 1024, 1152], P('fsdp', 'seq'), may hold values from -6 to 6
- lengths: int32 [16], P('fsdp'), may hold values from 128 to 1024, as said below
- cotangent: bfloat16 [16, 1024, 1152], P('fsdp', 'seq'), may hold values from -6 to 6
- attn_gain: float32 [1152], replicated, may hold values from 0.25 to 1.75
- attn_shift: float32 [1152], replicated, may hold values from -2 to 2
- qkv_weight: bfloat16 [1152, 3456], P('fsdp'), may hold values from -0.1875 to 0.1875
- query_bias: float32 [1152], replicated, may hold values from -3 to 3
- value_bias: float32 [1152], replicated, may hold values from -3 to 3
- out_weight: bfloat16 [1152, 1152], P('fsdp'), may hold values from -3 to 3
- out_bias: float32 [1152], replicated, may hold values from -2 to 2
- mlp_gain: float32 [1152], replicated, may hold values from 0.25 to 1.75
- mlp_shift: float32 [1152], replicated, may hold values from -2 to 2
- up_weight: bfloat16 [1152, 4304], P('fsdp'), may hold values from -0.1875 to 0.1875
- up_bias: float32 [4304], replicated, may hold values from -3 to 3
- down_weight: bfloat16 [4304, 1152], P(None, 'fsdp'), may hold values from -0.09375 to 0.09375
- down_bias: float32 [1152], replicated, may hold values from -2 to 2
Outputs:
- outputs: bfloat16 [16, 1024, 1152], P('fsdp', 'seq')
- grad_tokens: float32 [16, 1024, 1152], P('fsdp', 'seq')
- grad_attn_gain: float32 [1152], replicated
- grad_attn_shift: float32 [1152], replicated
- grad_qkv: float32 [1152, 3456], P('fsdp')
- grad_query_bias: float32 [1152], replicated
- grad_value_bias: float32 [1152], replicated
- grad_out: float32 [1152, 1152], P('fsdp')
- grad_out_bias: float32 [1152], replicated
- grad_mlp_gain: float32 [1152], replicated
- grad_mlp_shift: float32 [1152], replicated
- grad_up: float32 [1152, 4304], P('fsdp')
- grad_up_bias: float32 [4304], replicated
- grad_down: float32 [4304, 1152], P(None, 'fsdp')
- grad_down_bias: float32 [1152], replicated
Inputs may be any that keep to these rules, and one draw needn't show every extreme that they name: `lengths`: of the 1 images of each fsdp index, one has at least 960 valid tokens.
All inputs are finite; a program needn't handle non-finite values.
Results may differ from a plain program's by a relative error of at most 0.015.
Values may be sent and summed in bfloat16 or wider, within the bound.
No kernel may reach another device: no remote copies, remote signals or barrier semaphores. Data moves between devices by JAX's collectives and lax.ppermute only.
A program may use at most 256 MiB of HBM per device.

v0:
```python
import jax
import jax.numpy as jnp
from jax import lax
from jax.sharding import PartitionSpec as P

HD = 72


epsilon = 1e-06
masked_score = -1e30


def norm_layer(tensor, gain_vec, shift_vec):
    centered = tensor - jnp.mean(tensor, axis=-1, keepdims=True)
    variance = jnp.mean(centered * centered, axis=-1, keepdims=True)
    return centered * lax.rsqrt(variance + epsilon) * gain_vec + shift_vec


def gelu_tanh(tensor):
    return (
        0.5
        * tensor
        * (1.0 + jnp.tanh(0.7978845608028654 * (tensor + 0.044715 * tensor * tensor * tensor)))
    )


def contract_rows(left_rows, right_rows):
    return lax.dot_general(
        left_rows, right_rows, (((0,), (0,)), ((), ())), preferred_element_type=jnp.float32
    )


def times_transpose(left_rows, matrix):
    return lax.dot_general(
        left_rows, matrix, (((1,), (1,)), ((), ())), preferred_element_type=jnp.float32
    )


def column_sum(tensor):
    return jnp.sum(tensor.astype(jnp.float32), axis=0)


def body(
    tokens,
    lengths,
    cotangent,
    attn_gain,
    attn_shift,
    qkv_weight,
    query_bias,
    value_bias,
    out_weight,
    out_bias,
    mlp_gain,
    mlp_shift,
    up_weight,
    up_bias,
    down_weight,
    down_bias,
):
    groups = lax.axis_size("seq")
    images, local_len, model_width = tokens.shape
    full_len = local_len * groups
    row_count = images * local_len
    head_width = model_width // groups
    heads_here = head_width // HD
    block_rows = min(512, full_len)
    block_count = full_len // block_rows
    scaling = HD ** (-0.5)
    positions = lax.broadcasted_iota(jnp.int32, (images, full_len), 1)
    key_mask = (positions < lengths[:, None])[:, None, None, :]
    full_qkv, full_out, full_up, full_down = (
        lax.all_gather(qkv_weight, "fsdp", axis=0, tiled=True),
        lax.all_gather(out_weight, "fsdp", axis=0, tiled=True),
        lax.all_gather(up_weight, "fsdp", axis=0, tiled=True),
        lax.all_gather(down_weight, "fsdp", axis=1, tiled=True),
    )
    inputs = tokens.reshape(row_count, model_width).astype(jnp.float32)
    normed_one = norm_layer(inputs, attn_gain, attn_shift).astype(jnp.bfloat16)
    projected = jnp.dot(normed_one, full_qkv, preferred_element_type=jnp.float32)
    queries = (projected[:, :model_width] + query_bias).astype(jnp.bfloat16)
    keys_local = projected[:, model_width : 2 * model_width].astype(jnp.bfloat16)
    values_local = (projected[:, 2 * model_width :] + value_bias).astype(jnp.bfloat16)
    layout = (images, local_len, groups, head_width)
    arrived = (
        lax.all_to_all(queries.reshape(layout), "seq", split_axis=2, concat_axis=1, tiled=True),
        lax.all_to_all(keys_local.reshape(layout), "seq", split_axis=2, concat_axis=1, tiled=True),
        lax.all_to_all(
            values_local.reshape(layout), "seq", split_axis=2, concat_axis=1, tiled=True
        ),
    )
    query_heads, key_heads, value_heads = (
        member.reshape(images, full_len, heads_here, HD) for member in arrived
    )

    def masked_scores(query_block):
        raw_scores = jnp.einsum(
            "ibhd,ijhd->ihbj", query_block, key_heads, preferred_element_type=jnp.float32
        )
        return jnp.where(key_mask, raw_scores * scaling, masked_score)

    attended_parts = []
    lse_parts = []
    for block_index in range(block_count):
        first_row = block_index * block_rows
        scores = masked_scores(query_heads[:, first_row : first_row + block_rows])
        row_peak = jnp.max(scores, axis=-1, keepdims=True)
        exponent = jnp.exp(scores - row_peak)
        row_total = jnp.sum(exponent, axis=-1, keepdims=True)
        weights = (exponent / row_total).astype(jnp.bfloat16)
        attended_parts.append(
            jnp.einsum(
                "ihbj,ijhd->ibhd", weights, value_heads, preferred_element_type=jnp.float32
            ).astype(jnp.bfloat16)
        )
        lse_parts.append(row_peak + jnp.log(row_total))
    attended_heads = jnp.concatenate(attended_parts, axis=1)
    attended = lax.all_to_all(
        attended_heads.reshape(images, full_len, 1, head_width),
        "seq",
        split_axis=1,
        concat_axis=2,
        tiled=True,
    ).reshape(row_count, model_width)
    resid_one = inputs + jnp.dot(attended, full_out, preferred_element_type=jnp.float32) + out_bias
    normed_two = norm_layer(resid_one, mlp_gain, mlp_shift).astype(jnp.bfloat16)
    hidden = jnp.dot(normed_two, full_up, preferred_element_type=jnp.float32) + up_bias
    active = gelu_tanh(hidden).astype(jnp.bfloat16)
    final = resid_one + jnp.dot(active, full_down, preferred_element_type=jnp.float32) + down_bias
    outputs = final.astype(jnp.bfloat16).reshape(images, local_len, model_width)
    qkv_again, out_again, up_again, down_again = (
        lax.all_gather(qkv_weight, "fsdp", axis=0, tiled=True),
        lax.all_gather(out_weight, "fsdp", axis=0, tiled=True),
        lax.all_gather(up_weight, "fsdp", axis=0, tiled=True),
        lax.all_gather(down_weight, "fsdp", axis=1, tiled=True),
    )
    back_low = cotangent.reshape(row_count, model_width)
    back_grad = back_low.astype(jnp.float32)
    grad_down_bias = column_sum(back_low)
    grad_down = contract_rows(active, back_low)
    d_active = times_transpose(back_low, down_again)
    gelu_pull = jax.vjp(gelu_tanh, hidden)[1]
    d_hidden = gelu_pull(d_active)[0].astype(jnp.bfloat16)
    grad_up_bias = column_sum(d_hidden)
    grad_up = contract_rows(normed_two, d_hidden)
    d_two = times_transpose(d_hidden, up_again)
    norm_pull_two = jax.vjp(norm_layer, resid_one, mlp_gain, mlp_shift)[1]
    d_resid, grad_mlp_gain, grad_mlp_shift = norm_pull_two(d_two)
    d_resid = d_resid + back_grad
    out_low = d_resid.astype(jnp.bfloat16)
    grad_out_bias = column_sum(out_low)
    grad_out = contract_rows(attended, out_low)
    d_attended = times_transpose(out_low, out_again).astype(jnp.bfloat16)
    d_heads = lax.all_to_all(
        d_attended.reshape(layout), "seq", split_axis=2, concat_axis=1, tiled=True
    ).reshape(images, full_len, heads_here, HD)
    query_parts = []
    d_key = jnp.zeros((images, full_len, heads_here, HD), jnp.float32)
    d_value = jnp.zeros((images, full_len, heads_here, HD), jnp.float32)
    for block_index in range(block_count):
        first_row = block_index * block_rows
        query_block = query_heads[:, first_row : first_row + block_rows]
        grad_block = d_heads[:, first_row : first_row + block_rows]
        probs = jnp.exp(masked_scores(query_block) - lse_parts[block_index])
        d_probs = jnp.einsum(
            "ibhd,ijhd->ihbj", grad_block, value_heads, preferred_element_type=jnp.float32
        )
        row_dot = jnp.sum(probs * d_probs, axis=-1, keepdims=True)
        d_scores = (probs * (d_probs - row_dot)).astype(jnp.bfloat16)
        query_parts.append(
            jnp.einsum("ihbj,ijhd->ibhd", d_scores, key_heads, preferred_element_type=jnp.float32)
            * scaling
        )
        d_key = (
            d_key
            + jnp.einsum(
                "ihbj,ibhd->ijhd", d_scores, query_block, preferred_element_type=jnp.float32
            )
            * scaling
        )
        d_value = d_value + jnp.einsum(
            "ihbj,ibhd->ijhd",
            probs.astype(jnp.bfloat16),
            grad_block,
            preferred_element_type=jnp.float32,
        )
    d_query = jnp.concatenate(query_parts, axis=1)
    back_shape = (images, full_len, 1, head_width)
    returned = (
        lax.all_to_all(
            d_query.astype(jnp.bfloat16).reshape(back_shape),
            "seq",
            split_axis=1,
            concat_axis=2,
            tiled=True,
        ),
        lax.all_to_all(
            d_key.astype(jnp.bfloat16).reshape(back_shape),
            "seq",
            split_axis=1,
            concat_axis=2,
            tiled=True,
        ),
        lax.all_to_all(
            d_value.astype(jnp.bfloat16).reshape(back_shape),
            "seq",
            split_axis=1,
            concat_axis=2,
            tiled=True,
        ),
    )
    query_rows, key_rows, value_rows = (
        member.reshape(row_count, model_width) for member in returned
    )
    grad_query_bias = column_sum(query_rows)
    grad_value_bias = column_sum(value_rows)
    d_projected = jnp.concatenate([query_rows, key_rows, value_rows], axis=1)
    grad_qkv = contract_rows(normed_one, d_projected)
    d_one = times_transpose(d_projected, qkv_again)
    norm_pull_one = jax.vjp(norm_layer, inputs, attn_gain, attn_shift)[1]
    d_inputs, grad_attn_gain, grad_attn_shift = norm_pull_one(d_one)
    grad_tokens = (d_inputs + d_resid).reshape(images, local_len, model_width)
    shards = (
        lax.psum_scatter(
            grad_qkv.astype(jnp.bfloat16), "fsdp", scatter_dimension=0, tiled=True
        ).astype(jnp.float32),
        lax.psum_scatter(
            grad_out.astype(jnp.bfloat16), "fsdp", scatter_dimension=0, tiled=True
        ).astype(jnp.float32),
        lax.psum_scatter(
            grad_up.astype(jnp.bfloat16), "fsdp", scatter_dimension=0, tiled=True
        ).astype(jnp.float32),
        lax.psum_scatter(
            grad_down.astype(jnp.bfloat16), "fsdp", scatter_dimension=1, tiled=True
        ).astype(jnp.float32),
    )
    narrow = (
        lax.psum_scatter(
            shards[0].astype(jnp.bfloat16), "seq", scatter_dimension=1, tiled=True
        ).astype(jnp.float32),
        lax.psum_scatter(
            shards[1].astype(jnp.bfloat16), "seq", scatter_dimension=1, tiled=True
        ).astype(jnp.float32),
        lax.psum_scatter(
            shards[2].astype(jnp.bfloat16), "seq", scatter_dimension=1, tiled=True
        ).astype(jnp.float32),
        lax.psum_scatter(
            shards[3].astype(jnp.bfloat16), "seq", scatter_dimension=0, tiled=True
        ).astype(jnp.float32),
    )
    grad_qkv, grad_out, grad_up, grad_down = (
        lax.all_gather(narrow[0].astype(jnp.bfloat16), "seq", axis=1, tiled=True).astype(
            jnp.float32
        ),
        lax.all_gather(narrow[1].astype(jnp.bfloat16), "seq", axis=1, tiled=True).astype(
            jnp.float32
        ),
        lax.all_gather(narrow[2].astype(jnp.bfloat16), "seq", axis=1, tiled=True).astype(
            jnp.float32
        ),
        lax.all_gather(narrow[3].astype(jnp.bfloat16), "seq", axis=0, tiled=True).astype(
            jnp.float32
        ),
    )
    (
        grad_attn_gain,
        grad_attn_shift,
        grad_query_bias,
        grad_value_bias,
        grad_out_bias,
        grad_mlp_gain,
        grad_mlp_shift,
        grad_up_bias,
        grad_down_bias,
    ) = lax.psum(
        (
            grad_attn_gain,
            grad_attn_shift,
            grad_query_bias,
            grad_value_bias,
            grad_out_bias,
            grad_mlp_gain,
            grad_mlp_shift,
            grad_up_bias,
            grad_down_bias,
        ),
        ("fsdp", "seq"),
    )
    return (
        outputs,
        grad_tokens,
        grad_attn_gain,
        grad_attn_shift,
        grad_qkv,
        grad_query_bias,
        grad_value_bias,
        grad_out,
        grad_out_bias,
        grad_mlp_gain,
        grad_mlp_shift,
        grad_up,
        grad_up_bias,
        grad_down,
        grad_down_bias,
    )


def solution(mesh):
    return jax.shard_map(
        body,
        mesh=mesh,
        in_specs=(
            P("fsdp", "seq", None),
            P("fsdp"),
            P("fsdp", "seq", None),
            P(),
            P(),
            P("fsdp", None),
            P(),
            P(),
            P("fsdp", None),
            P(),
            P(),
            P(),
            P("fsdp", None),
            P(),
            P(None, "fsdp"),
            P(),
        ),
        out_specs=(
            P("fsdp", "seq", None),
            P("fsdp", "seq", None),
            P(),
            P(),
            P("fsdp", None),
            P(),
            P(),
            P("fsdp", None),
            P(),
            P(),
            P(),
            P("fsdp", None),
            P(),
            P(None, "fsdp"),
            P(),
        ),
        check_vma=False,
    )
```

profile of v0, /device:TPU:0, one launch (start us, length us, event | category | flops | bytes accessed | tf_op | source)
XLA Modules:
  0.0 1005.5 jit_solution(1089655962664451311)
XLA Ops:
  11.3 73.8 %all-gather.9.cloned.1.call-done = bf16[1152,3456]{1,0:T(8,128)(2,1)} async-done(((bf16[72,3456]{1,0:T(8,128)(2,1)}), bf16[1152,3456]{1,0:T(8,128)(2,1)}) %all-gather.9.cloned.1.call-update) | async-done | bytes 7962640 | tf_op jit(solution)/shard_map/all_gather | solution.py:73
  85.2 7.7 fusion.59
  97.4 4.5 all-to-all-start.2
  106.0 11.6 %all-to-all-done.2 = bf16[1,512,2,576]{1,3,0,2:T(8,128)(2,1)} async-done(((bf16[1,512,2,576]{1,3,0,2:T(8,128)(2,1)}), bf16[1,512,2,576]{1,3,0,2:T(8,128)(2,1)}, u32[]{:S(2)}, u32[]{:S(2)}) %all-to-all-start.2) | async-done | bytes 1179680 | tf_op jit(solution)/shard_map/all_to_all | solution.py:87
  122.7 13.4 %all-to-all-done.1 = bf16[1,512,2,576]{1,3,0,2:T(8,128)(2,1)S(1)} async-done(((bf16[1,512,2,576]{1,3,0,2:T(8,128)(2,1)}), bf16[1,512,2,576]{1,3,0,2:T(8,128)(2,1)S(1)}, u32[]{:S(2)}, u32[]{:S(2)}) %all-to-all-start.1) | async-done | bytes 1179680 | tf_op jit(solution)/shard_map/all_to_all | solution.py:86
  136.1 4.5 all-to-all-start
  162.2 8.8 fusion.65
  173.9 13.6 %fusion.1 = f32[8,512]{1,0:T(8,128)S(1)} fusion(f32[8,512,1024]{2,1,0:T(8,128)} %get-tuple-element.41, f32[8,512]{1,0:T(8,128)S(1)} %get-tuple-element.40), kind=kLoop, calls=%fused_computation.16 | loop fusion | flops 8384512 | bytes 16809984 | tf_op jit(solution)/shard_map/reduce_sum | solution.py:109
  191.3 7.5 fusion.45
  207.5 9.9 reduce.17
  220.2 17.7 %all_to_all.120 = bf16[2,2,147456]{2,1,0:T(2,128)(2,1)S(1)} all-to-all(bf16[2,2,147456]{2,1,0:T(2,128)(2,1)} %reshape.431), channel_id=1, replica_groups=mesh['fsdp'=16,'seq'=2] {'seq'}, dimensions={0} | all-to-all | bytes 2359296 | tf_op jit(solution)/shard_map/all_to_all | solution.py:118
  253.7 11.3 %convolution_add_fusion = f32[512,4304]{0,1:T(8,128)} fusion(bf16[1152,4304]{1,0:T(8,128)(2,1)} %all-gather.13.cloned.1.call-done, f32[4304]{0:T(1024)} %param.29, f32[512,1152]{1,0:T(8,128)S(1)} %get-tuple-element.45, f32[1152]{0:T(1024)} %param.27, f32[1152]{0:T(1024)} %param.26, f32[512]{0:T(512)} %fusion.55, f32[512]{0:T(512)} %copy-done.37), kind=kOutput, calls=%fused_computation.37 | convolution fusion | flops 5082357760 | bytes 21120832 | tf_op jit(solution)/shard_map/dot_general | solution.py:127
  265.0 35.3 %all-gather.15.cloned.1.call-done = bf16[4304,1152]{0,1:T(8,128)(2,1)} async-done(((bf16[4304,72]{0,1:T(8,128)(2,1)}), bf16[4304,1152]{0,1:T(8,128)(2,1)}) %all-gather.15.cloned.1.call-update) | async-done | bytes 9916432 | tf_op jit(solution)/shard_map/all_gather | solution.py:76
  300.3 19.9 %convert_reduce_fusion = (f32[4304]{0:T(1024)}, bf16[512,4304]{0,1:T(8,128)(2,1)}) fusion(f32[512,4304]{0,1:T(8,128)} %convolution_add_fusion, bf16[4304,1152]{0,1:T(8,128)(2,1)} %all-gather.15.cloned.1.call-done, bf16[1,512,1152]{2,1,0:T(8,128)(2,1)S(1)} %copy-done.21), kind=kOutput, calls=%fused_computation.29 | convolution fusion | flops 5134495744 | bytes 24335168 | tf_op jit(solution)/shard_map/dot_general | solution.py:34
  320.2 9.3 multiply_reduce_fusion.2
  345.2 10.3 %all-to-all-done.4 = bf16[1,512,2,576]{1,3,0,2:T(8,128)(2,1)S(1)} async-done(((bf16[1,512,2,576]{1,3,0,2:T(8,128)(2,1)}), bf16[1,512,2,576]{1,3,0,2:T(8,128)(2,1)S(1)}, u32[]{:S(2)}, u32[]{:S(2)}) %all-to-all-start.4) | async-done | bytes 1179680 | tf_op jit(solution)/shard_map/all_to_all | solution.py:154
  358.6 9.2 fusion.10
  367.9 13.9 %multiply_reduce_fusion = (f32[8,512]{1,0:T(8,128)S(1)}, f32[8,512,1024]{2,1,0:T(8,128)}) fusion(f32[8,512,1024]{2,1,0:T(8,128)} %get-tuple-element.41, f32[8,512]{1,0:T(8,128)S(1)} %copy-done.27, bf16[1024,8,72]{0,2,1:T(8,128)(2,1)} %reshape.382, bf16[1,1024,8,72]{1,3,2,0:T(8,128)(2,1)} %copy-done.18), kind=kOutput, calls=%fused_computation.3 | convolution fusion | flops 616558592 | bytes 35356672 | tf_op jit(solution)/shard_map/ibhd,ijhd->ihbj/dot_general | solution.py:165
  382.1 9.5 multiply_reduce_fusion.1
  391.6 5.3 add_convert_fusion
  396.8 5.3 copy.144
  402.2 10.1 %reduce.18 = bf16[1024,576]{1,0:T(8,128)(2,1)} reduce(bf16[1024,1,1,576]{3,2,1,0:T(2,128)(2,1)S(1)} %bitcast.230, bf16[]{:T(256)} %broadcast.206), dimensions={1,2}, to_apply=%bitcast.177.reduce_sub_computation | reduce | bytes 2359298
  415.8 4.5 all-to-all-start.7
  420.3 12.4 %multiply_convert_fusion = bf16[8,512,1024]{2,1,0:T(8,128)(2,1)S(1)} fusion(f32[8,512,1024]{2,1,0:T(8,128)} %get-tuple-element.50, f32[8,512,1024]{2,1,0:T(8,128)} %get-tuple-element.41, f32[8,512]{1,0:T(8,128)S(1)} %get-tuple-element.49, f32[8,512]{1,0:T(8,128)S(1)} %copy-done.27), kind=kLoop, calls=%fused_computation.2 | loop fusion | flops 16777216 | bytes 41975808 | tf_op jit(solution)/shard_map/convert_element_type | solution.py:169
  438.8 10.3 %multiply_convert_fusion.1 = bf16[8,512,1024]{2,1,0:T(8,128)(2,1)} fusion(f32[8,512,1024]{2,1,0:T(8,128)} %get-tuple-element.48, f32[8,512,1024]{2,1,0:T(8,128)S(1)} %bitcast.224, f32[8,512]{1,0:T(8,128)S(1)} %get-tuple-element.47, f32[8,512]{1,0:T(8,128)S(1)} %log_add_fusion.1), kind=kLoop, calls=%fused_computation.5 | loop fusion | flops 16777216 | bytes 41975808 | tf_op jit(solution)/shard_map/convert_element_type | solution.py:169
  459.7 10.0 reduce.20
  472.1 5.0 fusion.51
  477.0 4.5 all-to-all-start.5
  481.6 6.0 multiply_convert_fusion.3
  487.6 5.3 copy.141
  492.9 10.1 %reduce.19 = bf16[1024,576]{1,0:T(8,128)(2,1)} reduce(bf16[1024,1,1,576]{3,2,1,0:T(2,128)(2,1)S(1)} %bitcast.228, bf16[]{:T(256)} %broadcast.206), dimensions={1,2}, to_apply=%bitcast.179.reduce_sub_computation | reduce | bytes 2359298
  506.5 4.5 all-to-all-start.6
  540.1 10.2 %convolution_convert_fusion.2 = bf16[1152,3456]{1,0:T(8,128)(2,1)} fusion(bf16[512,1152]{0,1:T(8,128)(2,1)S(1)} %bitcast.256, bf16[512,1152]{0,1:T(8,128)(2,1)S(1)} %bitcast.259, bf16[512,1152]{0,1:T(8,128)(2,1)S(1)} %bitcast.258, bf16[1,512,1152]{2,1,0:T(8,128)(2,1)S(1)} %copy-done.4, f32[1152]{0:T(1024)S(1)} %copy-done.54, f32[1152]{0:T(1024)S(1)} %copy-done.34, ...), kind=kOutput, calls=%fused_computation.14 | convolution fusion | flops 4095000576 | bytes 12694528 | tf_op jit(solution)/shard_map/dot_general | solution.py:28
  551.6 11.0 %convolution_convert_fusion = bf16[4304,1152]{0,1:T(8,128)(2,1)} fusion(bf16[1,512,1152]{2,1,0:T(8,128)(2,1)S(1)} %copy-done.22, f32[512,4304]{0,1:T(8,128)} %convolution_add_fusion), kind=kOutput, calls=%fused_computation | convolution fusion | flops 5101996032 | bytes 19910656 | tf_op jit(solution)/shard_map/dot_general | solution.py:28
  564.5 11.0 %convolution_convert_fusion.1 = bf16[1152,4304]{1,0:T(8,128)(2,1)} fusion(bf16[512,4304]{0,1:T(8,128)(2,1)} %get-tuple-element.53, f32[512,1152]{1,0:T(8,128)S(1)} %copy-done.10, f32[1152]{0:T(1024)} %param.27, f32[1152]{0:T(1024)} %param.26, f32[512]{0:T(512)} %fusion.55, f32[512]{0:T(512)S(1)} %copy-done.39), kind=kOutput, calls=%fused_computation.1 | convolution fusion | flops 5085112320 | bytes 16696320 | tf_op jit(solution)/shard_map/dot_general | solution.py:28
  577.3 13.4 %fusion.26 = bf16[1,512,1152]{2,1,0:T(8,128)(2,1)} fusion(f32[512,1152]{1,0:T(8,128)S(1)} %copy-done.10, bf16[4304,1152]{0,1:T(8,128)(2,1)} %all-gather.15.cloned.1.call-done, f32[1152]{0:T(1024)} %param.31, f32[512,4304]{0,1:T(8,128)} %convolution_add_fusion), kind=kOutput, calls=%fused_computation.57 | convolution fusion | flops 5098807296 | bytes 22274560 | tf_op jit(solution)/shard_map/dot_general | solution.py:129
  592.9 11.5 %fusion.62 = (f32[1152]{0:T(1024)}, f32[512]{0:T(512)}, f32[512,1152]{1,0:T(8,128)}) fusion(f32[1152]{0:T(1024)S(1)} %copy-done.34, f32[512]{0:T(512)S(1)} %copy-done.36, bf16[1,512,1152]{2,1,0:T(8,128)(2,1)S(1)} %copy-done.4, bf16[1152,3456]{1,0:T(8,128)(2,1)} %all-gather.9.cloned.1.call-done, bf16[512,1152]{0,1:T(8,128)(2,1)} %bitcast.255, ...), kind=kOutput, calls=%fused_computation.121 | convolution fusion | flops 4091017728 | bytes 15053824 | tf_op jit(solution)/shard_map/dot_general | solution.py:34
  604.4 45.8 %reduce-scatter.25.cloned.1.call-done = bf16[72,3456]{1,0:T(8,128)(2,1)} async-done(((bf16[1152,3456]{1,0:T(8,128)(2,1)}), bf16[72,3456]{1,0:T(8,128)(2,1)}) %reduce-scatter.25.cloned.1.call-update) | async-done | bytes 497680
  662.8 44.0 %all-reduce.4 = (f32[1152]{0:T(1024)}, f32[1152]{0:T(1024)}, f32[1152]{0:T(1024)}, f32[1152]{0:T(1024)}, f32[1152]{0:T(1024)}, /*index=5*/f32[1152]{0:T(1024)}, f32[1152]{0:T(1024)}, f32[4304]{0:T(1024)}, f32[1152]{0:T(1024)}) all-reduce(f32[1152]{0:T(1024)} %get-tuple-element.17, ...), channel_id=1, replica_groups=mesh['fsdp'=16,'seq'=2] {'fsdp','seq'}, use_global_device_ids=true, to_apply=%region_15.16 | all-reduce | flops 13520 | bytes 108160 | tf_op jit(solution)/shard_map/psum | solution.py:275
  706.7 64.1 %reduce-scatter.19.cloned.1.call-done = bf16[4304,72]{0,1:T(8,128)(2,1)} async-done(((bf16[4304,1152]{0,1:T(8,128)(2,1)}), bf16[4304,72]{0,1:T(8,128)(2,1)}) %reduce-scatter.19.cloned.1.call-update) | async-done | bytes 619792 | tf_op jit(solution)/shard_map/reduce_scatter | solution.py:233
  770.8 119.6 %reduce-scatter.17.cloned.1.call-done = bf16[72,4304]{1,0:T(8,128)(2,1)} async-done(((bf16[1152,4304]{1,0:T(8,128)(2,1)}), bf16[72,4304]{1,0:T(8,128)(2,1)}) %reduce-scatter.17.cloned.1.call-update) | async-done | bytes 619792 | tf_op jit(solution)/shard_map/reduce_scatter | solution.py:230
  894.8 9.0 reduce-scatter.23.cloned.1.call-done
  904.9 5.2 all-gather.1
  911.3 13.8 %reduce-scatter.21.cloned.1.call-done = bf16[1728,72]{1,0:T(8,128)(2,1)} async-done(((bf16[3456,72]{1,0:T(8,128)(2,1)}), bf16[1728,72]{1,0:T(8,128)(2,1)}) %reduce-scatter.21.cloned.1.call-update) | async-done | bytes 248848
  926.3 9.3 all-gather
  937.8 34.8 %all-reduce.8.cloned.1.call-done = (bf16[72,4304]{1,0:T(8,128)(2,1)}, bf16[4304,72]{0,1:T(8,128)(2,1)}) async-done(((bf16[72,4304]{1,0:T(8,128)(2,1)}, bf16[4304,72]{0,1:T(8,128)(2,1)}), (bf16[72,4304]{1,0:T(8,128)(2,1)}, bf16[4304,72]{0,1:T(8,128)(2,1)})) %all-reduce.8.cloned.1.call-update) | async-done | bytes 1239568
  974.8 9.8 all-gather.3
  984.6 8.9 all-gather.2
  (247 shorter events, 182.6 us)
Async XLA Ops:
  7.2 78.0 %copy-start.33 = (f32[1152]{0:T(1024)S(1)}, f32[1152]{0:T(1024)}, u32[]{:S(2)}) copy-start(f32[1152]{0:T(1024)} %param.19) | copy-start | bytes 13828
  7.2 77.9 %copy-start.53 = (f32[1152]{0:T(1024)S(1)}, f32[1152]{0:T(1024)}, u32[]{:S(2)}) copy-start(f32[1152]{0:T(1024)} %param.20) | copy-start | bytes 13828
  7.2 77.9 %all-gather.9.cloned.1.call-start = ((), (), s32[]{:S(2)}) async-start(), calls=%async_computation.14 | async-start | bytes 8460288 | tf_op jit(solution)/shard_map/all_gather | solution.py:73
  7.9 239.7 %all-gather.11.cloned.1.call-start = ((), (), s32[]{:S(2)}) async-start(), calls=%async_computation.15 | async-start | bytes 2820096 | tf_op jit(solution)/shard_map/all_gather | solution.py:74
  8.7 245.0 %all-gather.13.cloned.1.call-start = ((), (), s32[]{:S(2)}) async-start(), calls=%async_computation.16 | async-start | bytes 10653696 | tf_op jit(solution)/shard_map/all_gather | solution.py:75
  9.4 290.8 %all-gather.15.cloned.1.call-start = ((), (), s32[]{:S(2)}) async-start(), calls=%async_computation.17 | async-start | bytes 10653696 | tf_op jit(solution)/shard_map/all_gather | solution.py:76
  10.3 74.9 %copy-start.35 = (f32[512]{0:T(512)}, f32[512]{0:T(512)S(1)}, u32[]{:S(2)}) copy-start(f32[512]{0:T(512)S(1)} %broadcast_multiply_fusion.1) | copy-start | bytes 6148
  11.3 73.8 %copy-start.44 = (f32[512]{0:T(512)}, f32[512]{0:T(512)S(1)}, u32[]{:S(2)}) copy-start(f32[512]{0:T(512)S(1)} %fusion.54) | copy-start | bytes 6148
  97.4 20.2 %all-to-all-start.2 = ((bf16[1,512,2,576]{1,3,0,2:T(8,128)(2,1)}), bf16[1,512,2,576]{1,3,0,2:T(8,128)(2,1)}, u32[]{:S(2)}, u32[]{:S(2)}) async-start(bf16[1,512,2,576]{1,3,0,2:T(8,128)(2,1)} %bitcast.12), calls=%async_computation.2 | async-start | bytes 2359296 | tf_op jit(solution)/shard_map/all_to_all | solution.py:87
  117.6 18.5 %all-to-all-start.1 = ((bf16[1,512,2,576]{1,3,0,2:T(8,128)(2,1)}), bf16[1,512,2,576]{1,3,0,2:T(8,128)(2,1)S(1)}, u32[]{:S(2)}, u32[]{:S(2)}) async-start(bf16[1,512,2,576]{1,3,0,2:T(8,128)(2,1)} %bitcast.244), calls=%async_computation.1 | async-start | bytes 2359296 | tf_op jit(solution)/shard_map/all_to_all | solution.py:86
  136.1 18.6 %all-to-all-start = ((bf16[1,512,2,576]{1,3,0,2:T(8,128)(2,1)}), bf16[1,512,2,576]{1,3,0,2:T(8,128)(2,1)}, u32[]{:S(2)}, u32[]{:S(2)}) async-start(bf16[1,512,2,576]{1,3,0,2:T(8,128)(2,1)} %bitcast.243), calls=%async_computation | async-start | bytes 2359296 | tf_op jit(solution)/shard_map/all_to_all | solution.py:88
  148.8 22.2 %copy-start.5 = (bf16[1024,8,72]{0,2,1:T(8,128)(2,1)}, bf16[1024,8,72]{0,2,1:T(8,128)(2,1)S(1)}, u32[]{:S(2)}) copy-start(bf16[1024,8,72]{0,2,1:T(8,128)(2,1)S(1)} %reshape.387) | copy-start | bytes 3538948
  154.3 16.7 %copy-start.11 = (bf16[1,1024,8,72]{1,3,2,0:T(8,128)(2,1)}, bf16[1,1024,8,72]{1,3,2,0:T(8,128)(2,1)S(1)}, u32[]{:S(2)}) copy-start(bf16[1,1024,8,72]{1,3,2,0:T(8,128)(2,1)S(1)} %reshape.384) | copy-start | bytes 3538948
  162.2 8.8 copy-start.51
  173.9 24.9 %copy-start = (f32[8,512,1024]{2,1,0:T(8,128)}, f32[8,512,1024]{2,1,0:T(8,128)S(1)}, u32[]{:S(2)}) copy-start(f32[8,512,1024]{2,1,0:T(8,128)S(1)} %get-tuple-element.43) | copy-start | bytes 50331652
  173.9 24.9 %copy-start.28 = (f32[8,512]{1,0:T(8,128)}, f32[8,512]{1,0:T(8,128)S(1)}, u32[]{:S(2)}) copy-start(f32[8,512]{1,0:T(8,128)S(1)} %get-tuple-element.42) | copy-start | bytes 49156
  251.8 77.8 %copy-start.9 = (f32[512,1152]{1,0:T(8,128)}, f32[512,1152]{1,0:T(8,128)S(1)}, u32[]{:S(2)}) copy-start(f32[512,1152]{1,0:T(8,128)S(1)} %get-tuple-element.45) | copy-start | bytes 7077892
  253.7 46.5 %copy-start.21 = (bf16[1,512,1152]{2,1,0:T(8,128)(2,1)S(1)}, bf16[1,512,1152]{2,1,0:T(8,128)(2,1)}, u32[]{:S(2)}) copy-start(bf16[1,512,1152]{2,1,0:T(8,128)(2,1)} %param.18) | copy-start | bytes 3538948
  300.3 19.9 %copy-start.38 = (f32[512]{0:T(512)S(1)}, f32[512]{0:T(512)}, u32[]{:S(2)}) copy-start(f32[512]{0:T(512)} %copy-done.37) | copy-start | bytes 6148
  300.3 19.9 %copy-start.49 = (f32[1152]{0:T(1024)S(1)}, f32[1152]{0:T(1024)}, u32[]{:S(2)}) copy-start(f32[1152]{0:T(1024)} %param.26) | copy-start | bytes 13828
  300.3 19.9 %copy-start.50 = (f32[512]{0:T(512)S(1)}, f32[512]{0:T(512)}, u32[]{:S(2)}) copy-start(f32[512]{0:T(512)} %fusion.55) | copy-start | bytes 6148
  300.3 19.9 %copy-start.52 = (bf16[1152,4304]{1,0:T(8,128)(2,1)S(1)}, bf16[1152,4304]{1,0:T(8,128)(2,1)}, u32[]{:S(2)}) copy-start(bf16[1152,4304]{1,0:T(8,128)(2,1)} %all-gather.13.cloned.1.call-done) | copy-start | bytes 29749252
  320.2 9.4 copy-start.42
  336.2 19.3 %all-to-all-start.4 = ((bf16[1,512,2,576]{1,3,0,2:T(8,128)(2,1)}), bf16[1,512,2,576]{1,3,0,2:T(8,128)(2,1)S(1)}, u32[]{:S(2)}, u32[]{:S(2)}) async-start(bf16[1,512,2,576]{1,3,0,2:T(8,128)(2,1)} %bitcast.26), calls=%async_computation.4 | async-start | bytes 2359296 | tf_op jit(solution)/shard_map/all_to_all | solution.py:154
  339.9 250.9 %reduce-scatter.27.cloned.1.call-start = ((), (), s32[]{:S(2)}) async-start(), calls=%async_computation.23 | async-start | bytes 2820096
  358.6 23.1 %slice-start = ((s8[16777216]{0:T(1024)(128)(4,1)}), s8[4194304]{0:T(1024)(128)(4,1)S(1)}, s32[]{:S(2)}) async-start(s8[16777216]{0:T(1024)(128)(4,1)} %bitcast.221), calls=%async_computation.25 | async-start | bytes 8388608
  358.6 23.1 %slice-start.1 = ((s8[16777216]{0:T(1024)(128)(4,1)}), s8[4194304]{0:T(1024)(128)(4,1)S(1)}, s32[]{:S(2)}) async-start(s8[16777216]{0:T(1024)(128)(4,1)} %bitcast.221), calls=%async_computation.26 | async-start | bytes 8388608
  367.9 13.9 %slice-start.2 = ((s8[16777216]{0:T(1024)(128)(4,1)}), s8[4194304]{0:T(1024)(128)(4,1)S(1)}, s32[]{:S(2)}) async-start(s8[16777216]{0:T(1024)(128)(4,1)} %bitcast.221), calls=%async_computation.27 | async-start | bytes 8388608
  367.9 14.2 %slice-start.3 = ((s8[16777216]{0:T(1024)(128)(4,1)}), s8[4194304]{0:T(1024)(128)(4,1)S(1)}, s32[]{:S(2)}) async-start(s8[16777216]{0:T(1024)(128)(4,1)} %bitcast.221), calls=%async_computation.28 | async-start | bytes 8388608
  415.8 61.3 %all-to-all-start.7 = ((bf16[2,2,147456]{2,1,0:T(2,128)(2,1)}), bf16[2,2,147456]{2,1,0:T(2,128)(2,1)}, u32[]{:S(2)}, u32[]{:S(2)}) async-start(bf16[2,2,147456]{2,1,0:T(2,128)(2,1)} %reshape.433), calls=%async_computation.7 | async-start | bytes 2359296 | tf_op jit(solution)/shard_map/all_to_all | solution.py:204
  420.2 12.5 %slice-start.4 = ((s8[16777216]{0:T(1024)(128)(4,1)}), s8[4194304]{0:T(1024)(128)(4,1)S(1)}, s32[]{:S(2)}) async-start(s8[16777216]{0:T(1024)(128)(4,1)} %bitcast.223), calls=%async_computation.29 | async-start | bytes 8388608
  420.3 13.1 %slice-start.5 = ((s8[16777216]{0:T(1024)(128)(4,1)}), s8[4194304]{0:T(1024)(128)(4,1)S(1)}, s32[]{:S(2)}) async-start(s8[16777216]{0:T(1024)(128)(4,1)} %bitcast.223), calls=%async_computation.30 | async-start | bytes 8388608
  420.3 16.2 %slice-start.6 = ((s8[16777216]{0:T(1024)(128)(4,1)}), s8[4194304]{0:T(1024)(128)(4,1)S(1)}, s32[]{:S(2)}) async-start(s8[16777216]{0:T(1024)(128)(4,1)} %bitcast.223), calls=%async_computation.31 | async-start | bytes 8388608
  420.3 18.5 %slice-start.7 = ((s8[16777216]{0:T(1024)(128)(4,1)}), s8[4194304]{0:T(1024)(128)(4,1)S(1)}, s32[]{:S(2)}) async-start(s8[16777216]{0:T(1024)(128)(4,1)} %bitcast.223), calls=%async_computation.32 | async-start | bytes 8388608
  432.7 16.3 %copy-start.1 = (bf16[8,512,1024]{2,1,0:T(8,128)(2,1)}, bf16[8,512,1024]{2,1,0:T(8,128)(2,1)S(1)}, u32[]{:S(2)}) copy-start(bf16[8,512,1024]{2,1,0:T(8,128)(2,1)S(1)} %multiply_convert_fusion) | copy-start | bytes 25165828
  438.8 10.3 %copy-start.6 = (bf16[1024,8,72]{0,2,1:T(8,128)(2,1)S(1)}, bf16[1024,8,72]{0,2,1:T(8,128)(2,1)}, u32[]{:S(2)}) copy-start(bf16[1024,8,72]{0,2,1:T(8,128)(2,1)} %copy-done.5) | copy-start | bytes 3538948
  459.6 12.4 %copy-start.12 = (bf16[1,1024,8,72]{1,3,2,0:T(8,128)(2,1)S(1)}, bf16[1,1024,8,72]{1,3,2,0:T(8,128)(2,1)}, u32[]{:S(2)}) copy-start(bf16[1,1024,8,72]{1,3,2,0:T(8,128)(2,1)} %copy-done.11) | copy-start | bytes 3538948
  477.0 29.5 %all-to-all-start.5 = ((bf16[2,2,147456]{2,1,0:T(2,128)(2,1)}), bf16[2,2,147456]{2,1,0:T(2,128)(2,1)}, u32[]{:S(2)}, u32[]{:S(2)}) async-start(bf16[2,2,147456]{2,1,0:T(2,128)(2,1)} %reshape.437), calls=%async_computation.5 | async-start | bytes 2359296 | tf_op jit(solution)/shard_map/all_to_all | solution.py:190
  506.5 22.7 %all-to-all-start.6 = ((bf16[2,2,147456]{2,1,0:T(2,128)(2,1)}), bf16[2,2,147456]{2,1,0:T(2,128)(2,1)}, u32[]{:S(2)}, u32[]{:S(2)}) async-start(bf16[2,2,147456]{2,1,0:T(2,128)(2,1)} %reshape.435), calls=%async_computation.6 | async-start | bytes 2359296 | tf_op jit(solution)/shard_map/all_to_all | solution.py:197
  510.9 139.3 %reduce-scatter.25.cloned.1.call-start = ((), (), s32[]{:S(2)}) async-start(), calls=%async_computation.22 | async-start | bytes 8460288
  550.3 220.5 %reduce-scatter.19.cloned.1.call-start = ((), (), s32[]{:S(2)}) async-start(), calls=%async_computation.19 | async-start | bytes 10653696 | tf_op jit(solution)/shard_map/reduce_scatter | solution.py:233
  562.6 327.9 %reduce-scatter.17.cloned.1.call-start = ((), (), s32[]{:S(2)}) async-start(), calls=%async_computation.18 | async-start | bytes 10653696 | tf_op jit(solution)/shard_map/reduce_scatter | solution.py:230
  575.4 328.4 %reduce-scatter.23.cloned.1.call-start = ((), (), s32[]{:S(2)}) async-start(), calls=%async_computation.21 | async-start | bytes 442368
  592.6 332.5 %reduce-scatter.21.cloned.1.call-start = ((), (), s32[]{:S(2)}) async-start(), calls=%async_computation.20 | async-start | bytes 1327104
  604.4 48.2 %copy-start.15 = (bf16[1,2,512,1,576]{2,1,4,3,0:T(2,128)(2,1)S(1)}, bf16[1,2,512,1,576]{2,1,4,3,0:T(2,128)(2,1)}, u32[]{:S(2)}) copy-start(bf16[1,2,512,1,576]{2,1,4,3,0:T(2,128)(2,1)} %copy-done.14) | copy-start | bytes 3538948
  604.4 51.7 %copy-start.17 = (bf16[1,2,512,1,576]{2,1,4,3,0:T(2,128)(2,1)S(1)}, bf16[1,2,512,1,576]{2,1,4,3,0:T(2,128)(2,1)}, u32[]{:S(2)}) copy-start(bf16[1,2,512,1,576]{2,1,4,3,0:T(2,128)(2,1)} %copy-done.16) | copy-start | bytes 3538948
  652.5 320.1 %all-reduce.8.cloned.1.call-start = ((), (), s32[]{:S(2)}) async-start(), calls=%async_computation.24 | async-start | bytes 2506752
  659.3 231.8 %copy-start.8 = (f32[512,1152]{1,0:T(8,128)S(1)}, f32[512,1152]{1,0:T(8,128)}, u32[]{:S(2)}) copy-start(f32[512,1152]{1,0:T(8,128)} %copy-done.7) | copy-start | bytes 7077892
  (34 other events, 115.8 us)
Sparse Core Ops, SparseCore 0:
  10.2 74.8 all-gather.8
  87.3 41.6 all-gather.10
  131.2 83.7 all-gather.12
  217.0 83.2 all-gather.14
  345.3 62.6 reduce-scatter.26
  550.5 99.7 reduce-scatter.24
  654.4 116.3 reduce-scatter.18
  774.9 115.4 reduce-scatter.16
  892.7 11.1 reduce-scatter.22
  906.5 18.5 reduce-scatter.20
  927.5 44.9 all-reduce.7
where the time goes:
time: 1010 us
  waiting for transfers between devices  435 us (43%)
  matrix products  192 us (19%)
  local copies, waits for them, and re-layouts  137 us (14%)
  other arithmetic  101 us (10%)
  blocking collectives  95 us (9%)
  starting transfers between devices  30.3 us (3%)
  between operations  16.5 us (2%)
    reduce_scatter x1, waiting for transfers between devices, body(): lax.psum_scatter(grad_up.astype(jnp.bfloat16), 'fsdp', scatter_dimension=...  120 us
    unnamed x16, waiting for transfers between devices  106 us
    all_gather x1, waiting for transfers between devices, body(): lax.all_gather(qkv_weight, 'fsdp', axis=0, tiled=True)  73.8 us
    reduce_scatter x1, waiting for transfers between devices, body(): lax.psum_scatter(grad_down.astype(jnp.bfloat16), 'fsdp', scatter_dimensio...  64.1 us
    unnamed x148, local copies, waits for them, and re-layouts  62.8 us
    psum x1, blocking collectives, body(): lax.psum((grad_attn_gain, grad_attn_shift, grad_query_bias, grad_value_bi...  44 us
    dot_general x4, matrix products, times_transpose(): lax.dot_general(left_rows, matrix, (((1,), (1,)), ((), ())), preferred_el...  42.6 us
    unnamed x6, other arithmetic  40.2 us
  transfers between devices with their start and end apart: 18, of which 12 were waited for; matrix products, arithmetic and copies ran while one was open for 37% of the time, Pallas kernels for 0%

commit v1 on v0

v1 whole, which is shorter than its diff:
```python
import functools

import jax
import jax.numpy as jnp
from jax import lax
from jax.experimental import pallas as pl
from jax.experimental.pallas import tpu as pltpu
from jax.sharding import PartitionSpec as P

HD = 72
WIDE = 128
SCALE = HD ** (-0.5)
masked_score = -1e30
epsilon = 1e-06
f32, bf16 = jnp.float32, jnp.bfloat16


def spread_heads(source, target, heads):
    for head in range(heads):
        target[head, :, :HD] = source[0, :, head * HD : (head + 1) * HD]


def turn_heads(source, target, heads):
    for head in range(heads):
        target[head] = jnp.transpose(source[head])


def join_heads(source, heads):
    return jnp.concatenate([source[head, :, :HD] for head in range(heads)], axis=1)


def nt(left, right):
    return lax.dot_general(left, right, (((1,), (1,)), ((), ())), preferred_element_type=f32)


def nn(left, right):
    return jnp.dot(left, right, preferred_element_type=f32)


def attend_kernel(parts, heads, block, earlier, info, *refs):
    q_in = refs[0]
    k_in = refs[1 : 1 + parts]
    v_in = refs[1 + parts : 1 + 2 * parts]
    refs = refs[1 + 2 * parts + earlier :]
    out, lse = refs[:2]
    scratch = refs[2:]
    q_s, o_s = scratch[:2]
    k_s = scratch[2 : 2 + parts]
    vt_s = scratch[2 + parts : 2 + 2 * parts]
    head = pl.program_id(0)
    rows = q_s.shape[1]

    @pl.when(head == 0)
    def _():
        q_s[...] = jnp.zeros_like(q_s)
        spread_heads(q_in, q_s, heads)
        for part in range(parts):
            k_s[part][...] = jnp.zeros_like(k_s[part])
            spread_heads(v_in[part], k_s[part], heads)
            turn_heads(k_s[part], vt_s[part], heads)
            spread_heads(k_in[part], k_s[part], heads)

    masks = []
    for part in range(parts):
        length = k_s[part].shape[1]
        masks.append(
            info[1 + part] + lax.broadcasted_iota(jnp.int32, (length, 1), 0) < info[0]
        )
    for start in range(0, rows, block):
        q_rows = q_s[head, start : start + block]
        scores = [
            jnp.where(masks[part], nt(k_s[part][head], q_rows), masked_score)
            for part in range(parts)
        ]
        peak = functools.reduce(
            jnp.maximum, [jnp.max(member, axis=0, keepdims=True) for member in scores]
        )
        total = 0.0
        result = 0.0
        for part in range(parts):
            grown = jnp.exp((scores[part] - peak) * SCALE)
            total = total + jnp.sum(grown, axis=0, keepdims=True)
            result = result + nn(vt_s[part][head], grown.astype(bf16))
        result = result / total
        o_s[head, start : start + block] = jnp.transpose(result).astype(bf16)
        lse[0, :, start : start + block] = peak * SCALE + jnp.log(total)

    @pl.when(head == heads - 1)
    def _():
        out[0] = join_heads(o_s, heads)


def attend_back_kernel(parts, heads, block, earlier, info, *refs):
    q_in, d_in, lse = refs[:3]
    k_in = refs[3 : 3 + parts]
    v_in = refs[3 + parts : 3 + 2 * parts]
    refs = refs[3 + 2 * parts + earlier :]
    dq_out = refs[0]
    dk_out = refs[1 : 1 + parts]
    dv_out = refs[1 + parts : 1 + 2 * parts]
    refs = refs[1 + 2 * parts :]
    q_s, d_s, dq_s = refs[:3]
    refs = refs[3:]
    k_s, v_s, kt_s, dk_s, dv_s = (refs[i * parts : (i + 1) * parts] for i in range(5))
    head = pl.program_id(0)
    rows = q_s.shape[1]

    @pl.when(head == 0)
    def _():
        q_s[...] = jnp.zeros_like(q_s)
        d_s[...] = jnp.zeros_like(d_s)
        spread_heads(q_in, q_s, heads)
        spread_heads(d_in, d_s, heads)
        for part in range(parts):
            k_s[part][...] = jnp.zeros_like(k_s[part])
            v_s[part][...] = jnp.zeros_like(v_s[part])
            spread_heads(k_in[part], k_s[part], heads)
            spread_heads(v_in[part], v_s[part], heads)
            turn_heads(k_s[part], kt_s[part], heads)

    masks = []
    for part in range(parts):
        length = k_s[part].shape[1]
        masks.append(
            info[1 + part] + lax.broadcasted_iota(jnp.int32, (length, 1), 0) < info[0]
        )
    d_key = [0.0] * parts
    d_value = [0.0] * parts
    for start in range(0, rows, block):
        q_rows = q_s[head, start : start + block]
        d_rows = d_s[head, start : start + block]
        level = lse[0, :, start : start + block]
        probs = []
        d_probs = []
        row_dot = 0.0
        for part in range(parts):
            scores = jnp.where(masks[part], nt(k_s[part][head], q_rows) * SCALE, masked_score)
            probs.append(jnp.exp(scores - level))
            d_probs.append(nt(v_s[part][head], d_rows))
            row_dot = row_dot + jnp.sum(probs[part] * d_probs[part], axis=0, keepdims=True)
        d_query = 0.0
        for part in range(parts):
            d_scores = (probs[part] * (d_probs[part] - row_dot)).astype(bf16)
            d_value[part] = d_value[part] + nn(probs[part].astype(bf16), d_rows)
            d_key[part] = d_key[part] + nn(d_scores, q_rows)
            d_query = d_query + nn(kt_s[part][head], d_scores)
        dq_s[head, start : start + block] = jnp.transpose(d_query * SCALE).astype(bf16)
    for part in range(parts):
        dk_s[part][head] = (d_key[part] * SCALE).astype(bf16)
        dv_s[part][head] = d_value[part].astype(bf16)

    @pl.when(head == heads - 1)
    def _():
        dq_out[0] = join_heads(dq_s, heads)
        for part in range(parts):
            dk_out[part][0] = join_heads(dk_s[part], heads)
            dv_out[part][0] = join_heads(dv_s[part], heads)


def whole(shape):
    return pl.BlockSpec(shape, lambda head: (0,) * len(shape))


def anywhere(arrays):
    return [pl.BlockSpec(memory_space=pl.ANY)] * len(arrays)


def attend(info, query, keys, values, earlier=(), block=512):
    _, rows, width = query.shape
    heads = width // HD
    parts = len(keys)
    lengths = [member.shape[1] for member in keys]
    total = sum(lengths)
    return pl.pallas_call(
        functools.partial(attend_kernel, parts, heads, min(block, rows), len(earlier)),
        grid=(heads,),
        in_specs=[pl.BlockSpec(memory_space=pltpu.SMEM), whole(query.shape)]
        + [whole(member.shape) for member in (*keys, *values)]
        + anywhere(earlier),
        out_specs=[whole(query.shape), pl.BlockSpec((1, 1, rows), lambda head: (head, 0, 0))],
        out_shape=[
            jax.ShapeDtypeStruct(query.shape, bf16),
            jax.ShapeDtypeStruct((heads, 1, rows), f32),
        ],
        scratch_shapes=[pltpu.VMEM((heads, rows, WIDE), bf16)] * 2
        + [pltpu.VMEM((heads, length, WIDE), bf16) for length in lengths]
        + [pltpu.VMEM((heads, WIDE, length), bf16) for length in lengths],
        compiler_params=pltpu.CompilerParams(vmem_limit_bytes=48 * 1024 * 1024),
        cost_estimate=pl.CostEstimate(
            flops=4 * heads * rows * total * 256,
            bytes_accessed=4 * (rows + total) * width,
            transcendentals=heads * rows * total,
        ),
    )(info, query, *keys, *values, *earlier)


def attend_back(info, query, d_out, lse, keys, values, earlier=(), block=256):
    _, rows, width = query.shape
    heads = width // HD
    parts = len(keys)
    lengths = [member.shape[1] for member in keys]
    total = sum(lengths)
    results = pl.pallas_call(
        functools.partial(attend_back_kernel, parts, heads, min(block, rows), len(earlier)),
        grid=(heads,),
        in_specs=[
            pl.BlockSpec(memory_space=pltpu.SMEM),
            whole(query.shape),
            whole(query.shape),
            pl.BlockSpec((1, 1, rows), lambda head: (head, 0, 0)),
        ]
        + [whole(member.shape) for member in (*keys, *values)]
        + anywhere(earlier),
        out_specs=[whole(member.shape) for member in (query, *keys, *values)],
        out_shape=[
            jax.ShapeDtypeStruct(member.shape, bf16) for member in (query, *keys, *values)
        ],
        scratch_shapes=[pltpu.VMEM((heads, rows, WIDE), bf16)] * 3
        + [pltpu.VMEM((heads, length, WIDE), bf16) for length in lengths] * 2
        + [pltpu.VMEM((heads, WIDE, length), bf16) for length in lengths]
        + [pltpu.VMEM((heads, length, WIDE), bf16) for length in lengths] * 2,
        compiler_params=pltpu.CompilerParams(vmem_limit_bytes=56 * 1024 * 1024),
        cost_estimate=pl.CostEstimate(
            flops=10 * heads * rows * total * 256,
            bytes_accessed=8 * (rows + total) * width,
            transcendentals=heads * rows * total,
        ),
    )(info, query, d_out, lse, *keys, *values, *earlier)
    return results[0], results[1 : 1 + parts], results[1 + parts :]


def contract_rows(left_rows, right_rows):
    return lax.dot_general(
        left_rows, right_rows, (((0,), (0,)), ((), ())), preferred_element_type=f32
    )


def column_sum(tensor):
    return jnp.sum(tensor.astype(f32), axis=0)


def after(value, *earlier):
    return lax.optimization_barrier((value, *earlier))[0]


def norm_parts(tensor):
    centered = tensor - jnp.mean(tensor, axis=-1, keepdims=True)
    scale = lax.rsqrt(jnp.mean(centered * centered, axis=-1, keepdims=True) + epsilon)
    return centered * scale, scale


def norm_back(upstream, normal, scale, gain):
    weighted = upstream * gain
    mean_one = jnp.mean(weighted, axis=-1, keepdims=True)
    mean_two = jnp.mean(weighted * normal, axis=-1, keepdims=True)
    return scale * (weighted - mean_one - normal * mean_two)


def gelu_and_slope(tensor):
    square = tensor * tensor
    bent = jnp.tanh(0.7978845608028654 * tensor * (1.0 + 0.044715 * square))
    half = 0.5 * (1.0 + bent)
    slope = half + 0.5 * tensor * (1.0 - bent * bent) * 0.7978845608028654 * (
        1.0 + 0.134145 * square
    )
    return tensor * half, slope


def place_kernel(count, slots, *refs):
    pieces, (out, sems) = refs[:count], refs[-2:]
    copies = []
    for piece in pieces:
        for line in range(piece.shape[0]):
            for part in range(piece.shape[1]):
                index = len(copies)
                copies.append(
                    pltpu.make_async_copy(
                        piece.at[line, part], out.at[slots[index]], sems.at[index]
                    )
                )
    for copy in copies:
        copy.start()
    for copy in copies:
        copy.wait()


def place(pieces, slots, earlier=()):
    rows, columns = pieces[0].shape[2:]
    total = sum(piece.shape[0] * piece.shape[1] for piece in pieces)
    return pl.pallas_call(
        functools.partial(place_kernel, len(pieces)),
        in_specs=[pl.BlockSpec(memory_space=pltpu.SMEM)]
        + anywhere(pieces)
        + anywhere(earlier),
        out_specs=pl.BlockSpec(memory_space=pltpu.VMEM),
        out_shape=jax.ShapeDtypeStruct((total, rows, columns), pieces[0].dtype),
        scratch_shapes=[pltpu.SemaphoreType.DMA((total,))],
        compiler_params=pltpu.CompilerParams(vmem_limit_bytes=32 * 1024 * 1024),
        cost_estimate=pl.CostEstimate(
            flops=0, bytes_accessed=4 * total * rows * columns, transcendentals=0
        ),
    )(slots, *pieces, *earlier)


class Grid:
    def __init__(self, shard_rows):
        self.size = lax.axis_size("fsdp")
        self.apart = HD // shard_rows
        self.depth = self.size // 4
        me = lax.axis_index("fsdp")
        self.twin = (me // self.apart) % 2
        member = (me // (2 * self.apart)) * self.apart + me % self.apart
        self.z, self.x = member // 2, member % 2

    def index(self, z, x, twin):
        member = z * 2 + x
        return (
            (member // self.apart) * 2 * self.apart + twin * self.apart + member % self.apart
        )

    def pairs(self, step_z=0, step_x=0, step_twin=0):
        return [
            (
                self.index(z, x, twin),
                self.index((z + step_z) % self.depth, x ^ step_x, twin ^ step_twin),
            )
            for z in range(self.depth)
            for x in range(2)
            for twin in range(2)
        ]

    def send(self, value, **steps):
        return lax.ppermute(value, "fsdp", self.pairs(**steps))

    def members(self):
        return [
            ((self.z + step_z) % self.depth) * 2 + (self.x ^ step_x)
            for step_x in range(2)
            for step_z in range(self.depth)
        ]

    def shards(self):
        return [
            (member // self.apart) * 2 * self.apart
            + (self.twin ^ step) * self.apart
            + member % self.apart
            for member in self.members()
            for step in range(2)
        ]

    def shards_by_seq(self):
        mine = self.shards()
        first = lax.axis_index("seq") == 0
        kinds = [mine[0::2], mine[1::2]]
        return [jnp.where(first, one, two) for one, two in zip(*kinds)] + [
            jnp.where(first, two, one) for one, two in zip(*kinds)
        ]

    def groups(self):
        return [
            [self.index(member // 2, member % 2, twin) for member in range(2 * self.depth)]
            for twin in range(2)
        ]

    def gather(self, block):
        whole = lax.all_gather(block, "fsdp", axis_index_groups=self.groups())
        _, _, rows, columns = whole.shape
        whole = whole.reshape(-1, self.apart, 2, rows, columns).transpose(0, 2, 1, 3, 4)
        return whole.reshape(-1, columns)

    def scatter(self, matrix):
        columns = matrix.shape[1]
        matrix = matrix.reshape(2 * self.depth // self.apart, 2, self.apart, -1, columns)
        matrix = matrix.transpose(0, 2, 1, 3, 4).reshape(-1, columns)
        return lax.psum_scatter(
            matrix, "fsdp", scatter_dimension=0, axis_index_groups=self.groups(), tiled=True
        )

    def own_half(self, halves):
        return jnp.where(self.twin == 0, halves[0], halves[1])

    def other_half(self, halves):
        return jnp.where(self.twin == 0, halves[1], halves[0])

    def swap_rows(self, partial, rows):
        sent = jnp.concatenate([partial[rows:], partial[:rows]], axis=0).astype(bf16)
        return self.send(sent, step_twin=1).astype(f32)

    def swap_mine(self, first, second):
        mine, sent = self.in_order(first, second)
        return self.in_order(mine, self.send(sent.astype(bf16), step_twin=1).astype(f32))

    def in_order(self, mine, other):
        first = self.twin == 0
        return jnp.where(first, mine, other), jnp.where(first, other, mine)


def order_matrix(places, rows):
    count = len(places) * rows
    source = (jnp.stack(places) * rows)[:, None] + jnp.arange(rows, dtype=jnp.int32)[None, :]
    return (jnp.arange(count, dtype=jnp.int32)[:, None] == source.reshape(1, count)).astype(bf16)


def reorder(rows, matrix):
    return jnp.dot(rows, matrix, preferred_element_type=f32).astype(bf16)


def gather_z(grid, block):
    sent = {step: grid.send(block, step_z=step) for step in range(1, grid.depth)}
    return [block] + [sent[grid.depth - step] for step in range(1, grid.depth)]


def gather_x(grid, blocks):
    joined = jnp.stack(blocks)
    return joined, grid.send(joined, step_x=1)


def gather_all(grid, block):
    lines = gather_z(grid, block)
    return lines, list(gather_x(grid, lines))


def by_seq(first_value, second_value):
    return jnp.where(lax.axis_index("seq") == 0, first_value, second_value)


def gather_by_seq(grid, block):
    lines = gather_z(grid, by_seq(block[:1], block[1:]))
    joined, across = gather_x(grid, lines)
    return lines, [joined, across, swap_seq(joined), swap_seq(across)]


def halves_of(left, right):
    half = left.shape[1] // 2
    going = contract_rows(left[:, half:], right).astype(bf16)
    return contract_rows(left[:, :half], right).astype(bf16), going


def add_pieces(kept, came, count):
    rows = kept.shape[0] // count
    return [
        (
            kept[step * rows : (step + 1) * rows].astype(f32)
            + came[step * rows : (step + 1) * rows].astype(f32)
        ).astype(bf16)
        for step in range(count)
    ]


def swap_seq(value):
    return lax.ppermute(value, "seq", [(0, 1), (1, 0)])


def sum_z(grid, sums):
    total = sums[0].astype(f32)
    for step in range(1, grid.depth):
        total = total + grid.send(sums[step], step_z=step).astype(f32)
    return total.astype(bf16)


class ScatterX:
    def __init__(self, grid, left, right):
        self.grid = grid
        self.kept, self.going = halves_of(left, right)
        self.came = grid.send(self.going, step_x=1)

    def add(self):
        self.sums = add_pieces(self.kept, self.came, self.grid.depth)
        return self.sums

    def finish(self):
        return sum_seq(sum_z(self.grid, self.sums))


class ScatterY:
    def __init__(self, grid, left, right):
        self.grid = grid
        self.kept, self.going = halves_of(left, right)
        self.came = swap_seq(self.going)

    def cross(self):
        self.kept, self.going = add_pieces(self.kept, self.came, 2)
        self.came = self.grid.send(self.going, step_x=1)
        return [self.kept, self.going]

    def add(self):
        self.sums = add_pieces(self.kept, self.came, self.grid.depth)
        return self.sums

    def finish(self):
        total = sum_z(self.grid, self.sums)
        other = swap_seq(total)
        first = lax.axis_index("seq") == 0
        return jnp.concatenate(
            [jnp.where(first, total, other), jnp.where(first, other, total)], axis=0
        ).astype(f32)


def sum_seq(value):
    groups = lax.axis_size("seq")
    if groups == 2:
        return value.astype(f32) + lax.ppermute(value, "seq", [(0, 1), (1, 0)]).astype(f32)
    return lax.psum(value.astype(f32), "seq")


def swap_twin(grid, total):
    rows = total.shape[0] // 2
    other = grid.send(total[rows:].astype(bf16), step_twin=1).astype(f32)
    return grid.in_order(total[:rows], other)


def sum_all(vector):
    for axis in ("fsdp", "seq"):
        count = lax.axis_size(axis)
        step = 1
        while step < count:
            vector = vector + lax.ppermute(
                vector, axis, [(member, member ^ step) for member in range(count)]
            )
            step *= 2
    return vector


def body(
    tokens,
    lengths,
    cotangent,
    attn_gain,
    attn_shift,
    qkv_weight,
    query_bias,
    value_bias,
    out_weight,
    out_bias,
    mlp_gain,
    mlp_shift,
    up_weight,
    up_bias,
    down_weight,
    down_bias,
):
    groups = lax.axis_size("seq")
    images, local_len, width = tokens.shape
    shard_rows = qkv_weight.shape[0]
    hidden_half = up_weight.shape[1] // 2
    rows = images * local_len
    heads = width // HD
    own_width = width // 2
    grid = Grid(shard_rows)
    all_members = jnp.stack(grid.members())

    def by_kind(matrix):
        lead = matrix.shape[0]
        split = matrix.reshape(lead, -1, heads // 2, 2, HD)
        return [split[:, :, :, kind].reshape(lead, -1) for kind in range(2)]

    def vector_kind(vector):
        return grid.own_half([vector.reshape(-1, 2, HD)[:, kind].reshape(-1) for kind in range(2)])

    def two_halves(matrix):
        return [matrix[:, :hidden_half], matrix[:, hidden_half:]]

    def pair_up(halves):
        other = grid.send(grid.other_half(halves), step_twin=1)
        return jnp.stack([grid.own_half(halves), other])

    qkv_block = pair_up(by_kind(qkv_weight))
    pair_block = qkv_block[:, :, own_width:]
    all_kinds = jnp.stack(grid.shards())
    up_block = pair_up(two_halves(up_weight))
    down_block = pair_up(two_halves(down_weight.T))
    own_up = grid.gather(jnp.stack(grid.in_order(*up_block)))
    own_down = grid.gather(jnp.stack(grid.in_order(*down_block)))
    if groups == 2:
        pair_lines, pair_pieces = gather_by_seq(grid, pair_block)
        pair_slots = jnp.stack(grid.shards_by_seq())
    else:
        pair_lines, pair_pieces = gather_all(grid, pair_block)
        pair_slots = all_kinds
    query_lines, query_pieces = gather_all(
        grid, after(qkv_block[:, :, :own_width], pair_lines[-1])
    )
    out_lines, out_pieces = gather_all(grid, after(out_weight[None], query_lines[-1]))

    def both(value):
        flat = value.reshape(rows, width)
        return jnp.concatenate([flat, grid.send(flat, step_twin=1)], axis=0)

    inputs = both(tokens).astype(f32)
    back_low = both(cotangent)
    sizes = jnp.concatenate([lengths, grid.send(lengths, step_twin=1)])

    order = order_matrix(grid.shards(), shard_rows)
    if groups == 2:
        scatter_seq, seq_order = ScatterY, order_matrix(grid.shards_by_seq(), shard_rows)
    else:
        scatter_seq, seq_order = ScatterX, order
    own_order = order_matrix(grid.members(), shard_rows)

    normal_one, scale_one = norm_parts(inputs)
    normed_one = (normal_one * attn_gain + attn_shift).astype(bf16)
    own_pair = place(pair_pieces, pair_slots, query_lines[1:]).reshape(width, 2 * own_width)
    pair_bias = jnp.concatenate([jnp.zeros((own_width,), f32), vector_kind(value_bias)])
    pairs = (jnp.dot(normed_one, own_pair, preferred_element_type=f32) + pair_bias).astype(bf16)
    own_query = place(query_pieces, all_kinds, out_lines[1:])
    own_query = own_query.reshape(width, own_width)
    queries = (
        jnp.dot(normed_one, own_query, preferred_element_type=f32) + vector_kind(query_bias)
    ).astype(bf16)

    place_seq = lax.axis_index("seq") * local_len
    attended_parts, saved = [], []
    for image in range(2 * images):
        span = slice(image * local_len, (image + 1) * local_len)
        query, near = queries[span][None], pairs[span][None]
        key, value = near[:, :, :own_width], near[:, :, own_width:]
        if groups == 2:
            far = swap_seq(near)
            key_parts = (key, far[:, :, :own_width])
            value_parts = (value, far[:, :, own_width:])
            info = jnp.stack([sizes[image], place_seq, local_len - place_seq])
        else:
            key_parts = (lax.all_gather(key, "seq", axis=1, tiled=True),)
            value_parts = (lax.all_gather(value, "seq", axis=1, tiled=True),)
            info = jnp.stack([sizes[image], jnp.zeros_like(sizes[image])])
        attended_part, lse = attend(info, query, key_parts, value_parts)
        attended_parts.append(attended_part[0])
        saved.append((info, query, key_parts, value_parts, lse))
    attended = jnp.concatenate(attended_parts, axis=0)

    own_out = place(out_pieces, all_members)
    own_out = own_out.reshape(own_width, width)
    partial = jnp.dot(attended, own_out, preferred_element_type=f32)
    resid = inputs + partial + grid.swap_rows(partial, rows) + out_bias
    normal_two, scale_two = norm_parts(resid)
    normed_two = (normal_two * mlp_gain + mlp_shift).astype(bf16)
    own_up_bias = grid.own_half([up_bias[:hidden_half], up_bias[hidden_half:]])
    hidden = jnp.dot(normed_two, own_up, preferred_element_type=f32) + own_up_bias
    active, slope = gelu_and_slope(hidden)
    active, slope = lax.optimization_barrier((active.astype(bf16), slope.astype(bf16)))
    grad_down = contract_rows(back_low, active).astype(bf16)
    back_low, grad_down = lax.optimization_barrier((back_low, grad_down))
    grad_down = grid.scatter(grad_down)

    d_active = jnp.dot(back_low, own_down, preferred_element_type=f32)
    d_hidden = (d_active * slope).astype(bf16)
    grad_up = contract_rows(normed_two, d_hidden).astype(bf16)
    d_hidden, grad_up = lax.optimization_barrier((d_hidden, grad_up))
    grad_up = grid.scatter(grad_up)
    partial = lax.dot_general(
        d_hidden, own_up, (((1,), (1,)), ((), ())), preferred_element_type=f32
    )
    d_two = partial + grid.swap_rows(partial, rows)
    d_resid = back_low.astype(f32) + norm_back(d_two, normal_two, scale_two, mlp_gain)
    out_low = d_resid.astype(bf16)
    grad_out = ScatterX(grid, reorder(attended, own_order), out_low)
    d_attended = lax.dot_general(
        out_low, own_out, (((1,), (1,)), ((), ())), preferred_element_type=f32
    ).astype(bf16)

    d_query, d_key, d_value = [], [], []
    for image in range(2 * images):
        span = slice(image * local_len, (image + 1) * local_len)
        info, query, key_parts, value_parts, lse = saved[image]
        if image == 0:
            on_their_way = [grad_out.kept, grad_out.going]
        else:
            on_their_way = grad_out.add() if image == images else []
        d_query_part, key_grads, value_grads = attend_back(
            info,
            query,
            d_attended[span][None],
            lse,
            key_parts,
            value_parts,
            on_their_way,
        )
        d_query.append(d_query_part[0])
        if groups == 2:
            far = swap_seq(jnp.concatenate([key_grads[1], value_grads[1]], axis=2))
            d_key.append((key_grads[0], far[:, :, :own_width]))
            d_value.append((value_grads[0], far[:, :, own_width:]))
        else:
            for into, member in ((d_key, key_grads[0]), (d_value, value_grads[0])):
                into.append(
                    (
                        lax.psum_scatter(
                            member.astype(f32), "seq", scatter_dimension=1, tiled=True
                        ),
                    )
                )
    d_query = jnp.concatenate(d_query, axis=0)
    one_rows = reorder(normed_one, order)
    grad_query = ScatterX(grid, one_rows, d_query)
    late_active, grad_query.kept = lax.optimization_barrier((active, grad_query.kept))
    partial = lax.dot_general(
        late_active, own_down, (((1,), (1,)), ((), ())), preferred_element_type=f32
    )
    came = grid.send(partial[rows:].astype(bf16), step_twin=1).astype(f32)
    outputs = (resid[:rows] + partial[:rows] + came + down_bias).astype(bf16)

    d_key, d_value = (
        jnp.concatenate(
            [sum(part.astype(f32) for part in parts)[0].astype(bf16) for parts in member], axis=0
        )
        for member in (d_key, d_value)
    )
    grad_key = scatter_seq(grid, reorder(normed_one, seq_order), d_key)
    grad_value = ScatterX(grid, one_rows, d_value)
    partial = sum(
        lax.dot_general(member, weight, (((1,), (1,)), ((), ())), preferred_element_type=f32)
        for member, weight in (
            (d_query, own_query),
            (d_key, own_pair[:, :own_width]),
            (d_value, own_pair[:, own_width:]),
        )
    )
    d_one = partial[:rows] + grid.send(partial[rows:].astype(bf16), step_twin=1).astype(f32)
    grad_tokens = d_resid[:rows] + norm_back(d_one, normal_one[:rows], scale_one[:rows], attn_gain)
    grad_query.add()
    if groups == 2:
        grad_key.cross()
    grad_value.add()
    grad_key.add()
    grad_out = grad_out.finish()
    grad_up, grad_down = sum_seq(grad_up), sum_seq(grad_down)
    grad_qkv = jnp.concatenate(
        [grad_query.finish(), grad_key.finish(), grad_value.finish()], axis=1
    )

    def by_kinds(total):
        half = total.shape[0] // 2
        return jnp.concatenate(grid.swap_mine(total[:half], total[half:]), axis=1)

    grad_up, grad_down = by_kinds(grad_up), by_kinds(grad_down).T
    grad_qkv = jnp.stack(
        [member.reshape(shard_rows, 3, heads // 2, HD) for member in swap_twin(grid, grad_qkv)],
        axis=3,
    ).reshape(shard_rows, 3 * width)

    def at_kind(vector, shape, axis):
        vector = vector.reshape(shape)
        nothing = jnp.zeros_like(vector)
        return jnp.stack(grid.in_order(vector, nothing), axis=axis).reshape(-1)

    vectors = sum_all(
        jnp.concatenate(
            [
                column_sum(d_one * normal_one[:rows]),
                column_sum(d_one),
                at_kind(column_sum(d_query), (heads // 2, HD), 1),
                at_kind(column_sum(d_value), (heads // 2, HD), 1),
                column_sum(out_low[:rows]),
                column_sum(d_two[:rows] * normal_two[:rows]),
                column_sum(d_two[:rows]),
                column_sum(back_low[:rows]),
                at_kind(column_sum(d_hidden), (-1,), 0),
            ]
        )
    )
    (
        grad_attn_gain,
        grad_attn_shift,
        grad_query_bias,
        grad_value_bias,
        grad_out_bias,
        grad_mlp_gain,
        grad_mlp_shift,
        grad_down_bias,
    ) = (vectors[step * width : (step + 1) * width] for step in range(8))
    grad_up_bias = vectors[8 * width :]
    shape = (images, local_len, width)
    return (
        outputs.reshape(shape),
        grad_tokens.reshape(shape),
        grad_attn_gain,
        grad_attn_shift,
        grad_qkv,
        grad_query_bias,
        grad_value_bias,
        grad_out,
        grad_out_bias,
        grad_mlp_gain,
        grad_mlp_shift,
        grad_up,
        grad_up_bias,
        grad_down,
        grad_down_bias,
    )


def solution(mesh):
    return jax.shard_map(
        body,
        mesh=mesh,
        in_specs=(
            P("fsdp", "seq", None),
            P("fsdp"),
            P("fsdp", "seq", None),
            P(),
            P(),
            P("fsdp", None),
            P(),
            P(),
            P("fsdp", None),
            P(),
            P(),
            P(),
            P("fsdp", None),
            P(),
            P(None, "fsdp"),
            P(),
        ),
        out_specs=(
            P("fsdp", "seq", None),
            P("fsdp", "seq", None),
            P(),
            P(),
            P("fsdp", None),
            P(),
            P(),
            P("fsdp", None),
            P(),
            P(),
            P(),
            P("fsdp", None),
            P(),
            P(None, "fsdp"),
            P(),
        ),
        check_vma=False,
    )
```

time: 1010 us -> 625 us (0.62)
  waiting for transfers between devices: 435 us -> 174 us
  blocking collectives: 95 us -> 0 us
  local copies, waits for them, and re-layouts: 137 us -> 46.1 us
  Pallas kernels: 0 us -> 88.7 us
  matrix products: 192 us -> 110 us
  starting transfers between devices: 30.3 us -> 108 us
  other arithmetic: 101 us -> 73.5 us
    reduce_scatter x2, waiting for transfers between devices: 184 us -> 0.01 us  [scatter(): lax.psum_scatter(matrix, 'fsdp', scatter_dimension=0, axis_index_groups=s...]
    ppermute x0 -> x59, waiting for transfers between devices: none -> 174 us  [the longest x41 119 us: send(): return lax.ppermute(value, 'fsdp', self.pairs(**steps))]
    all_gather x4 -> x2, waiting for transfers between devices: 109 us -> 0.02 us  [gather(): whole = lax.all_gather(block, 'fsdp', axis_index_groups=self.groups())]
    ppermute x0 -> x59, starting transfers between devices: none -> 108 us  [the longest x41 84.2 us: send(): return lax.ppermute(value, 'fsdp', self.pairs(**steps))]
    unnamed x16 -> x4, waiting for transfers between devices: 106 us -> 0.07 us
    pallas_call x0 -> x7, Pallas kernels: none -> 88.7 us  [the longest x2 49.9 us: attend_back(): pl.pallas_call(functools.partial(attend_back_kernel, parts, heads, min(bl...]
    dot_general x20 -> x14, matrix products: 156 us -> 74 us  [the longest x1 16.9 us: body(): jnp.dot(normed_two, own_up, preferred_element_type=f32) + own_up_bias]
    psum x1 -> x0, blocking collectives: 44 us -> none  [body(): lax.psum((grad_attn_gain, grad_attn_shift, grad_query_bias, grad_value_bi...]
  transfers between devices with their start and end apart: 18 -> 63, of which waited for: 12 -> 27; matrix products, arithmetic and copies ran while one was open for 37% -> 35% of each run, Pallas kernels for 0% -> 14%
where the time goes in v1:
time: 625 us; the launch traced here: 617 us
  waiting for transfers between devices  174 us (28%)
  matrix products  110 us (18%)
  starting transfers between devices  108 us (17%)
  Pallas kernels  88.7 us (14%)
  other arithmetic  73.5 us (12%)
  local copies, waits for them, and re-layouts  46.1 us (7%)
  between operations  16.6 us (3%)
    ppermute x41, waiting for transfers between devices, send(): return lax.ppermute(value, 'fsdp', self.pairs(**steps))  119 us
    ppermute x41, starting transfers between devices, send(): return lax.ppermute(value, 'fsdp', self.pairs(**steps))  84.2 us
    pallas_call x2, Pallas kernels, attend_back(): pl.pallas_call(functools.partial(attend_back_kernel, parts, heads, min(bl...  49.9 us
    dot_general x10, matrix products, contract_rows(): lax.dot_general(left_rows, right_rows, (((0,), (0,)), ((), ())), preferre...  36 us
    pallas_call x2, Pallas kernels, attend(): pl.pallas_call(functools.partial(attend_kernel, parts, heads, min(block,...  29.3 us
    ppermute x8, waiting for transfers between devices, swap_seq(): return lax.ppermute(value, 'seq', [(0, 1), (1, 0)])  27.5 us
    unnamed x188, local copies, waits for them, and re-layouts  23.7 us
    ppermute x5, waiting for transfers between devices, sum_seq(): lax.ppermute(value, 'seq', [(0, 1), (1, 0)]).astype(f32)  21.3 us
  transfers between devices with their start and end apart: 63, of which 27 were waited for; matrix products, arithmetic and copies ran while one was open for 35% of the time, Pallas kernels for 14%

profile of v1, /device:TPU:0, one launch (start us, length us, event | category | flops | bytes accessed | tf_op | source)
XLA Modules:
  0.0 617.2 jit_solution(17436119998918152974)
XLA Ops:
  26.6 6.0 collective-permute-done.2
  32.5 9.5 %collective-permute-start.3 = (bf16[2,72,576]{2,1,0:T(8,128)(2,1)S(1)}, bf16[2,72,576]{2,1,0:T(8,128)(2,1)S(1)}, u32[]{:S(2)}, u32[]{:S(2)}) collective-permute-start(bf16[2,72,576]{2,1,0:T(8,128)(2,1)S(1)} %pad_maximum_fusion.22), channel_id=1, source_target_pairs={{0,24},{2,26},{4,28},{6,30},{8,0},{10,2},{12,4},{14,6},{16,8},{18,... | collective-permute-start | bytes 497672 | tf_op jit(solution)/shard_map/ppermute | solution.py:333
  46.3 10.5 %collective-permute-done.11 = bf16[1,72,1152]{2,1,0:T(8,128)(2,1)S(1)} collective-permute-done((bf16[1,72,1152]{2,1,0:T(8,128)(2,1)S(1)}, bf16[1,72,1152]{2,1,0:T(8,128)(2,1)S(1)}, u32[]{:S(2)}, u32[]{:S(2)}) %collective-permute-start.11) | collective-permute-done | bytes 165920 | tf_op jit(solution)/shard_map/ppermute | solution.py:333
  58.2 9.7 %collective-permute-done.5.refs_6_ = bf16[2,72,576]{2,1,0:T(8,128)(2,1)S(1)} collective-permute-done((bf16[2,72,576]{2,1,0:T(8,128)(2,1)S(1)}, bf16[2,72,576]{2,1,0:T(8,128)(2,1)S(1)}, u32[]{:S(2)}, u32[]{:S(2)}) %collective-permute-start.5) | collective-permute-done | bytes 165920 | tf_op jit(solution)/shard_map/ppermute | solution.py:333
  69.6 11.3 %collective-permute-start.8 = (bf16[1,72,1152]{2,1,0:T(8,128)(2,1)S(1)}, bf16[1,72,1152]{2,1,0:T(8,128)(2,1)S(1)}, u32[]{:S(2)}, u32[]{:S(2)}) collective-permute-start(bf16[1,72,1152]{2,1,0:T(8,128)(2,1)S(1)} %bitcast.174), channel_id=1, source_target_pairs={{0,16},{2,18},{4,20},{6,22},{8,24},{10,26},{12,28},{14,30},{16,0},... | collective-permute-start | bytes 497672 | tf_op jit(solution)/shard_map/ppermute | solution.py:333
  85.6 23.7 %collective-permute-done.8.refs_3_ = bf16[1,72,1152]{2,1,0:T(8,128)(2,1)S(1)} collective-permute-done((bf16[1,72,1152]{2,1,0:T(8,128)(2,1)S(1)}, bf16[1,72,1152]{2,1,0:T(8,128)(2,1)S(1)}, u32[]{:S(2)}, u32[]{:S(2)}) %collective-permute-start.8) | collective-permute-done | bytes 165920 | tf_op jit(solution)/shard_map/ppermute | solution.py:333
  117.4 4.8 fusion
  122.2 6.5 %collective-permute-done.6.refs_1_ = bf16[4,2,72,576]{3,2,1,0:T(8,128)(2,1)S(1)} collective-permute-done((bf16[4,2,72,576]{3,2,1,0:T(8,128)(2,1)S(1)}, bf16[4,2,72,576]{3,2,1,0:T(8,128)(2,1)S(1)}, u32[]{:S(2)}, u32[]{:S(2)}) %collective-permute-start.6) | collective-permute-done | bytes 663584 | tf_op jit(solution)/shard_map/ppermute | solution.py:333
  131.7 4.1 shard_map.272
  135.9 3.7 add_convert_fusion.2
  147.4 21.4 %collective-permute-done.15 = bf16[1,512,1152]{2,1,0:T(8,128)(2,1)S(1)} collective-permute-done((bf16[1,512,1152]{2,1,0:T(8,128)(2,1)S(1)}, bf16[1,512,1152]{2,1,0:T(8,128)(2,1)S(1)}, u32[]{:S(2)}, u32[]{:S(2)}) %collective-permute-start.15) | collective-permute-done | bytes 1179680 | tf_op jit(solution)/shard_map/ppermute | solution.py:451
  169.2 14.5 %shard_map.273 = (bf16[1,512,576]{2,1,0:T(8,128)(2,1)S(1)}, f32[8,1,512]{2,1,0:T(1,128)S(1)}) custom-call(s32[3]{0:T(128)S(1)} %add_add_fusion.1.info, bf16[1,512,576]{2,1,0:T(8,128)(2,1)S(1)} %get-tuple-element.137.refs_0_, bf16[1,512,576]{2,1,0:T(8,128)(2,1)S(1)} %get-tuple-element.148.refs_1_.refs_3_, ...), custom_call_target="tpu_custom_call" | custom-call | flops 4294967296 | bytes 3538944 | tf_op jit(solution)/shard_map/pallas_call | solution.py:174
  187.7 14.7 %shard_map.274 = (bf16[1,512,576]{2,1,0:T(8,128)(2,1)S(1)}, f32[8,1,512]{2,1,0:T(1,128)S(1)}) custom-call(s32[3]{0:T(128)S(1)} %add_add_fusion.2.info, bf16[1,512,576]{2,1,0:T(8,128)(2,1)S(1)} %get-tuple-element.138.refs_0_, bf16[1,512,576]{2,1,0:T(8,128)(2,1)S(1)} %get-tuple-element.152.refs_1_.refs_3_, ...), custom_call_target="tpu_custom_call" | custom-call | flops 4294967296 | bytes 3538944 | tf_op jit(solution)/shard_map/pallas_call | solution.py:174
  206.3 5.0 collective-permute-done.21
  220.5 16.9 %add_convert_fusion = (bf16[1024,2152]{0,1:T(8,128)(2,1)}, bf16[1024,2152]{0,1:T(8,128)(2,1)S(1)}) fusion(f32[2152]{0:T(1024)S(1)} %slice_select_fusion.3, bf16[1152,2152]{1,0:T(8,128)(2,1)} %bitcast.180, f32[1024,1152]{1,0:T(8,128)} %subtract_multiply_fusion, f32[1152]{0:T(1024)S(1)} %copy-done.70, f32[1152]{0:T(1024)S(1)} %copy-done.56), kind=kOutput, calls=%fused_computation.4 | convolution fusion | flops 5124816896 | bytes 18509216 | tf_op jit(solution)/shard_map/dot_general | solution.py:638
  239.4 7.7 %convolution_convert_fusion.1 = bf16[1152,2152]{0,1:T(8,128)(2,1)} fusion(bf16[1024,2152]{0,1:T(8,128)(2,1)S(1)} %get-tuple-element.51, bf16[512,1152]{1,0:T(8,128)(2,1)S(1)} %copy-done.33, bf16[512,1152]{1,0:T(8,128)(2,1)S(1)} %bitcast.160), kind=kOutput, calls=%fused_computation.1 | convolution fusion | flops 5084402688 | bytes 11724800 | tf_op jit(solution)/shard_map/dot_general | solution.py:233
  247.2 8.4 %copy.66 = bf16[1152,2152]{1,0:T(8,128)(2,1)} copy(bf16[1152,2152]{0,1:T(8,128)(2,1)} %convolution_convert_fusion.1) | data formatting | bytes 9916416
  256.2 10.2 %multiply_convert_fusion = bf16[1024,2152]{0,1:T(8,128)(2,1)S(1)} fusion(bf16[1024,2152]{0,1:T(8,128)(2,1)} %get-tuple-element.45, bf16[1024,1152]{1,0:T(8,128)(2,1)} %pad_maximum_fusion.2, bf16[1152,2152]{1,0:T(8,128)(2,1)} %bitcast.184), kind=kOutput, calls=%fused_computation.3 | convolution fusion | flops 5083815936 | bytes 16132096 | tf_op jit(solution)/shard_map/dot_general | solution.py:645
  266.5 11.7 %convolution_convert_fusion = bf16[1152,2152]{0,1:T(8,128)(2,1)} fusion(bf16[1024,2152]{0,1:T(8,128)(2,1)S(1)} %multiply_convert_fusion, f32[1024,1152]{1,0:T(8,128)} %subtract_multiply_fusion, f32[1152]{0:T(1024)S(1)} %copy-done.70, f32[1152]{0:T(1024)S(1)} %copy-done.56), kind=kOutput, calls=%fused_computation | convolution fusion | flops 5083223040 | bytes 14093312 | tf_op jit(solution)/shard_map/dot_general | solution.py:233
  278.2 8.2 %fusion.56 = (bf16[1024,1152]{1,0:T(8,128)(2,1)S(1)}, f32[1024,1152]{1,0:T(8,128)}) fusion(bf16[1024,2152]{0,1:T(8,128)(2,1)S(1)} %multiply_convert_fusion, bf16[1152,2152]{1,0:T(8,128)(2,1)S(1)} %bitcast.183), kind=kOutput, calls=%fused_computation.222 | convolution fusion | flops 5078384640 | bytes 16443392 | tf_op jit(solution)/shard_map/dot_general | solution.py:650
  289.1 4.9 fusion.8
  294.0 5.0 fusion.7
  301.2 8.4 %copy.64 = bf16[1152,2152]{1,0:T(8,128)(2,1)} copy(bf16[1152,2152]{0,1:T(8,128)(2,1)} %convolution_convert_fusion) | data formatting | bytes 9916416
  314.2 5.9 multiply_reduce_fusion.2
  330.6 24.7 %shard_map.276 = (bf16[1,512,576]{2,1,0:T(8,128)(2,1)}, bf16[1,512,576]{2,1,0:T(8,128)(2,1)}, bf16[1,512,576]{2,1,0:T(8,128)(2,1)}, bf16[1,512,576]{2,1,0:T(8,128)(2,1)}, bf16[1,512,576]{2,1,0:T(8,128)(2,1)}) custom-call(s32[3]{0:T(128)} %copy-done.15, bf16[1,512,576]{2,1,0:T(8,128)(2,1)} %copy-done.9, bf16[1,512,576]{2,1,0:T(8,128)(2,1)} %get-tuple-element.135.refs_1_, ...), custom_call_target="tpu_custom_call" | custom-call | flops 10737418240 | bytes 7077888 | tf_op jit(solution)/shard_map/pallas_call | solution.py:203
  362.2 4.3 collective-permute-start.51
  373.7 13.1 %collective-permute-done.52 = bf16[72,1152]{1,0:T(8,128)(2,1)S(1)} collective-permute-done((bf16[72,1152]{1,0:T(8,128)(2,1)S(1)}, bf16[72,1152]{1,0:T(8,128)(2,1)S(1)}, u32[]{:S(2)}, u32[]{:S(2)}) %collective-permute-start.52) | collective-permute-done | bytes 165920 | tf_op jit(solution)/shard_map/ppermute | solution.py:333
  387.6 25.3 %shard_map.277 = (bf16[1,512,576]{2,1,0:T(8,128)(2,1)}, bf16[1,512,576]{2,1,0:T(8,128)(2,1)}, bf16[1,512,576]{2,1,0:T(8,128)(2,1)}, bf16[1,512,576]{2,1,0:T(8,128)(2,1)}, bf16[1,512,576]{2,1,0:T(8,128)(2,1)}) custom-call(s32[3]{0:T(128)} %copy-done.14, bf16[1,512,576]{2,1,0:T(8,128)(2,1)} %copy-done.4, bf16[1,512,576]{2,1,0:T(8,128)(2,1)} %get-tuple-element.136.refs_1_, ...), custom_call_target="tpu_custom_call" | custom-call | flops 10737418240 | bytes 7077888 | tf_op jit(solution)/shard_map/pallas_call | solution.py:203
  412.9 3.5 convolution_convert_fusion.10
  422.7 8.2 %fusion.57 = f32[1024,1152]{1,0:T(8,128)} fusion(bf16[1024,2152]{0,1:T(8,128)(2,1)S(1)} %bitcast.189, bf16[1152,2152]{1,0:T(8,128)(2,1)S(1)} %bitcast.187), kind=kOutput, calls=%fused_computation.223 | convolution fusion | flops 5077204992 | bytes 14084096 | tf_op jit(solution)/shard_map/dot_general | solution.py:696
  433.6 3.5 fusion.42
  437.1 14.4 %collective-permute-done.34 = bf16[576,576]{1,0:T(8,128)(2,1)} collective-permute-done((bf16[576,576]{1,0:T(8,128)(2,1)}, bf16[576,576]{1,0:T(8,128)(2,1)}, u32[]{:S(2)}, u32[]{:S(2)}) %collective-permute-start.34) | collective-permute-done | bytes 663584 | tf_op jit(solution)/shard_map/ppermute | solution.py:333
  452.8 4.5 collective-permute-start.35
  461.6 4.1 collective-permute-done.35
  465.7 11.3 %collective-permute-done.36 = bf16[144,576]{1,0:T(8,128)(2,1)S(1)} collective-permute-done((bf16[144,576]{1,0:T(8,128)(2,1)S(1)}, bf16[144,576]{1,0:T(8,128)(2,1)S(1)}, u32[]{:S(2)}, u32[]{:S(2)}) %collective-permute-start.36) | collective-permute-done | bytes 165920 | tf_op jit(solution)/shard_map/ppermute | solution.py:333
  483.3 3.7 collective-permute-done.38
  505.6 3.5 convolution_convert_fusion.7
  515.7 8.9 %collective-permute-start.46 = (bf16[144,576]{1,0:T(8,128)(2,1)S(1)}, bf16[144,576]{1,0:T(8,128)(2,1)S(1)}, u32[]{:S(2)}, u32[]{:S(2)}) collective-permute-start(bf16[144,576]{1,0:T(8,128)(2,1)S(1)} %get-tuple-element.124), channel_id=1, source_target_pairs={{0,8},{2,10},{4,12},{6,14},{8,16},{10,18},{12,20},{14,22},{16,24},... | collective-permute-start | bytes 497672 | tf_op jit(solution)/shard_map/ppermute | solution.py:333
  524.6 3.5 collective-permute-start.47
  528.2 3.6 collective-permute-start.41
  536.0 4.9 collective-permute-done.47
  540.9 5.0 collective-permute-start.43
  562.0 3.9 collective-permute-done.30
  565.8 3.6 collective-permute-start.31
  572.7 5.2 fusion.12
  582.4 3.7 reshape.630
  589.2 7.7 %collective-permute-done.57 = bf16[144,2152]{1,0:T(8,128)(2,1)S(1)} collective-permute-done((bf16[144,2152]{1,0:T(8,128)(2,1)}, bf16[144,2152]{1,0:T(8,128)(2,1)S(1)}, u32[]{:S(2)}, u32[]{:S(2)}) %collective-permute-start.57) | collective-permute-done | bytes 619808 | tf_op jit(solution)/shard_map/ppermute | solution.py:502
  597.2 9.9 %collective-permute-done.55 = bf16[144,2152]{1,0:T(8,128)(2,1)S(1)} collective-permute-done((bf16[144,2152]{1,0:T(8,128)(2,1)}, bf16[144,2152]{1,0:T(8,128)(2,1)S(1)}, u32[]{:S(2)}, u32[]{:S(2)}) %collective-permute-start.55) | collective-permute-done | bytes 619808 | tf_op jit(solution)/shard_map/ppermute | solution.py:502
  (443 shorter events, 184.1 us)
Async XLA Ops:
  7.2 213.3 %all-gather.5.cloned.1.call-start = ((), (), s32[]{:S(2)}) async-start(), calls=%async_computation.2 | async-start | bytes 5640192 | tf_op jit(solution)/shard_map/all_gather | solution.py:366
  12.4 243.8 %all-gather.7.cloned.1.call-start = ((), (), s32[]{:S(2)}) async-start(), calls=%async_computation.3 | async-start | bytes 5640192 | tf_op jit(solution)/shard_map/all_gather | solution.py:366
  16.2 96.7 %collective-permute-start = (bf16[512,1152]{1,0:T(8,128)(2,1)}, bf16[512,1152]{1,0:T(8,128)(2,1)}, u32[]{:S(2)}, u32[]{:S(2)}) collective-permute-start(bf16[512,1152]{1,0:T(8,128)(2,1)} %bitcast), channel_id=1, source_target_pairs={{0,2},{2,0},{4,6},{6,4},{8,10},{10,8},{12,14},{14,12},{16,18},{18,... | collective-permute-start | bytes 3538952 | tf_op jit(solution)/shard_map/ppermute | solution.py:333
  16.9 9.5 %collective-permute-start.22 = (bf16[72,2152]{1,0:T(8,128)(2,1)S(1)}, bf16[72,2152]{1,0:T(8,128)(2,1)S(1)}, u32[]{:S(2)}, u32[]{:S(2)}) collective-permute-start(bf16[72,2152]{1,0:T(8,128)(2,1)S(1)} %broadcast_select_fusion.2), channel_id=1, source_target_pairs={{0,2},{2,0},{4,6},{6,4},{8,10},{10,8},{12,14},{14,12},{16,18},{18,... | collective-permute-start | bytes 929672 | tf_op jit(solution)/shard_map/ppermute | solution.py:333
  20.3 12.2 %collective-permute-start.2 = (bf16[1,72,1152]{2,1,0:T(8,128)(2,1)S(1)}, bf16[1,72,1152]{2,1,0:T(8,128)(2,1)S(1)}, u32[]{:S(2)}, u32[]{:S(2)}) collective-permute-start(bf16[1,72,1152]{2,1,0:T(8,128)(2,1)S(1)} %slice_select_fusion.2), channel_id=1, source_target_pairs={{0,8},{2,10},{4,12},{6,14},{8,16},{10,18},{12,20},{14,22},{16,24},... | collective-permute-start | bytes 497672 | tf_op jit(solution)/shard_map/ppermute | solution.py:333
  23.3 20.9 %collective-permute-start.10 = (bf16[1,72,1152]{2,1,0:T(8,128)(2,1)S(1)}, bf16[1,72,1152]{2,1,0:T(8,128)(2,1)S(1)}, u32[]{:S(2)}, u32[]{:S(2)}) collective-permute-start(bf16[1,72,1152]{2,1,0:T(8,128)(2,1)S(1)} %slice_select_fusion.2), channel_id=1, source_target_pairs={{0,24},{2,26},{4,28},{6,30},{8,0},{10,2},{12,4},{14,6},{16,8},{18,... | collective-permute-start | bytes 497672 | tf_op jit(solution)/shard_map/ppermute | solution.py:333
  25.4 31.3 %collective-permute-start.11 = (bf16[1,72,1152]{2,1,0:T(8,128)(2,1)S(1)}, bf16[1,72,1152]{2,1,0:T(8,128)(2,1)S(1)}, u32[]{:S(2)}, u32[]{:S(2)}) collective-permute-start(bf16[1,72,1152]{2,1,0:T(8,128)(2,1)S(1)} %slice_select_fusion.2), channel_id=1, source_target_pairs={{0,16},{2,18},{4,20},{6,22},{8,24},{10,26},{12,28},{14,30},{16,0},... | collective-permute-start | bytes 497672 | tf_op jit(solution)/shard_map/ppermute | solution.py:333
  32.5 37.0 %collective-permute-start.3 = (bf16[2,72,576]{2,1,0:T(8,128)(2,1)S(1)}, bf16[2,72,576]{2,1,0:T(8,128)(2,1)S(1)}, u32[]{:S(2)}, u32[]{:S(2)}) collective-permute-start(bf16[2,72,576]{2,1,0:T(8,128)(2,1)S(1)} %pad_maximum_fusion.22), channel_id=1, source_target_pairs={{0,24},{2,26},{4,28},{6,30},{8,0},{10,2},{12,4},{14,6},{16,8},{18,... | collective-permute-start | bytes 497672 | tf_op jit(solution)/shard_map/ppermute | solution.py:333
  42.1 38.8 %collective-permute-start.4 = (bf16[2,72,576]{2,1,0:T(8,128)(2,1)S(1)}, bf16[2,72,576]{2,1,0:T(8,128)(2,1)S(1)}, u32[]{:S(2)}, u32[]{:S(2)}) collective-permute-start(bf16[2,72,576]{2,1,0:T(8,128)(2,1)S(1)} %pad_maximum_fusion.22), channel_id=1, source_target_pairs={{0,16},{2,18},{4,20},{6,22},{8,24},{10,26},{12,28},{14,30},{16,0},... | collective-permute-start | bytes 497672 | tf_op jit(solution)/shard_map/ppermute | solution.py:333
  44.2 23.6 %collective-permute-start.5 = (bf16[2,72,576]{2,1,0:T(8,128)(2,1)S(1)}, bf16[2,72,576]{2,1,0:T(8,128)(2,1)S(1)}, u32[]{:S(2)}, u32[]{:S(2)}) collective-permute-start(bf16[2,72,576]{2,1,0:T(8,128)(2,1)S(1)} %pad_maximum_fusion.22), channel_id=1, source_target_pairs={{0,8},{2,10},{4,12},{6,14},{8,16},{10,18},{12,20},{14,22},{16,24},... | collective-permute-start | bytes 497672 | tf_op jit(solution)/shard_map/ppermute | solution.py:333
  56.9 54.6 %collective-permute-start.12 = (bf16[4,1,72,1152]{3,2,1,0:T(8,128)(2,1)S(1)}, bf16[4,1,72,1152]{3,2,1,0:T(8,128)(2,1)S(1)}, u32[]{:S(2)}, u32[]{:S(2)}) collective-permute-start(bf16[4,1,72,1152]{3,2,1,0:T(8,128)(2,1)S(1)} %pad_maximum_fusion.15.refs_0_), channel_id=1, source_target_pairs={{0,4},{2,6},{4,0},{6,2},{8,12},{10,14},{12,8},{14,10},{16,20},{18,... | collective-permute-start | bytes 1990664 | tf_op jit(solution)/shard_map/ppermute | solution.py:333
  67.8 16.1 %collective-permute-start.7 = (bf16[1,72,1152]{2,1,0:T(8,128)(2,1)S(1)}, bf16[1,72,1152]{2,1,0:T(8,128)(2,1)S(1)}, u32[]{:S(2)}, u32[]{:S(2)}) collective-permute-start(bf16[1,72,1152]{2,1,0:T(8,128)(2,1)S(1)} %bitcast.173), channel_id=1, source_target_pairs={{0,24},{2,26},{4,28},{6,30},{8,0},{10,2},{12,4},{14,6},{16,8},{18,... | collective-permute-start | bytes 497672 | tf_op jit(solution)/shard_map/ppermute | solution.py:333
  69.6 39.6 %collective-permute-start.8 = (bf16[1,72,1152]{2,1,0:T(8,128)(2,1)S(1)}, bf16[1,72,1152]{2,1,0:T(8,128)(2,1)S(1)}, u32[]{:S(2)}, u32[]{:S(2)}) collective-permute-start(bf16[1,72,1152]{2,1,0:T(8,128)(2,1)S(1)} %bitcast.174), channel_id=1, source_target_pairs={{0,16},{2,18},{4,20},{6,22},{8,24},{10,26},{12,28},{14,30},{16,0},... | collective-permute-start | bytes 497672 | tf_op jit(solution)/shard_map/ppermute | solution.py:333
  80.9 29.7 %collective-permute-start.9 = (bf16[1,72,1152]{2,1,0:T(8,128)(2,1)S(1)}, bf16[1,72,1152]{2,1,0:T(8,128)(2,1)S(1)}, u32[]{:S(2)}, u32[]{:S(2)}) collective-permute-start(bf16[1,72,1152]{2,1,0:T(8,128)(2,1)S(1)} %bitcast.175), channel_id=1, source_target_pairs={{0,8},{2,10},{4,12},{6,14},{8,16},{10,18},{12,20},{14,22},{16,24},... | collective-permute-start | bytes 497672 | tf_op jit(solution)/shard_map/ppermute | solution.py:333
  83.8 495.9 %reduce-scatter.9.cloned.1.call-start = ((), (), s32[]{:S(2)}) async-start(), calls=%async_computation.5 | async-start | bytes 5640192 | tf_op jit(solution)/shard_map/reduce_scatter | solution.py:375
  84.0 47.7 %collective-permute-start.13 = (bf16[4,1,72,1152]{3,2,1,0:T(8,128)(2,1)S(1)}, bf16[4,1,72,1152]{3,2,1,0:T(8,128)(2,1)S(1)}, u32[]{:S(2)}, u32[]{:S(2)}) collective-permute-start(bf16[4,1,72,1152]{3,2,1,0:T(8,128)(2,1)S(1)} %pad_maximum_fusion.15.refs_0_), channel_id=1, source_target_pairs={{0,1},{1,0},{2,3},{3,2},{4,5},{5,4},{6,7},{7,6},{8,9},{9,8},{10,11... | collective-permute-start | bytes 1990664 | tf_op jit(solution)/shard_map/ppermute | solution.py:451
  109.2 19.4 %collective-permute-start.6 = (bf16[4,2,72,576]{3,2,1,0:T(8,128)(2,1)S(1)}, bf16[4,2,72,576]{3,2,1,0:T(8,128)(2,1)S(1)}, u32[]{:S(2)}, u32[]{:S(2)}) collective-permute-start(bf16[4,2,72,576]{3,2,1,0:T(8,128)(2,1)S(1)} %pad_maximum_fusion.14.refs_0_), channel_id=1, source_target_pairs={{0,4},{2,6},{4,0},{6,2},{8,12},{10,14},{12,8},{14,10},{16,20},{18,... | collective-permute-start | bytes 1990664 | tf_op jit(solution)/shard_map/ppermute | solution.py:333
  110.7 32.8 %collective-permute-start.18 = (bf16[4,1,72,1152]{3,2,1,0:T(8,128)(2,1)S(1)}, bf16[4,1,72,1152]{3,2,1,0:T(8,128)(2,1)S(1)}, u32[]{:S(2)}, u32[]{:S(2)}) collective-permute-start(bf16[4,1,72,1152]{3,2,1,0:T(8,128)(2,1)S(1)} %pad_maximum_fusion.16.refs_0_), channel_id=1, source_target_pairs={{0,4},{2,6},{4,0},{6,2},{8,12},{10,14},{12,8},{14,10},{16,20},{18,... | collective-permute-start | bytes 1990664 | tf_op jit(solution)/shard_map/ppermute | solution.py:333
  111.5 20.3 %collective-permute-start.14 = (bf16[4,1,72,1152]{3,2,1,0:T(8,128)(2,1)S(1)}, bf16[4,1,72,1152]{3,2,1,0:T(8,128)(2,1)S(1)}, u32[]{:S(2)}, u32[]{:S(2)}) collective-permute-start(bf16[4,1,72,1152]{3,2,1,0:T(8,128)(2,1)S(1)} %collective-permute-done.12.refs_1_), channel_id=1, source_target_pairs={{0,1},{1,0},{2,3},{3,2},{4,5},{5,4},{6,7},{7,6},{8,9},{9,8},{10,11... | collective-permute-start | bytes 1990664 | tf_op jit(solution)/shard_map/ppermute | solution.py:451
  139.8 29.0 %collective-permute-start.15 = (bf16[1,512,1152]{2,1,0:T(8,128)(2,1)S(1)}, bf16[1,512,1152]{2,1,0:T(8,128)(2,1)S(1)}, u32[]{:S(2)}, u32[]{:S(2)}) collective-permute-start(bf16[1,512,1152]{2,1,0:T(8,128)(2,1)S(1)} %get-tuple-element.116), channel_id=1, source_target_pairs={{0,1},{1,0},{2,3},{3,2},{4,5},{5,4},{6,7},{7,6},{8,9},{9,8},{10,11... | collective-permute-start | bytes 3538952 | tf_op jit(solution)/shard_map/ppermute | solution.py:451
  145.9 41.3 %collective-permute-start.17 = (bf16[1,512,1152]{2,1,0:T(8,128)(2,1)S(1)}, bf16[1,512,1152]{2,1,0:T(8,128)(2,1)S(1)}, u32[]{:S(2)}, u32[]{:S(2)}) collective-permute-start(bf16[1,512,1152]{2,1,0:T(8,128)(2,1)S(1)} %get-tuple-element.117), channel_id=1, source_target_pairs={{0,1},{1,0},{2,3},{3,2},{4,5},{5,4},{6,7},{7,6},{8,9},{9,8},{10,11... | collective-permute-start | bytes 3538952 | tf_op jit(solution)/shard_map/ppermute | solution.py:451
  255.6 331.8 %reduce-scatter.7.cloned.1.call-start = ((), (), s32[]{:S(2)}) async-start(), calls=%async_computation.4 | async-start | bytes 5640192 | tf_op jit(solution)/shard_map/reduce_scatter | solution.py:375
  288.1 26.1 %collective-permute-start.23 = (bf16[1024,1152]{1,0:T(8,128)(2,1)}, bf16[1024,1152]{1,0:T(8,128)(2,1)}, u32[]{:S(2)}, u32[]{:S(2)}) collective-permute-start(bf16[1024,1152]{1,0:T(8,128)(2,1)} %pad_maximum_fusion.3), channel_id=1, source_target_pairs={{0,2},{2,0},{4,6},{6,4},{8,10},{10,8},{12,14},{14,12},{16,18},{18,... | collective-permute-start | bytes 7077896 | tf_op jit(solution)/shard_map/ppermute | solution.py:333
  329.4 32.6 %collective-permute-start.24 = (bf16[288,1152]{1,0:T(8,128)(2,1)S(1)}, bf16[288,1152]{1,0:T(8,128)(2,1)S(1)}, u32[]{:S(2)}, u32[]{:S(2)}) collective-permute-start(bf16[288,1152]{1,0:T(8,128)(2,1)S(1)} %convolution_convert_fusion.2.refs_8_), channel_id=1, source_target_pairs={{0,4},{2,6},{4,0},{6,2},{8,12},{10,14},{12,8},{14,10},{16,20},{18,... | collective-permute-start | bytes 1990664 | tf_op jit(solution)/shard_map/ppermute | solution.py:333
  357.9 124.8 %collective-permute-start.26 = (bf16[1,512,1152]{2,1,0:T(8,128)(2,1)}, bf16[1,512,1152]{2,1,0:T(8,128)(2,1)S(1)}, u32[]{:S(2)}, u32[]{:S(2)}) collective-permute-start(bf16[1,512,1152]{2,1,0:T(8,128)(2,1)} %pad_maximum_fusion.10), channel_id=1, source_target_pairs={{0,1},{1,0},{2,3},{3,2},{4,5},{5,4},{6,7},{7,6},{8,9},{9,8},{10,11... | collective-permute-start | bytes 3538952 | tf_op jit(solution)/shard_map/ppermute | solution.py:451
  362.2 11.5 %collective-permute-start.51 = (bf16[72,1152]{1,0:T(8,128)(2,1)S(1)}, bf16[72,1152]{1,0:T(8,128)(2,1)S(1)}, u32[]{:S(2)}, u32[]{:S(2)}) collective-permute-start(bf16[72,1152]{1,0:T(8,128)(2,1)S(1)} %get-tuple-element.132.refs_8_), channel_id=1, source_target_pairs={{0,8},{2,10},{4,12},{6,14},{8,16},{10,18},{12,20},{14,22},{16,24},... | collective-permute-start | bytes 497672 | tf_op jit(solution)/shard_map/ppermute | solution.py:333
  366.5 20.3 %collective-permute-start.52 = (bf16[72,1152]{1,0:T(8,128)(2,1)S(1)}, bf16[72,1152]{1,0:T(8,128)(2,1)S(1)}, u32[]{:S(2)}, u32[]{:S(2)}) collective-permute-start(bf16[72,1152]{1,0:T(8,128)(2,1)S(1)} %get-tuple-element.134.refs_9_), channel_id=1, source_target_pairs={{0,16},{2,18},{4,20},{6,22},{8,24},{10,26},{12,28},{14,30},{16,0},... | collective-permute-start | bytes 497672 | tf_op jit(solution)/shard_map/ppermute | solution.py:333
  369.1 17.7 %collective-permute-start.53 = (bf16[72,1152]{1,0:T(8,128)(2,1)S(1)}, bf16[72,1152]{1,0:T(8,128)(2,1)S(1)}, u32[]{:S(2)}, u32[]{:S(2)}) collective-permute-start(bf16[72,1152]{1,0:T(8,128)(2,1)S(1)} %get-tuple-element.133.refs_10_), channel_id=1, source_target_pairs={{0,24},{2,26},{4,28},{6,30},{8,0},{10,2},{12,4},{14,6},{16,8},{18,... | collective-permute-start | bytes 497672 | tf_op jit(solution)/shard_map/ppermute | solution.py:333
  417.9 39.4 %collective-permute-start.54 = (bf16[72,1152]{1,0:T(8,128)(2,1)}, bf16[72,1152]{1,0:T(8,128)(2,1)}, u32[]{:S(2)}, u32[]{:S(2)}) collective-permute-start(bf16[72,1152]{1,0:T(8,128)(2,1)} %get-tuple-element.101), channel_id=1, source_target_pairs={{0,1},{1,0},{2,3},{3,2},{4,5},{5,4},{6,7},{7,6},{8,9},{9,8},{10,11... | collective-permute-start | bytes 497672 | tf_op jit(solution)/shard_map/ppermute | solution.py:502
  419.7 67.3 %collective-permute-start.27 = (bf16[1,512,1152]{2,1,0:T(8,128)(2,1)}, bf16[1,512,1152]{2,1,0:T(8,128)(2,1)}, u32[]{:S(2)}, u32[]{:S(2)}) collective-permute-start(bf16[1,512,1152]{2,1,0:T(8,128)(2,1)} %pad_maximum_fusion.11), channel_id=1, source_target_pairs={{0,1},{1,0},{2,3},{3,2},{4,5},{5,4},{6,7},{7,6},{8,9},{9,8},{10,11... | collective-permute-start | bytes 3538952 | tf_op jit(solution)/shard_map/ppermute | solution.py:451
  421.4 30.1 %collective-permute-start.34 = (bf16[576,576]{1,0:T(8,128)(2,1)}, bf16[576,576]{1,0:T(8,128)(2,1)}, u32[]{:S(2)}, u32[]{:S(2)}) collective-permute-start(bf16[576,576]{1,0:T(8,128)(2,1)} %convolution_convert_fusion.10), channel_id=1, source_target_pairs={{0,4},{2,6},{4,0},{6,2},{8,12},{10,14},{12,8},{14,10},{16,20},{18,... | collective-permute-start | bytes 1990664 | tf_op jit(solution)/shard_map/ppermute | solution.py:333
  452.8 12.9 %collective-permute-start.35 = (bf16[144,576]{1,0:T(8,128)(2,1)S(1)}, bf16[144,576]{1,0:T(8,128)(2,1)S(1)}, u32[]{:S(2)}, u32[]{:S(2)}) collective-permute-start(bf16[144,576]{1,0:T(8,128)(2,1)S(1)} %get-tuple-element.129), channel_id=1, source_target_pairs={{0,8},{2,10},{4,12},{6,14},{8,16},{10,18},{12,20},{14,22},{16,24},... | collective-permute-start | bytes 497672 | tf_op jit(solution)/shard_map/ppermute | solution.py:333
  457.3 19.8 %collective-permute-start.36 = (bf16[144,576]{1,0:T(8,128)(2,1)S(1)}, bf16[144,576]{1,0:T(8,128)(2,1)S(1)}, u32[]{:S(2)}, u32[]{:S(2)}) collective-permute-start(bf16[144,576]{1,0:T(8,128)(2,1)S(1)} %get-tuple-element.131), channel_id=1, source_target_pairs={{0,16},{2,18},{4,20},{6,22},{8,24},{10,26},{12,28},{14,30},{16,0},... | collective-permute-start | bytes 497672 | tf_op jit(solution)/shard_map/ppermute | solution.py:333
  457.3 23.0 %collective-permute-start.37 = (bf16[144,576]{1,0:T(8,128)(2,1)S(1)}, bf16[144,576]{1,0:T(8,128)(2,1)S(1)}, u32[]{:S(2)}, u32[]{:S(2)}) collective-permute-start(bf16[144,576]{1,0:T(8,128)(2,1)S(1)} %get-tuple-element.130), channel_id=1, source_target_pairs={{0,24},{2,26},{4,28},{6,30},{8,0},{10,2},{12,4},{14,6},{16,8},{18,... | collective-permute-start | bytes 497672 | tf_op jit(solution)/shard_map/ppermute | solution.py:333
  465.7 35.8 %collective-permute-start.25 = (bf16[512,1152]{1,0:T(8,128)(2,1)S(1)}, bf16[512,1152]{1,0:T(8,128)(2,1)S(1)}, u32[]{:S(2)}, u32[]{:S(2)}) collective-permute-start(bf16[512,1152]{1,0:T(8,128)(2,1)S(1)} %slice.710), channel_id=1, source_target_pairs={{0,2},{2,0},{4,6},{6,4},{8,10},{10,8},{12,14},{14,12},{16,18},{18,... | collective-permute-start | bytes 3538952 | tf_op jit(solution)/shard_map/ppermute | solution.py:333
  491.2 23.1 %collective-permute-start.45 = (bf16[576,576]{1,0:T(8,128)(2,1)}, bf16[576,576]{1,0:T(8,128)(2,1)}, u32[]{:S(2)}, u32[]{:S(2)}) collective-permute-start(bf16[576,576]{1,0:T(8,128)(2,1)} %convolution_convert_fusion.6), channel_id=1, source_target_pairs={{0,4},{2,6},{4,0},{6,2},{8,12},{10,14},{12,8},{14,10},{16,20},{18,... | collective-permute-start | bytes 1990664 | tf_op jit(solution)/shard_map/ppermute | solution.py:333
  494.6 15.6 %collective-permute-start.39 = (bf16[576,576]{1,0:T(8,128)(2,1)}, bf16[576,576]{1,0:T(8,128)(2,1)}, u32[]{:S(2)}, u32[]{:S(2)}) collective-permute-start(bf16[576,576]{1,0:T(8,128)(2,1)} %convolution_convert_fusion.8), channel_id=1, source_target_pairs={{0,1},{1,0},{2,3},{3,2},{4,5},{5,4},{6,7},{7,6},{8,9},{9,8},{10,11... | collective-permute-start | bytes 1990664 | tf_op jit(solution)/shard_map/ppermute | solution.py:451
  501.2 54.2 %collective-permute-start.28 = (bf16[512,1152]{1,0:T(8,128)(2,1)}, bf16[512,1152]{1,0:T(8,128)(2,1)S(1)}, u32[]{:S(2)}, u32[]{:S(2)}) collective-permute-start(bf16[512,1152]{1,0:T(8,128)(2,1)} %slice.709), channel_id=1, source_target_pairs={{0,2},{2,0},{4,6},{6,4},{8,10},{10,8},{12,14},{14,12},{16,18},{18,... | collective-permute-start | bytes 3538952 | tf_op jit(solution)/shard_map/ppermute | solution.py:333
  512.3 15.8 %collective-permute-start.40 = (bf16[288,576]{1,0:T(8,128)(2,1)}, bf16[288,576]{1,0:T(8,128)(2,1)S(1)}, u32[]{:S(2)}, u32[]{:S(2)}) collective-permute-start(bf16[288,576]{1,0:T(8,128)(2,1)} %get-tuple-element.128), channel_id=1, source_target_pairs={{0,4},{2,6},{4,0},{6,2},{8,12},{10,14},{12,8},{14,10},{16,20},{18,... | collective-permute-start | bytes 995336 | tf_op jit(solution)/shard_map/ppermute | solution.py:333
  515.7 17.3 %collective-permute-start.46 = (bf16[144,576]{1,0:T(8,128)(2,1)S(1)}, bf16[144,576]{1,0:T(8,128)(2,1)S(1)}, u32[]{:S(2)}, u32[]{:S(2)}) collective-permute-start(bf16[144,576]{1,0:T(8,128)(2,1)S(1)} %get-tuple-element.124), channel_id=1, source_target_pairs={{0,8},{2,10},{4,12},{6,14},{8,16},{10,18},{12,20},{14,22},{16,24},... | collective-permute-start | bytes 497672 | tf_op jit(solution)/shard_map/ppermute | solution.py:333
  524.6 16.3 %collective-permute-start.47 = (bf16[144,576]{1,0:T(8,128)(2,1)S(1)}, bf16[144,576]{1,0:T(8,128)(2,1)S(1)}, u32[]{:S(2)}, u32[]{:S(2)}) collective-permute-start(bf16[144,576]{1,0:T(8,128)(2,1)S(1)} %get-tuple-element.126), channel_id=1, source_target_pairs={{0,16},{2,18},{4,20},{6,22},{8,24},{10,26},{12,28},{14,30},{16,0},... | collective-permute-start | bytes 497672 | tf_op jit(solution)/shard_map/ppermute | solution.py:333
  528.1 17.9 %collective-permute-start.48 = (bf16[144,576]{1,0:T(8,128)(2,1)S(1)}, bf16[144,576]{1,0:T(8,128)(2,1)S(1)}, u32[]{:S(2)}, u32[]{:S(2)}) collective-permute-start(bf16[144,576]{1,0:T(8,128)(2,1)S(1)} %get-tuple-element.125), channel_id=1, source_target_pairs={{0,24},{2,26},{4,28},{6,30},{8,0},{10,2},{12,4},{14,6},{16,8},{18,... | collective-permute-start | bytes 497672 | tf_op jit(solution)/shard_map/ppermute | solution.py:333
  528.2 20.9 %collective-permute-start.41 = (bf16[72,576]{1,0:T(8,128)(2,1)S(1)}, bf16[72,576]{1,0:T(8,128)(2,1)S(1)}, u32[]{:S(2)}, u32[]{:S(2)}) collective-permute-start(bf16[72,576]{1,0:T(8,128)(2,1)S(1)} %get-tuple-element.159), channel_id=1, source_target_pairs={{0,8},{2,10},{4,12},{6,14},{8,16},{10,18},{12,20},{14,22},{16,24},... | collective-permute-start | bytes 248840 | tf_op jit(solution)/shard_map/ppermute | solution.py:333
  533.1 17.4 %collective-permute-start.42 = (bf16[72,576]{1,0:T(8,128)(2,1)S(1)}, bf16[72,576]{1,0:T(8,128)(2,1)S(1)}, u32[]{:S(2)}, u32[]{:S(2)}) collective-permute-start(bf16[72,576]{1,0:T(8,128)(2,1)S(1)} %get-tuple-element.161), channel_id=1, source_target_pairs={{0,16},{2,18},{4,20},{6,22},{8,24},{10,26},{12,28},{14,30},{16,0},... | collective-permute-start | bytes 248840 | tf_op jit(solution)/shard_map/ppermute | solution.py:333
  561.0 18.9 %collective-permute-start.50 = (bf16[72,1728]{1,0:T(8,128)(2,1)S(1)}, bf16[72,1728]{1,0:T(8,128)(2,1)S(1)}, u32[]{:S(2)}, u32[]{:S(2)}) collective-permute-start(bf16[72,1728]{1,0:T(8,128)(2,1)S(1)} %slice.711), channel_id=1, source_target_pairs={{0,2},{2,0},{4,6},{6,4},{8,10},{10,8},{12,14},{14,12},{16,18},{18,... | collective-permute-start | bytes 746504 | tf_op jit(solution)/shard_map/ppermute | solution.py:333
  579.6 17.3 %collective-permute-start.57 = (bf16[144,2152]{1,0:T(8,128)(2,1)}, bf16[144,2152]{1,0:T(8,128)(2,1)S(1)}, u32[]{:S(2)}, u32[]{:S(2)}) collective-permute-start(bf16[144,2152]{1,0:T(8,128)(2,1)} %reduce-scatter.9.cloned.1.call-done), channel_id=1, source_target_pairs={{0,1},{1,0},{2,3},{3,2},{4,5},{5,4},{6,7},{7,6},{8,9},{9,8},{10,11... | collective-permute-start | bytes 1859336 | tf_op jit(solution)/shard_map/ppermute | solution.py:502
  587.4 19.7 %collective-permute-start.55 = (bf16[144,2152]{1,0:T(8,128)(2,1)}, bf16[144,2152]{1,0:T(8,128)(2,1)S(1)}, u32[]{:S(2)}, u32[]{:S(2)}) collective-permute-start(bf16[144,2152]{1,0:T(8,128)(2,1)} %reduce-scatter.7.cloned.1.call-done), channel_id=1, source_target_pairs={{0,1},{1,0},{2,3},{3,2},{4,5},{5,4},{6,7},{7,6},{8,9},{9,8},{10,11... | collective-permute-start | bytes 1859336 | tf_op jit(solution)/shard_map/ppermute | solution.py:502
  597.1 10.3 %collective-permute-start.58 = (bf16[72,2152]{1,0:T(8,128)(2,1)S(1)}, bf16[72,2152]{1,0:T(8,128)(2,1)S(1)}, u32[]{:S(2)}, u32[]{:S(2)}) collective-permute-start(bf16[72,2152]{1,0:T(8,128)(2,1)S(1)} %select_convert_fusion), channel_id=1, source_target_pairs={{0,2},{2,0},{4,6},{6,4},{8,10},{10,8},{12,14},{14,12},{16,18},{18,... | collective-permute-start | bytes 929672 | tf_op jit(solution)/shard_map/ppermute | solution.py:333
  (105 other events, 1514.6 us)
Sparse Core Ops, SparseCore 0:
  12.5 123.9 all-gather.4
  138.7 82.6 all-gather.6
  255.7 106.8 reduce-scatter.8
  366.6 126.0 reduce-scatter.6

commit v2 on v1

--- a/solution.py
+++ b/solution.py
@@ -229,10 +229,35 @@
     return results[0], results[1 : 1 + parts], results[1 + parts :]
 
 
-def contract_rows(left_rows, right_rows):
-    return lax.dot_general(
-        left_rows, right_rows, (((0,), (0,)), ((), ())), preferred_element_type=f32
-    )
+def contract_kernel(left, right, out, turned):
+    @pl.when(pl.program_id(0) == 0)
+    def _():
+        turned[...] = jnp.transpose(left[...])
+
+    out[...] = nn(turned[...], right[...]).astype(bf16)
+
+
+def contract_rows(left, right, block=512):
+    rows, width = left.shape
+    columns = right.shape[1]
+    block = min(block, columns)
+    return pl.pallas_call(
+        contract_kernel,
+        grid=(pl.cdiv(columns, block),),
+        in_specs=[
+            pl.BlockSpec((rows, width), lambda step: (0, 0)),
+            pl.BlockSpec((rows, block), lambda step: (0, step)),
+        ],
+        out_specs=pl.BlockSpec((width, block), lambda step: (0, step)),
+        out_shape=jax.ShapeDtypeStruct((width, columns), bf16),
+        scratch_shapes=[pltpu.VMEM((width, rows), bf16)],
+        compiler_params=pltpu.CompilerParams(vmem_limit_bytes=40 * 1024 * 1024),
+        cost_estimate=pl.CostEstimate(
+            flops=2 * rows * width * columns,
+            bytes_accessed=2 * (rows * width + (rows + width) * columns),
+            transcendentals=0,
+        ),
+    )(left, right)
 
 
 def column_sum(tensor):
@@ -241,6 +266,10 @@
 
 def after(value, *earlier):
     return lax.optimization_barrier((value, *earlier))[0]
+
+
+def together(*values):
+    return lax.optimization_barrier(values)
 
 
 def norm_parts(tensor):
@@ -348,6 +377,16 @@
             for step in range(2)
         ]
 
+    def kinds_by_seq(self):
+        kinds = [
+            [self.index(member // 2, member % 2, twin) for member in range(2 * self.depth)]
+            for twin in range(2)
+        ]
+        first = lax.axis_index("seq") == 0
+        return [jnp.where(first, one, two) for one, two in zip(*kinds)] + [
+            jnp.where(first, two, one) for one, two in zip(*kinds)
+        ]
+
     def shards_by_seq(self):
         mine = self.shards()
         first = lax.axis_index("seq") == 0
@@ -402,7 +441,11 @@
 
 
 def reorder(rows, matrix):
-    return jnp.dot(rows, matrix, preferred_element_type=f32).astype(bf16)
+    half = matrix.shape[1] // 2
+    return [
+        jnp.dot(rows, part, preferred_element_type=f32).astype(bf16)
+        for part in (matrix[:, :half], matrix[:, half:])
+    ]
 
 
 def gather_z(grid, block):
@@ -424,16 +467,16 @@
     return jnp.where(lax.axis_index("seq") == 0, first_value, second_value)
 
 
-def gather_by_seq(grid, block):
+def gather_by_seq(grid, block, *beside):
     lines = gather_z(grid, by_seq(block[:1], block[1:]))
-    joined, across = gather_x(grid, lines)
-    return lines, [joined, across, swap_seq(joined), swap_seq(across)]
+    joined, *beside = together(jnp.stack(lines), *beside)
+    across = grid.send(joined, step_x=1)
+    return lines, [joined, across, swap_seq(joined), swap_seq(across)], beside
 
 
 def halves_of(left, right):
-    half = left.shape[1] // 2
-    going = contract_rows(left[:, half:], right).astype(bf16)
-    return contract_rows(left[:, :half], right).astype(bf16), going
+    going = contract_rows(left[1], right)
+    return contract_rows(left[0], right), going
 
 
 def add_pieces(kept, came, count):
@@ -564,41 +607,53 @@
         other = grid.send(grid.other_half(halves), step_twin=1)
         return jnp.stack([grid.own_half(halves), other])
 
+    def both(value):
+        flat = value.reshape(rows, width)
+        return jnp.concatenate([flat, grid.send(flat, step_twin=1)], axis=0)
+
     qkv_block = pair_up(by_kind(qkv_weight))
     pair_block = qkv_block[:, :, own_width:]
     all_kinds = jnp.stack(grid.shards())
-    up_block = pair_up(two_halves(up_weight))
-    down_block = pair_up(two_halves(down_weight.T))
-    own_up = grid.gather(jnp.stack(grid.in_order(*up_block)))
-    own_down = grid.gather(jnp.stack(grid.in_order(*down_block)))
+    order = order_matrix(grid.shards(), shard_rows)
+    own_order = order_matrix(grid.members(), shard_rows)
+    inputs = both(tokens).astype(f32)
+    normal_one, scale_one = norm_parts(inputs)
+    normed_one = (normal_one * attn_gain + attn_shift).astype(bf16)
+    up_weight, down_turned = after((up_weight, down_weight.T), qkv_block)
+    up_block = jnp.stack(grid.in_order(*pair_up(two_halves(up_weight))))
+    down_block = jnp.stack(grid.in_order(*pair_up(two_halves(down_turned))))
+    sizes = jnp.concatenate([lengths, grid.send(lengths, step_twin=1)])
     if groups == 2:
-        pair_lines, pair_pieces = gather_by_seq(grid, pair_block)
+        scatter_seq, seq_order = ScatterY, order_matrix(grid.shards_by_seq(), shard_rows)
+        pair_lines, pair_pieces, (normed_one, up_block, down_block, sizes) = gather_by_seq(
+            grid, pair_block, normed_one, up_block, down_block, sizes
+        )
         pair_slots = jnp.stack(grid.shards_by_seq())
     else:
+        scatter_seq, seq_order = ScatterX, order
         pair_lines, pair_pieces = gather_all(grid, pair_block)
         pair_slots = all_kinds
     query_lines, query_pieces = gather_all(
-        grid, after(qkv_block[:, :, :own_width], pair_lines[-1])
-    )
-    out_lines, out_pieces = gather_all(grid, after(out_weight[None], query_lines[-1]))
-
-    def both(value):
-        flat = value.reshape(rows, width)
-        return jnp.concatenate([flat, grid.send(flat, step_twin=1)], axis=0)
-
-    inputs = both(tokens).astype(f32)
+        grid, after(qkv_block[:, :, :own_width], *pair_lines[1:])
+    )
+    out_lines, out_pieces = gather_all(grid, after(out_weight[None], *query_lines[1:]))
+
+    down_block = after(down_block, pair_pieces[1])
+    if groups == 2:
+        kinds_by_seq = jnp.stack(grid.kinds_by_seq())
+        own_down = lax.all_gather(
+            by_seq(down_block[0], down_block[1])[None],
+            "fsdp",
+            axis_index_groups=grid.groups(),
+        )
+        own_down = [own_down, swap_seq(own_down)]
+    else:
+        own_down = grid.gather(down_block)
+    up_block = after(up_block, *query_lines[1:])
+    own_up = grid.gather(up_block)
+
     back_low = both(cotangent)
-    sizes = jnp.concatenate([lengths, grid.send(lengths, step_twin=1)])
-
-    order = order_matrix(grid.shards(), shard_rows)
-    if groups == 2:
-        scatter_seq, seq_order = ScatterY, order_matrix(grid.shards_by_seq(), shard_rows)
-    else:
-        scatter_seq, seq_order = ScatterX, order
-    own_order = order_matrix(grid.members(), shard_rows)
-
-    normal_one, scale_one = norm_parts(inputs)
-    normed_one = (normal_one * attn_gain + attn_shift).astype(bf16)
+
     own_pair = place(pair_pieces, pair_slots, query_lines[1:]).reshape(width, 2 * own_width)
     pair_bias = jnp.concatenate([jnp.zeros((own_width,), f32), vector_kind(value_bias)])
     pairs = (jnp.dot(normed_one, own_pair, preferred_element_type=f32) + pair_bias).astype(bf16)
@@ -607,6 +662,13 @@
     queries = (
         jnp.dot(normed_one, own_query, preferred_element_type=f32) + vector_kind(query_bias)
     ).astype(bf16)
+
+    one_rows = reorder(normed_one, order)
+    seq_rows = reorder(normed_one, seq_order) if groups == 2 else one_rows
+    kind_rows = []
+    if groups == 2:
+        kind_rows = reorder(back_low, order_matrix(grid.kinds_by_seq(), shard_rows))
+    made = [*one_rows, *seq_rows, *kind_rows]
 
     place_seq = lax.axis_index("seq") * local_len
     attended_parts, saved = [], []
@@ -623,7 +685,9 @@
             key_parts = (lax.all_gather(key, "seq", axis=1, tiled=True),)
             value_parts = (lax.all_gather(value, "seq", axis=1, tiled=True),)
             info = jnp.stack([sizes[image], jnp.zeros_like(sizes[image])])
-        attended_part, lse = attend(info, query, key_parts, value_parts)
+        attended_part, lse = attend(
+            info, query, key_parts, value_parts, made if image == 0 else ()
+        )
         attended_parts.append(attended_part[0])
         saved.append((info, query, key_parts, value_parts, lse))
     attended = jnp.concatenate(attended_parts, axis=0)
@@ -635,16 +699,22 @@
     normal_two, scale_two = norm_parts(resid)
     normed_two = (normal_two * mlp_gain + mlp_shift).astype(bf16)
     own_up_bias = grid.own_half([up_bias[:hidden_half], up_bias[hidden_half:]])
+    if groups == 2:
+        normed_two, own_down[1] = together(normed_two, own_down[1])
     hidden = jnp.dot(normed_two, own_up, preferred_element_type=f32) + own_up_bias
     active, slope = gelu_and_slope(hidden)
     active, slope = lax.optimization_barrier((active.astype(bf16), slope.astype(bf16)))
-    grad_down = contract_rows(back_low, active).astype(bf16)
-    back_low, grad_down = lax.optimization_barrier((back_low, grad_down))
-    grad_down = grid.scatter(grad_down)
+    if groups == 2:
+        down_kept, down_going = halves_of(kind_rows, active)
+        down_came = swap_seq(down_going)
+        own_down = place(own_down, kinds_by_seq, [down_kept, down_going])
+        own_down = own_down.reshape(width, hidden_half)
+    else:
+        grad_down = grid.scatter(contract_rows(back_low, active))
 
     d_active = jnp.dot(back_low, own_down, preferred_element_type=f32)
     d_hidden = (d_active * slope).astype(bf16)
-    grad_up = contract_rows(normed_two, d_hidden).astype(bf16)
+    grad_up = contract_rows(normed_two, d_hidden)
     d_hidden, grad_up = lax.optimization_barrier((d_hidden, grad_up))
     grad_up = grid.scatter(grad_up)
     partial = lax.dot_general(
@@ -664,8 +734,11 @@
         info, query, key_parts, value_parts, lse = saved[image]
         if image == 0:
             on_their_way = [grad_out.kept, grad_out.going]
+        elif image == images and groups == 2:
+            on_their_way = add_pieces(down_kept, down_came, 1)
+            down_total = on_their_way[0]
         else:
-            on_their_way = grad_out.add() if image == images else []
+            on_their_way = []
         d_query_part, key_grads, value_grads = attend_back(
             info,
             query,
@@ -677,7 +750,11 @@
         )
         d_query.append(d_query_part[0])
         if groups == 2:
-            far = swap_seq(jnp.concatenate([key_grads[1], value_grads[1]], axis=2))
+            near = jnp.concatenate([key_grads[1], value_grads[1]], axis=2)
+            d_query[-1], near = together(d_query[-1], near)
+            far = swap_seq(near)
+            if image == 2 * images - 1:
+                last_far = far
             d_key.append((key_grads[0], far[:, :, :own_width]))
             d_value.append((value_grads[0], far[:, :, own_width:]))
         else:
@@ -690,14 +767,21 @@
                     )
                 )
     d_query = jnp.concatenate(d_query, axis=0)
-    one_rows = reorder(normed_one, order)
     grad_query = ScatterX(grid, one_rows, d_query)
-    late_active, grad_query.kept = lax.optimization_barrier((active, grad_query.kept))
+    late_active, grad_query.kept, grad_query.going = together(
+        active, grad_query.kept, grad_query.going
+    )
     partial = lax.dot_general(
         late_active, own_down, (((1,), (1,)), ((), ())), preferred_element_type=f32
     )
     came = grid.send(partial[rows:].astype(bf16), step_twin=1).astype(f32)
     outputs = (resid[:rows] + partial[:rows] + came + down_bias).astype(bf16)
+    grad_out.add()
+    grad_query.add()
+    if groups == 2:
+        last_far, grad_up, *grad_query.sums = together(last_far, grad_up, *grad_query.sums)
+        d_key[-1] = (d_key[-1][0], last_far[:, :, :own_width])
+        d_value[-1] = (d_value[-1][0], last_far[:, :, own_width:])
 
     d_key, d_value = (
         jnp.concatenate(
@@ -705,8 +789,19 @@
         )
         for member in (d_key, d_value)
     )
-    grad_key = scatter_seq(grid, reorder(normed_one, seq_order), d_key)
+    grad_key = scatter_seq(grid, seq_rows, d_key)
     grad_value = ScatterX(grid, one_rows, d_value)
+    d_query, d_key, d_value, grad_key.kept, grad_key.going, grad_value.kept, grad_value.going = (
+        together(
+            d_query,
+            d_key,
+            d_value,
+            grad_key.kept,
+            grad_key.going,
+            grad_value.kept,
+            grad_value.going,
+        )
+    )
     partial = sum(
         lax.dot_general(member, weight, (((1,), (1,)), ((), ())), preferred_element_type=f32)
         for member, weight in (
@@ -716,23 +811,40 @@
         )
     )
     d_one = partial[:rows] + grid.send(partial[rows:].astype(bf16), step_twin=1).astype(f32)
-    grad_tokens = d_resid[:rows] + norm_back(d_one, normal_one[:rows], scale_one[:rows], attn_gain)
-    grad_query.add()
+    grad_value.add()
     if groups == 2:
         grad_key.cross()
-    grad_value.add()
+        d_one, grad_key.going, *grad_value.sums = together(
+            d_one, grad_key.going, *grad_value.sums
+        )
+    grad_tokens = d_resid[:rows] + norm_back(d_one, normal_one[:rows], scale_one[:rows], attn_gain)
     grad_key.add()
     grad_out = grad_out.finish()
-    grad_up, grad_down = sum_seq(grad_up), sum_seq(grad_down)
+    grad_up = sum_seq(grad_up)
+    if groups == 2:
+        grad_down = lax.psum_scatter(
+            down_total,
+            "fsdp",
+            scatter_dimension=0,
+            axis_index_groups=grid.groups(),
+            tiled=True,
+        )
+        grad_down, *grad_key.sums = together(grad_down, *grad_key.sums)
+        other = swap_seq(grad_down)
+        grad_down = by_seq(
+            jnp.concatenate([grad_down, other]), jnp.concatenate([other, grad_down])
+        ).astype(f32)
+    else:
+        grad_down = sum_seq(grad_down)
     grad_qkv = jnp.concatenate(
         [grad_query.finish(), grad_key.finish(), grad_value.finish()], axis=1
     )
 
-    def by_kinds(total):
-        half = total.shape[0] // 2
-        return jnp.concatenate(grid.swap_mine(total[:half], total[half:]), axis=1)
-
-    grad_up, grad_down = by_kinds(grad_up), by_kinds(grad_down).T
+    grad_up, grad_down = (
+        jnp.concatenate(grid.swap_mine(total[:shard_rows], total[shard_rows:]), axis=1)
+        for total in (grad_up, grad_down)
+    )
+    grad_down = grad_down.T
     grad_qkv = jnp.stack(
         [member.reshape(shard_rows, 3, heads // 2, HD) for member in swap_twin(grid, grad_qkv)],
         axis=3,

time: 625 us -> 675 us (1.080)
  Pallas kernels: 88.7 us -> 127 us
  waiting for transfers between devices: 174 us -> 205 us
  other arithmetic: 73.5 us -> 101 us
  matrix products: 110 us -> 88.5 us
  starting transfers between devices: 108 us -> 87.8 us
  local copies, waits for them, and re-layouts: 46.1 us -> 38 us
    ppermute x8 -> x11, waiting for transfers between devices: 27.5 us -> 91.5 us  [swap_seq(): return lax.ppermute(value, 'seq', [(0, 1), (1, 0)])]
    ppermute x41, waiting for transfers between devices: 119 us -> 71.8 us  [send(): return lax.ppermute(value, 'fsdp', self.pairs(**steps))]
    pallas_call x0 -> x11, Pallas kernels: none -> 37.7 us  [contract_rows(): pl.pallas_call(contract_kernel, grid=(pl.cdiv(columns, block),), in_specs...]
    ppermute x41, starting transfers between devices: 84.2 us -> 61.3 us  [send(): return lax.ppermute(value, 'fsdp', self.pairs(**steps))]
    dot_general x13 -> x8, matrix products: 48.1 us -> 26 us  [reorder(): jnp.dot(rows, part, preferred_element_type=f32).astype(bf16)]
    unnamed x188 -> x211, local copies, waits for them, and re-layouts: 23.7 us -> 11 us
    ppermute x5 -> x4, waiting for transfers between devices: 21.3 us -> 29.6 us  [sum_seq(): lax.ppermute(value, 'seq', [(0, 1), (1, 0)]).astype(f32)]
  transfers between devices with their start and end apart: 63 -> 65, of which waited for: 27 -> 28; matrix products, arithmetic and copies ran while one was open for 35% -> 29% of each run, Pallas kernels for 14% -> 16%
where the time goes in v2:
time: 675 us; the launch traced here: 664 us
  waiting for transfers between devices  205 us (30%)
  Pallas kernels  127 us (19%)
  other arithmetic  101 us (15%)
  matrix products  88.5 us (13%)
  starting transfers between devices  87.8 us (13%)
  local copies, waits for them, and re-layouts  38 us (6%)
  between operations  16.8 us (2%)
    ppermute x11, waiting for transfers between devices, swap_seq(): return lax.ppermute(value, 'seq', [(0, 1), (1, 0)])  91.5 us
    ppermute x41, waiting for transfers between devices, send(): return lax.ppermute(value, 'fsdp', self.pairs(**steps))  71.8 us
    ppermute x41, starting transfers between devices, send(): return lax.ppermute(value, 'fsdp', self.pairs(**steps))  61.3 us
    pallas_call x2, Pallas kernels, attend_back(): pl.pallas_call(functools.partial(attend_back_kernel, parts, heads, min(bl...  49.5 us
    pallas_call x11, Pallas kernels, contract_rows(): pl.pallas_call(contract_kernel, grid=(pl.cdiv(columns, block),), in_specs...  37.7 us
    ppermute x4, waiting for transfers between devices, sum_seq(): lax.ppermute(value, 'seq', [(0, 1), (1, 0)]).astype(f32)  29.6 us
    pallas_call x2, Pallas kernels, attend(): pl.pallas_call(functools.partial(attend_kernel, parts, heads, min(block,...  29.3 us
    dot_general x8, matrix products, reorder(): jnp.dot(rows, part, preferred_element_type=f32).astype(bf16)  26 us
  transfers between devices with their start and end apart: 65, of which 28 were waited for; matrix products, arithmetic and copies ran while one was open for 29% of the time, Pallas kernels for 16%

profile of v2, /device:TPU:0, one launch (start us, length us, event | category | flops | bytes accessed | tf_op | source)
XLA Modules:
  0.0 663.9 jit_solution(15803115244625045054)
XLA Ops:
  12.1 4.5 reshape.784
  35.6 5.9 collective-permute-done.3
  44.7 3.9 fusion
  50.8 14.5 %collective-permute-done.15.refs_1_ = bf16[4,1,72,1152]{3,2,1,0:T(8,128)(2,1)S(1)} collective-permute-done((bf16[4,1,72,1152]{3,2,1,0:T(8,128)(2,1)S(1)}, bf16[4,1,72,1152]{3,2,1,0:T(8,128)(2,1)S(1)}, u32[]{:S(2)}, u32[]{:S(2)}) %collective-permute-start.15) | collective-permute-done | bytes 663584 | tf_op jit(solution)/shard_map/ppermute | solution.py:362
  72.7 4.1 collective-permute-start.10
  81.6 3.9 collective-permute-done.10.refs_6_
  85.5 11.3 %collective-permute-done.9.refs_5_ = bf16[2,72,576]{2,1,0:T(8,128)(2,1)S(1)} collective-permute-done((bf16[2,72,576]{2,1,0:T(8,128)(2,1)S(1)}, bf16[2,72,576]{2,1,0:T(8,128)(2,1)S(1)}, u32[]{:S(2)}, u32[]{:S(2)}) %collective-permute-start.9) | collective-permute-done | bytes 165920 | tf_op jit(solution)/shard_map/ppermute | solution.py:362
  98.0 6.9 %collective-permute-start.14 = (bf16[1,72,1152]{2,1,0:T(8,128)(2,1)}, bf16[1,72,1152]{2,1,0:T(8,128)(2,1)S(1)}, u32[]{:S(2)}, u32[]{:S(2)}) collective-permute-start(bf16[1,72,1152]{2,1,0:T(8,128)(2,1)} %bitcast.33), channel_id=1, source_target_pairs={{0,8},{2,10},{4,12},{6,14},{8,16},{10,18},{12,20},{14,22},{16,24},... | collective-permute-start | bytes 497672 | tf_op jit(solution)/shard_map/ppermute | solution.py:362
  111.6 12.0 %collective-permute-done.13.refs_3_ = bf16[1,72,1152]{2,1,0:T(8,128)(2,1)S(1)} collective-permute-done((bf16[1,72,1152]{2,1,0:T(8,128)(2,1)}, bf16[1,72,1152]{2,1,0:T(8,128)(2,1)S(1)}, u32[]{:S(2)}, u32[]{:S(2)}) %collective-permute-start.13) | collective-permute-done | bytes 165920 | tf_op jit(solution)/shard_map/ppermute | solution.py:362
  130.1 5.4 fusion.25.refs_6_.left
  138.5 3.6 fusion.31.refs_8_.left
  142.1 4.7 fusion.37.refs_10_.left
  146.7 4.6 fusion.34.refs_9_.left
  153.2 3.6 fusion.28.refs_7_.left
  159.4 6.0 collective-permute-done.17.refs_3_
  165.4 3.5 shard_map.272
  169.0 3.8 add_convert_fusion.3
  180.8 21.1 %collective-permute-done.18 = bf16[1,512,1152]{2,1,0:T(8,128)(2,1)S(1)} collective-permute-done((bf16[1,512,1152]{2,1,0:T(8,128)(2,1)S(1)}, bf16[1,512,1152]{2,1,0:T(8,128)(2,1)S(1)}, u32[]{:S(2)}, u32[]{:S(2)}) %collective-permute-start.18) | collective-permute-done | bytes 1179680 | tf_op jit(solution)/shard_map/ppermute | solution.py:494
  202.3 20.3 %collective-permute-done.20 = bf16[1,512,1152]{2,1,0:T(8,128)(2,1)S(1)} collective-permute-done((bf16[1,512,1152]{2,1,0:T(8,128)(2,1)S(1)}, bf16[1,512,1152]{2,1,0:T(8,128)(2,1)S(1)}, u32[]{:S(2)}, u32[]{:S(2)}) %collective-permute-start.20) | collective-permute-done | bytes 1179680 | tf_op jit(solution)/shard_map/ppermute | solution.py:494
  223.1 14.5 %shard_map.274 = (bf16[1,512,576]{2,1,0:T(8,128)(2,1)S(1)}, f32[8,1,512]{2,1,0:T(1,128)S(1)}) custom-call(s32[3]{0:T(128)S(1)} %add_add_fusion.2.info, bf16[1,512,576]{2,1,0:T(8,128)(2,1)S(1)} %get-tuple-element.178.refs_0_, bf16[1,512,576]{2,1,0:T(8,128)(2,1)S(1)} %get-tuple-element.192.refs_1_.refs_3_, ...), custom_call_target="tpu_custom_call" | custom-call | flops 4294967296 | bytes 3538944 | tf_op jit(solution)/shard_map/pallas_call | solution.py:174
  238.3 14.8 %shard_map.273 = (bf16[1,512,576]{2,1,0:T(8,128)(2,1)S(1)}, f32[8,1,512]{2,1,0:T(1,128)S(1)}) custom-call(s32[3]{0:T(128)S(1)} %add_add_fusion.1.info, bf16[1,512,576]{2,1,0:T(8,128)(2,1)S(1)} %get-tuple-element.177.refs_0_, bf16[1,512,576]{2,1,0:T(8,128)(2,1)S(1)} %get-tuple-element.188.refs_1_.refs_3_, ...), custom_call_target="tpu_custom_call" | custom-call | flops 4294967296 | bytes 3538944 | tf_op jit(solution)/shard_map/pallas_call | solution.py:174
  253.1 4.3 fusion.70
  259.9 4.2 collective-permute-done.22
  264.1 4.6 fusion.59
  271.0 3.8 add_convert_fusion.2
  274.8 41.5 %collective-permute-done.23.refs_1_ = bf16[8,1,72,2152]{3,2,1,0:T(8,128)(2,1)S(1)} collective-permute-done((bf16[8,1,72,2152]{3,2,1,0:T(8,128)(2,1)}, bf16[8,1,72,2152]{3,2,1,0:T(8,128)(2,1)S(1)}, u32[]{:S(2)}, u32[]{:S(2)}) %collective-permute-start.23) | collective-permute-done | bytes 2479136 | tf_op jit(solution)/shard_map/ppermute | solution.py:494
  316.3 13.3 %add_convert_fusion = (bf16[1024,2152]{1,0:T(8,128)(2,1)}, bf16[1024,2152]{1,0:T(8,128)(2,1)S(1)}) fusion(f32[2152]{0:T(1024)S(1)} %slice_select_fusion.4, bf16[1024,1152]{1,0:T(8,128)(2,1)} %get-tuple-element.84.left, bf16[1152,2152]{1,0:T(8,128)(2,1)} %bitcast.199), kind=kOutput, calls=%fused_computation.2 | convolution fusion | flops 5121277952 | bytes 16140704 | tf_op jit(solution)/shard_map/dot_general | solution.py:704
  329.6 5.1 shard_map.277.refs_3_
  334.8 5.1 shard_map.276.refs_2_
  344.4 6.9 %multiply_convert_fusion.right = bf16[1024,2152]{1,0:T(8,128)(2,1)S(1)} fusion(bf16[1024,2152]{1,0:T(8,128)(2,1)S(1)} %bitcast.202, bf16[1152,2152]{1,0:T(8,128)(2,1)S(1)} %bitcast.154, bf16[512,1152]{1,0:T(8,128)(2,1)} %collective-permute-done.19, bf16[512,1152]{1,0:T(8,128)(2,1)S(1)} %bitcast.190), kind=kOutput, calls=%fused_computation.1 | convolution fusion | flops 5088534528 | bytes 16132096 | tf_op jit(solution)/shard_map/dot_general | solution.py:715
  351.3 8.7 %shard_map.279 = bf16[1152,2152]{1,0:T(8,128)(2,1)S(1)} custom-call(bf16[1024,1152]{1,0:T(8,128)(2,1)S(1)} %copy-done.15, bf16[1024,2152]{1,0:T(8,128)(2,1)S(1)} %multiply_convert_fusion.right), custom_call_target="tpu_custom_call" | custom-call | flops 5077204992 | bytes 11724800 | tf_op jit(solution)/shard_map/pallas_call | solution.py:244
  364.4 11.1 %fusion.71 = (bf16[1024,1152]{1,0:T(8,128)(2,1)S(1)}, f32[1024,1152]{1,0:T(8,128)}) fusion(bf16[1024,2152]{1,0:T(8,128)(2,1)} %copy-done.10, bf16[1152,2152]{1,0:T(8,128)(2,1)} %bitcast.200), kind=kOutput, calls=%fused_computation.225 | convolution fusion | flops 5078384640 | bytes 16443392 | tf_op jit(solution)/shard_map/dot_general | solution.py:720
  386.1 5.8 multiply_reduce_fusion.2
  392.3 4.7 fusion.58
  405.2 24.5 %shard_map.282 = (bf16[1,512,576]{2,1,0:T(8,128)(2,1)}, bf16[1,512,576]{2,1,0:T(8,128)(2,1)}, bf16[1,512,576]{2,1,0:T(8,128)(2,1)}, bf16[1,512,576]{2,1,0:T(8,128)(2,1)}, bf16[1,512,576]{2,1,0:T(8,128)(2,1)}) custom-call(s32[3]{0:T(128)} %copy-done.40, bf16[1,512,576]{2,1,0:T(8,128)(2,1)} %copy-done.34, bf16[1,512,576]{2,1,0:T(8,128)(2,1)} %get-tuple-element.176.refs_1_, ...), custom_call_target="tpu_custom_call" | custom-call | flops 10737418240 | bytes 7077888 | tf_op jit(solution)/shard_map/pallas_call | solution.py:203
  435.1 3.4 slice_reduce_fusion
  439.9 3.9 add_convert_fusion.1.refs_7_
  443.8 24.9 %shard_map.283 = (bf16[1,512,576]{2,1,0:T(8,128)(2,1)}, bf16[1,512,576]{2,1,0:T(8,128)(2,1)}, bf16[1,512,576]{2,1,0:T(8,128)(2,1)}, bf16[1,512,576]{2,1,0:T(8,128)(2,1)}, bf16[1,512,576]{2,1,0:T(8,128)(2,1)}) custom-call(s32[3]{0:T(128)} %copy-done.39, bf16[1,512,576]{2,1,0:T(8,128)(2,1)} %copy-done.29, bf16[1,512,576]{2,1,0:T(8,128)(2,1)} %get-tuple-element.175.refs_1_, ...), custom_call_target="tpu_custom_call" | custom-call | flops 10737418240 | bytes 7077888 | tf_op jit(solution)/shard_map/pallas_call | solution.py:203
  477.2 11.5 %collective-permute-start.53 = (bf16[72,1152]{1,0:T(8,128)(2,1)S(1)}, bf16[72,1152]{1,0:T(8,128)(2,1)S(1)}, u32[]{:S(2)}, u32[]{:S(2)}) collective-permute-start(bf16[72,1152]{1,0:T(8,128)(2,1)S(1)} %get-tuple-element.172), channel_id=1, source_target_pairs={{0,8},{2,10},{4,12},{6,14},{8,16},{10,18},{12,20},{14,22},{16,24},... | collective-permute-start | bytes 497672 | tf_op jit(solution)/shard_map/ppermute | solution.py:362
  490.2 9.8 %fusion.72 = f32[1024,1152]{1,0:T(8,128)S(1)} fusion(bf16[1024,2152]{1,0:T(8,128)(2,1)} %copy-done.43, bf16[1152,2152]{1,0:T(8,128)(2,1)} %bitcast.155), kind=kOutput, calls=%fused_computation.226 | convolution fusion | flops 5077204992 | bytes 14084096 | tf_op jit(solution)/shard_map/dot_general | solution.py:774
  503.3 7.9 %collective-permute-done.54 = bf16[72,1152]{1,0:T(8,128)(2,1)S(1)} collective-permute-done((bf16[72,1152]{1,0:T(8,128)(2,1)S(1)}, bf16[72,1152]{1,0:T(8,128)(2,1)S(1)}, u32[]{:S(2)}, u32[]{:S(2)}) %collective-permute-start.54) | collective-permute-done | bytes 165920 | tf_op jit(solution)/shard_map/ppermute | solution.py:362
  514.9 17.2 %collective-permute-done.56 = bf16[72,1152]{1,0:T(8,128)(2,1)S(1)} collective-permute-done((bf16[72,1152]{1,0:T(8,128)(2,1)S(1)}, bf16[72,1152]{1,0:T(8,128)(2,1)S(1)}, u32[]{:S(2)}, u32[]{:S(2)}) %collective-permute-start.56) | collective-permute-done | bytes 165920 | tf_op jit(solution)/shard_map/ppermute | solution.py:545
  549.3 3.5 collective-permute-start.38
  562.1 4.6 add_add_fusion
  577.9 11.3 %collective-permute-done.41 = bf16[144,576]{1,0:T(8,128)(2,1)S(1)} collective-permute-done((bf16[144,576]{1,0:T(8,128)(2,1)S(1)}, bf16[144,576]{1,0:T(8,128)(2,1)S(1)}, u32[]{:S(2)}, u32[]{:S(2)}) %collective-permute-start.41) | collective-permute-done | bytes 165920 | tf_op jit(solution)/shard_map/ppermute | solution.py:545
  597.3 3.3 collective-permute-done.42
  628.4 7.1 %collective-permute-done.35 = f32[13520]{0:T(1024)S(1)} collective-permute-done((f32[13520]{0:T(1024)S(1)}, f32[13520]{0:T(1024)S(1)}, u32[]{:S(2)}, u32[]{:S(2)}) %collective-permute-start.35) | collective-permute-done | bytes 54112 | tf_op jit(solution)/shard_map/ppermute | solution.py:560
  653.2 3.7 reshape.797
  (492 shorter events, 218.3 us)
Async XLA Ops:
  7.2 252.1 %all-gather.5.cloned.1.call-start = ((), (), s32[]{:S(2)}) async-start(), calls=%async_computation.3 | async-start | bytes 2820096 | tf_op jit(solution)/shard_map/all_gather | solution.py:644
  7.2 15.3 %collective-permute-start.7 = (s32[1]{0:T(128)}, s32[1]{0:T(128)}, u32[]{:S(2)}, u32[]{:S(2)}) collective-permute-start(s32[1]{0:T(128)} %param.17), channel_id=1, source_target_pairs={{0,2},{2,0},{4,6},{6,4},{8,10},{10,8},{12,14},{14,12},{16,18},{18,... | collective-permute-start | bytes 20 | tf_op jit(solution)/shard_map/ppermute | solution.py:362
  9.7 17.9 %collective-permute-start.6 = (bf16[72,2152]{1,0:T(8,128)(2,1)}, bf16[72,2152]{1,0:T(8,128)(2,1)}, u32[]{:S(2)}, u32[]{:S(2)}) collective-permute-start(bf16[72,2152]{1,0:T(8,128)(2,1)} %broadcast_select_fusion.2), channel_id=1, source_target_pairs={{0,2},{2,0},{4,6},{6,4},{8,10},{10,8},{12,14},{14,12},{16,18},{18,... | collective-permute-start | bytes 929672 | tf_op jit(solution)/shard_map/ppermute | solution.py:362
  11.7 20.5 %collective-permute-start.5 = (bf16[72,2152]{1,0:T(8,128)(2,1)}, bf16[72,2152]{1,0:T(8,128)(2,1)}, u32[]{:S(2)}, u32[]{:S(2)}) collective-permute-start(bf16[72,2152]{1,0:T(8,128)(2,1)} %broadcast_select_fusion.4), channel_id=1, source_target_pairs={{0,2},{2,0},{4,6},{6,4},{8,10},{10,8},{12,14},{14,12},{16,18},{18,... | collective-permute-start | bytes 929672 | tf_op jit(solution)/shard_map/ppermute | solution.py:362
  19.9 23.5 %collective-permute-start = (bf16[512,1152]{1,0:T(8,128)(2,1)S(1)}, bf16[512,1152]{1,0:T(8,128)(2,1)S(1)}, u32[]{:S(2)}, u32[]{:S(2)}) collective-permute-start(bf16[512,1152]{1,0:T(8,128)(2,1)S(1)} %bitcast.179), channel_id=1, source_target_pairs={{0,2},{2,0},{4,6},{6,4},{8,10},{10,8},{12,14},{14,12},{16,18},{18,... | collective-permute-start | bytes 3538952 | tf_op jit(solution)/shard_map/ppermute | solution.py:362
  22.5 119.5 %collective-permute-start.19 = (bf16[512,1152]{1,0:T(8,128)(2,1)}, bf16[512,1152]{1,0:T(8,128)(2,1)}, u32[]{:S(2)}, u32[]{:S(2)}) collective-permute-start(bf16[512,1152]{1,0:T(8,128)(2,1)} %bitcast.187), channel_id=1, source_target_pairs={{0,2},{2,0},{4,6},{6,4},{8,10},{10,8},{12,14},{14,12},{16,18},{18,... | collective-permute-start | bytes 3538952 | tf_op jit(solution)/shard_map/ppermute | solution.py:362
  24.6 11.1 %collective-permute-start.4 = (bf16[1,72,1152]{2,1,0:T(8,128)(2,1)S(1)}, bf16[1,72,1152]{2,1,0:T(8,128)(2,1)}, u32[]{:S(2)}, u32[]{:S(2)}) collective-permute-start(bf16[1,72,1152]{2,1,0:T(8,128)(2,1)S(1)} %slice_select_fusion.3), channel_id=1, source_target_pairs={{0,8},{2,10},{4,12},{6,14},{8,16},{10,18},{12,20},{14,22},{16,24},... | collective-permute-start | bytes 497672 | tf_op jit(solution)/shard_map/ppermute | solution.py:362
  27.6 13.9 %collective-permute-start.3 = (bf16[1,72,1152]{2,1,0:T(8,128)(2,1)S(1)}, bf16[1,72,1152]{2,1,0:T(8,128)(2,1)}, u32[]{:S(2)}, u32[]{:S(2)}) collective-permute-start(bf16[1,72,1152]{2,1,0:T(8,128)(2,1)S(1)} %slice_select_fusion.3), channel_id=1, source_target_pairs={{0,16},{2,18},{4,20},{6,22},{8,24},{10,26},{12,28},{14,30},{16,0},... | collective-permute-start | bytes 497672 | tf_op jit(solution)/shard_map/ppermute | solution.py:362
  48.6 16.7 %collective-permute-start.15 = (bf16[4,1,72,1152]{3,2,1,0:T(8,128)(2,1)S(1)}, bf16[4,1,72,1152]{3,2,1,0:T(8,128)(2,1)S(1)}, u32[]{:S(2)}, u32[]{:S(2)}) collective-permute-start(bf16[4,1,72,1152]{3,2,1,0:T(8,128)(2,1)S(1)} %pad_maximum_fusion.12.refs_0_), channel_id=1, source_target_pairs={{0,4},{2,6},{4,0},{6,2},{8,12},{10,14},{12,8},{14,10},{16,20},{18,... | collective-permute-start | bytes 1990664 | tf_op jit(solution)/shard_map/ppermute | solution.py:362
  67.3 248.9 %all-gather.7.cloned.1.call-start = ((), (), s32[]{:S(2)}) async-start(), calls=%async_computation.4 | async-start | bytes 5640192 | tf_op jit(solution)/shard_map/all_gather | solution.py:405
  72.7 12.8 %collective-permute-start.10 = (bf16[2,72,576]{2,1,0:T(8,128)(2,1)S(1)}, bf16[2,72,576]{2,1,0:T(8,128)(2,1)S(1)}, u32[]{:S(2)}, u32[]{:S(2)}) collective-permute-start(bf16[2,72,576]{2,1,0:T(8,128)(2,1)S(1)} %fusion.52), channel_id=1, source_target_pairs={{0,8},{2,10},{4,12},{6,14},{8,16},{10,18},{12,20},{14,22},{16,24},... | collective-permute-start | bytes 497672 | tf_op jit(solution)/shard_map/ppermute | solution.py:362
  76.8 20.0 %collective-permute-start.9 = (bf16[2,72,576]{2,1,0:T(8,128)(2,1)S(1)}, bf16[2,72,576]{2,1,0:T(8,128)(2,1)S(1)}, u32[]{:S(2)}, u32[]{:S(2)}) collective-permute-start(bf16[2,72,576]{2,1,0:T(8,128)(2,1)S(1)} %fusion.52), channel_id=1, source_target_pairs={{0,16},{2,18},{4,20},{6,22},{8,24},{10,26},{12,28},{14,30},{16,0},... | collective-permute-start | bytes 497672 | tf_op jit(solution)/shard_map/ppermute | solution.py:362
  77.7 20.3 %collective-permute-start.8 = (bf16[2,72,576]{2,1,0:T(8,128)(2,1)S(1)}, bf16[2,72,576]{2,1,0:T(8,128)(2,1)S(1)}, u32[]{:S(2)}, u32[]{:S(2)}) collective-permute-start(bf16[2,72,576]{2,1,0:T(8,128)(2,1)S(1)} %fusion.52), channel_id=1, source_target_pairs={{0,24},{2,26},{4,28},{6,30},{8,0},{10,2},{12,4},{14,6},{16,8},{18,... | collective-permute-start | bytes 497672 | tf_op jit(solution)/shard_map/ppermute | solution.py:362
  98.0 13.6 %collective-permute-start.14 = (bf16[1,72,1152]{2,1,0:T(8,128)(2,1)}, bf16[1,72,1152]{2,1,0:T(8,128)(2,1)S(1)}, u32[]{:S(2)}, u32[]{:S(2)}) collective-permute-start(bf16[1,72,1152]{2,1,0:T(8,128)(2,1)} %bitcast.33), channel_id=1, source_target_pairs={{0,8},{2,10},{4,12},{6,14},{8,16},{10,18},{12,20},{14,22},{16,24},... | collective-permute-start | bytes 497672 | tf_op jit(solution)/shard_map/ppermute | solution.py:362
  104.9 18.7 %collective-permute-start.13 = (bf16[1,72,1152]{2,1,0:T(8,128)(2,1)}, bf16[1,72,1152]{2,1,0:T(8,128)(2,1)S(1)}, u32[]{:S(2)}, u32[]{:S(2)}) collective-permute-start(bf16[1,72,1152]{2,1,0:T(8,128)(2,1)} %bitcast.33), channel_id=1, source_target_pairs={{0,16},{2,18},{4,20},{6,22},{8,24},{10,26},{12,28},{14,30},{16,0},... | collective-permute-start | bytes 497672 | tf_op jit(solution)/shard_map/ppermute | solution.py:362
  105.6 19.3 %collective-permute-start.12 = (bf16[1,72,1152]{2,1,0:T(8,128)(2,1)}, bf16[1,72,1152]{2,1,0:T(8,128)(2,1)S(1)}, u32[]{:S(2)}, u32[]{:S(2)}) collective-permute-start(bf16[1,72,1152]{2,1,0:T(8,128)(2,1)} %bitcast.33), channel_id=1, source_target_pairs={{0,24},{2,26},{4,28},{6,30},{8,0},{10,2},{12,4},{14,6},{16,8},{18,... | collective-permute-start | bytes 497672 | tf_op jit(solution)/shard_map/ppermute | solution.py:362
  108.4 48.4 %collective-permute-start.11 = (bf16[4,2,72,576]{3,2,1,0:T(8,128)(2,1)S(1)}, bf16[4,2,72,576]{3,2,1,0:T(8,128)(2,1)S(1)}, u32[]{:S(2)}, u32[]{:S(2)}) collective-permute-start(bf16[4,2,72,576]{3,2,1,0:T(8,128)(2,1)S(1)} %pad_maximum_fusion.11.refs_0_), channel_id=1, source_target_pairs={{0,4},{2,6},{4,0},{6,2},{8,12},{10,14},{12,8},{14,10},{16,20},{18,... | collective-permute-start | bytes 1990664 | tf_op jit(solution)/shard_map/ppermute | solution.py:362
  126.7 50.6 %collective-permute-start.21 = (bf16[4,1,72,1152]{3,2,1,0:T(8,128)(2,1)S(1)}, bf16[4,1,72,1152]{3,2,1,0:T(8,128)(2,1)}, u32[]{:S(2)}, u32[]{:S(2)}) collective-permute-start(bf16[4,1,72,1152]{3,2,1,0:T(8,128)(2,1)S(1)} %pad_maximum_fusion.13.refs_0_), channel_id=1, source_target_pairs={{0,4},{2,6},{4,0},{6,2},{8,12},{10,14},{12,8},{14,10},{16,20},{18,... | collective-permute-start | bytes 1990664 | tf_op jit(solution)/shard_map/ppermute | solution.py:362
  128.1 31.4 %collective-permute-start.16 = (bf16[4,1,72,1152]{3,2,1,0:T(8,128)(2,1)S(1)}, bf16[4,1,72,1152]{3,2,1,0:T(8,128)(2,1)}, u32[]{:S(2)}, u32[]{:S(2)}) collective-permute-start(bf16[4,1,72,1152]{3,2,1,0:T(8,128)(2,1)S(1)} %pad_maximum_fusion.12.refs_0_), channel_id=1, source_target_pairs={{0,1},{1,0},{2,3},{3,2},{4,5},{5,4},{6,7},{7,6},{8,9},{9,8},{10,11... | collective-permute-start | bytes 1990664 | tf_op jit(solution)/shard_map/ppermute | solution.py:494
  129.6 407.4 %reduce-scatter.5.cloned.1.call-start = ((), (), s32[]{:S(2)}) async-start(), calls=%async_computation.2 | async-start | bytes 5640192 | tf_op jit(solution)/shard_map/reduce_scatter | solution.py:414
  151.3 14.1 %collective-permute-start.17 = (bf16[4,1,72,1152]{3,2,1,0:T(8,128)(2,1)S(1)}, bf16[4,1,72,1152]{3,2,1,0:T(8,128)(2,1)S(1)}, u32[]{:S(2)}, u32[]{:S(2)}) collective-permute-start(bf16[4,1,72,1152]{3,2,1,0:T(8,128)(2,1)S(1)} %copy-done.27), channel_id=1, source_target_pairs={{0,1},{1,0},{2,3},{3,2},{4,5},{5,4},{6,7},{7,6},{8,9},{9,8},{10,11... | collective-permute-start | bytes 1990664 | tf_op jit(solution)/shard_map/ppermute | solution.py:494
  172.9 29.0 %collective-permute-start.18 = (bf16[1,512,1152]{2,1,0:T(8,128)(2,1)S(1)}, bf16[1,512,1152]{2,1,0:T(8,128)(2,1)S(1)}, u32[]{:S(2)}, u32[]{:S(2)}) collective-permute-start(bf16[1,512,1152]{2,1,0:T(8,128)(2,1)S(1)} %get-tuple-element.154), channel_id=1, source_target_pairs={{0,1},{1,0},{2,3},{3,2},{4,5},{5,4},{6,7},{7,6},{8,9},{9,8},{10,11... | collective-permute-start | bytes 3538952 | tf_op jit(solution)/shard_map/ppermute | solution.py:494
  173.5 49.1 %collective-permute-start.20 = (bf16[1,512,1152]{2,1,0:T(8,128)(2,1)S(1)}, bf16[1,512,1152]{2,1,0:T(8,128)(2,1)S(1)}, u32[]{:S(2)}, u32[]{:S(2)}) collective-permute-start(bf16[1,512,1152]{2,1,0:T(8,128)(2,1)S(1)} %get-tuple-element.155), channel_id=1, source_target_pairs={{0,1},{1,0},{2,3},{3,2},{4,5},{5,4},{6,7},{7,6},{8,9},{9,8},{10,11... | collective-permute-start | bytes 3538952 | tf_op jit(solution)/shard_map/ppermute | solution.py:494
  259.2 57.0 %collective-permute-start.23 = (bf16[8,1,72,2152]{3,2,1,0:T(8,128)(2,1)}, bf16[8,1,72,2152]{3,2,1,0:T(8,128)(2,1)S(1)}, u32[]{:S(2)}, u32[]{:S(2)}) collective-permute-start(bf16[8,1,72,2152]{3,2,1,0:T(8,128)(2,1)} %bitcast.156), channel_id=1, source_target_pairs={{0,1},{1,0},{2,3},{3,2},{4,5},{5,4},{6,7},{7,6},{8,9},{9,8},{10,11... | collective-permute-start | bytes 7437320 | tf_op jit(solution)/shard_map/ppermute | solution.py:494
  364.4 236.4 %reduce-scatter.7.cloned.1.call-start = ((), (), s32[]{:S(2)}) async-start(), calls=%async_computation.5 | async-start | bytes 2820096
  382.4 57.6 %collective-permute-start.25 = (bf16[576,2152]{1,0:T(8,128)(2,1)}, bf16[576,2152]{1,0:T(8,128)(2,1)}, u32[]{:S(2)}, u32[]{:S(2)}) collective-permute-start(bf16[576,2152]{1,0:T(8,128)(2,1)} %copy-done.14), channel_id=1, source_target_pairs={{0,1},{1,0},{2,3},{3,2},{4,5},{5,4},{6,7},{7,6},{8,9},{9,8},{10,11... | collective-permute-start | bytes 7437320 | tf_op jit(solution)/shard_map/ppermute | solution.py:494
  399.1 76.8 %collective-permute-start.52 = (bf16[288,1152]{1,0:T(8,128)(2,1)S(1)}, bf16[288,1152]{1,0:T(8,128)(2,1)}, u32[]{:S(2)}, u32[]{:S(2)}) collective-permute-start(bf16[288,1152]{1,0:T(8,128)(2,1)S(1)} %shard_map.281.refs_8_), channel_id=1, source_target_pairs={{0,4},{2,6},{4,0},{6,2},{8,12},{10,14},{12,8},{14,10},{16,20},{18,... | collective-permute-start | bytes 1990664 | tf_op jit(solution)/shard_map/ppermute | solution.py:362
  432.5 100.4 %collective-permute-start.27 = (bf16[1,512,1152]{2,1,0:T(8,128)(2,1)}, bf16[1,512,1152]{2,1,0:T(8,128)(2,1)}, u32[]{:S(2)}, u32[]{:S(2)}) collective-permute-start(bf16[1,512,1152]{2,1,0:T(8,128)(2,1)} %pad_maximum_fusion.9), channel_id=1, source_target_pairs={{0,1},{1,0},{2,3},{3,2},{4,5},{5,4},{6,7},{7,6},{8,9},{9,8},{10,11... | collective-permute-start | bytes 3538952 | tf_op jit(solution)/shard_map/ppermute | solution.py:494
  473.0 40.9 %collective-permute-start.29 = (bf16[576,576]{1,0:T(8,128)(2,1)S(1)}, bf16[576,576]{1,0:T(8,128)(2,1)S(1)}, u32[]{:S(2)}, u32[]{:S(2)}) collective-permute-start(bf16[576,576]{1,0:T(8,128)(2,1)S(1)} %shard_map.285), channel_id=1, source_target_pairs={{0,4},{2,6},{4,0},{6,2},{8,12},{10,14},{12,8},{14,10},{16,20},{18,... | collective-permute-start | bytes 1990664 | tf_op jit(solution)/shard_map/ppermute | solution.py:362
  477.2 23.0 %collective-permute-start.53 = (bf16[72,1152]{1,0:T(8,128)(2,1)S(1)}, bf16[72,1152]{1,0:T(8,128)(2,1)S(1)}, u32[]{:S(2)}, u32[]{:S(2)}) collective-permute-start(bf16[72,1152]{1,0:T(8,128)(2,1)S(1)} %get-tuple-element.172), channel_id=1, source_target_pairs={{0,8},{2,10},{4,12},{6,14},{8,16},{10,18},{12,20},{14,22},{16,24},... | collective-permute-start | bytes 497672 | tf_op jit(solution)/shard_map/ppermute | solution.py:362
  488.6 12.9 %collective-permute-start.55 = (bf16[72,1152]{1,0:T(8,128)(2,1)S(1)}, bf16[72,1152]{1,0:T(8,128)(2,1)S(1)}, u32[]{:S(2)}, u32[]{:S(2)}) collective-permute-start(bf16[72,1152]{1,0:T(8,128)(2,1)S(1)} %get-tuple-element.173), channel_id=1, source_target_pairs={{0,24},{2,26},{4,28},{6,30},{8,0},{10,2},{12,4},{14,6},{16,8},{18,... | collective-permute-start | bytes 497672 | tf_op jit(solution)/shard_map/ppermute | solution.py:362
  488.6 22.5 %collective-permute-start.54 = (bf16[72,1152]{1,0:T(8,128)(2,1)S(1)}, bf16[72,1152]{1,0:T(8,128)(2,1)S(1)}, u32[]{:S(2)}, u32[]{:S(2)}) collective-permute-start(bf16[72,1152]{1,0:T(8,128)(2,1)S(1)} %get-tuple-element.174), channel_id=1, source_target_pairs={{0,16},{2,18},{4,20},{6,22},{8,24},{10,26},{12,28},{14,30},{16,0},... | collective-permute-start | bytes 497672 | tf_op jit(solution)/shard_map/ppermute | solution.py:362
  500.2 35.5 %collective-permute-start.26 = (bf16[512,1152]{1,0:T(8,128)(2,1)S(1)}, bf16[512,1152]{1,0:T(8,128)(2,1)S(1)}, u32[]{:S(2)}, u32[]{:S(2)}) collective-permute-start(bf16[512,1152]{1,0:T(8,128)(2,1)S(1)} %slice.731), channel_id=1, source_target_pairs={{0,2},{2,0},{4,6},{6,4},{8,10},{10,8},{12,14},{14,12},{16,18},{18,... | collective-permute-start | bytes 3538952 | tf_op jit(solution)/shard_map/ppermute | solution.py:362
  501.6 35.5 %collective-permute-start.28 = (bf16[1,512,1152]{2,1,0:T(8,128)(2,1)S(1)}, bf16[1,512,1152]{2,1,0:T(8,128)(2,1)}, u32[]{:S(2)}, u32[]{:S(2)}) collective-permute-start(bf16[1,512,1152]{2,1,0:T(8,128)(2,1)S(1)} %pad_maximum_fusion.10), channel_id=1, source_target_pairs={{0,1},{1,0},{2,3},{3,2},{4,5},{5,4},{6,7},{7,6},{8,9},{9,8},{10,11... | collective-permute-start | bytes 3538952 | tf_op jit(solution)/shard_map/ppermute | solution.py:494
  512.2 20.0 %collective-permute-start.56 = (bf16[72,1152]{1,0:T(8,128)(2,1)S(1)}, bf16[72,1152]{1,0:T(8,128)(2,1)S(1)}, u32[]{:S(2)}, u32[]{:S(2)}) collective-permute-start(bf16[72,1152]{1,0:T(8,128)(2,1)S(1)} %add_convert_fusion.22), channel_id=1, source_target_pairs={{0,1},{1,0},{2,3},{3,2},{4,5},{5,4},{6,7},{7,6},{8,9},{9,8},{10,11... | collective-permute-start | bytes 497672 | tf_op jit(solution)/shard_map/ppermute | solution.py:545
  549.3 17.6 %collective-permute-start.38 = (bf16[144,576]{1,0:T(8,128)(2,1)}, bf16[144,576]{1,0:T(8,128)(2,1)}, u32[]{:S(2)}, u32[]{:S(2)}) collective-permute-start(bf16[144,576]{1,0:T(8,128)(2,1)} %get-tuple-element.118), channel_id=1, source_target_pairs={{0,8},{2,10},{4,12},{6,14},{8,16},{10,18},{12,20},{14,22},{16,24},... | collective-permute-start | bytes 497672 | tf_op jit(solution)/shard_map/ppermute | solution.py:362
  552.8 18.3 %collective-permute-start.39 = (bf16[144,576]{1,0:T(8,128)(2,1)}, bf16[144,576]{1,0:T(8,128)(2,1)}, u32[]{:S(2)}, u32[]{:S(2)}) collective-permute-start(bf16[144,576]{1,0:T(8,128)(2,1)} %get-tuple-element.119), channel_id=1, source_target_pairs={{0,16},{2,18},{4,20},{6,22},{8,24},{10,26},{12,28},{14,30},{16,0},... | collective-permute-start | bytes 497672 | tf_op jit(solution)/shard_map/ppermute | solution.py:362
  553.6 17.5 %collective-permute-start.40 = (bf16[144,576]{1,0:T(8,128)(2,1)}, bf16[144,576]{1,0:T(8,128)(2,1)}, u32[]{:S(2)}, u32[]{:S(2)}) collective-permute-start(bf16[144,576]{1,0:T(8,128)(2,1)} %get-tuple-element.120), channel_id=1, source_target_pairs={{0,24},{2,26},{4,28},{6,30},{8,0},{10,2},{12,4},{14,6},{16,8},{18,... | collective-permute-start | bytes 497672 | tf_op jit(solution)/shard_map/ppermute | solution.py:362
  555.4 35.9 %collective-permute-start.31 = (bf16[576,576]{1,0:T(8,128)(2,1)}, bf16[576,576]{1,0:T(8,128)(2,1)}, u32[]{:S(2)}, u32[]{:S(2)}) collective-permute-start(bf16[576,576]{1,0:T(8,128)(2,1)} %shard_map.287), channel_id=1, source_target_pairs={{0,1},{1,0},{2,3},{3,2},{4,5},{5,4},{6,7},{7,6},{8,9},{9,8},{10,11... | collective-permute-start | bytes 1990664 | tf_op jit(solution)/shard_map/ppermute | solution.py:494
  557.1 38.1 %collective-permute-start.32 = (bf16[576,576]{1,0:T(8,128)(2,1)S(1)}, bf16[576,576]{1,0:T(8,128)(2,1)}, u32[]{:S(2)}, u32[]{:S(2)}) collective-permute-start(bf16[576,576]{1,0:T(8,128)(2,1)S(1)} %shard_map.289), channel_id=1, source_target_pairs={{0,4},{2,6},{4,0},{6,2},{8,12},{10,14},{12,8},{14,10},{16,20},{18,... | collective-permute-start | bytes 1990664 | tf_op jit(solution)/shard_map/ppermute | solution.py:362
  566.9 23.1 %collective-permute-start.57 = (bf16[144,2152]{1,0:T(8,128)(2,1)S(1)}, bf16[144,2152]{1,0:T(8,128)(2,1)}, u32[]{:S(2)}, u32[]{:S(2)}) collective-permute-start(bf16[144,2152]{1,0:T(8,128)(2,1)S(1)} %copy-done.69), channel_id=1, source_target_pairs={{0,1},{1,0},{2,3},{3,2},{4,5},{5,4},{6,7},{7,6},{8,9},{9,8},{10,11... | collective-permute-start | bytes 1859336 | tf_op jit(solution)/shard_map/ppermute | solution.py:545
  572.3 16.9 %collective-permute-start.41 = (bf16[144,576]{1,0:T(8,128)(2,1)S(1)}, bf16[144,576]{1,0:T(8,128)(2,1)S(1)}, u32[]{:S(2)}, u32[]{:S(2)}) collective-permute-start(bf16[144,576]{1,0:T(8,128)(2,1)S(1)} %add_convert_fusion.13), channel_id=1, source_target_pairs={{0,1},{1,0},{2,3},{3,2},{4,5},{5,4},{6,7},{7,6},{8,9},{9,8},{10,11... | collective-permute-start | bytes 497672 | tf_op jit(solution)/shard_map/ppermute | solution.py:545
  577.9 35.7 %collective-permute-start.30 = (bf16[512,1152]{1,0:T(8,128)(2,1)}, bf16[512,1152]{1,0:T(8,128)(2,1)}, u32[]{:S(2)}, u32[]{:S(2)}) collective-permute-start(bf16[512,1152]{1,0:T(8,128)(2,1)} %slice.730), channel_id=1, source_target_pairs={{0,2},{2,0},{4,6},{6,4},{8,10},{10,8},{12,14},{14,12},{16,18},{18,... | collective-permute-start | bytes 3538952 | tf_op jit(solution)/shard_map/ppermute | solution.py:362
  595.3 11.2 %collective-permute-start.58 = (bf16[72,2152]{1,0:T(8,128)(2,1)}, bf16[72,2152]{1,0:T(8,128)(2,1)}, u32[]{:S(2)}, u32[]{:S(2)}) collective-permute-start(bf16[72,2152]{1,0:T(8,128)(2,1)} %select_convert_fusion.1), channel_id=1, source_target_pairs={{0,2},{2,0},{4,6},{6,4},{8,10},{10,8},{12,14},{14,12},{16,18},{18,... | collective-permute-start | bytes 929672 | tf_op jit(solution)/shard_map/ppermute | solution.py:362
  611.3 17.0 %collective-permute-start.59 = (bf16[72,2152]{1,0:T(8,128)(2,1)S(1)}, bf16[72,2152]{1,0:T(8,128)(2,1)S(1)}, u32[]{:S(2)}, u32[]{:S(2)}) collective-permute-start(bf16[72,2152]{1,0:T(8,128)(2,1)S(1)} %copy-done.70), channel_id=1, source_target_pairs={{0,1},{1,0},{2,3},{3,2},{4,5},{5,4},{6,7},{7,6},{8,9},{9,8},{10,11... | collective-permute-start | bytes 929672 | tf_op jit(solution)/shard_map/ppermute | solution.py:494
  617.1 24.8 %collective-permute-start.47 = (bf16[144,576]{1,0:T(8,128)(2,1)S(1)}, bf16[144,576]{1,0:T(8,128)(2,1)S(1)}, u32[]{:S(2)}, u32[]{:S(2)}) collective-permute-start(bf16[144,576]{1,0:T(8,128)(2,1)S(1)} %copy-done.71), channel_id=1, source_target_pairs={{0,8},{2,10},{4,12},{6,14},{8,16},{10,18},{12,20},{14,22},{16,24},... | collective-permute-start | bytes 497672 | tf_op jit(solution)/shard_map/ppermute | solution.py:362
  618.8 23.1 %collective-permute-start.48 = (bf16[144,576]{1,0:T(8,128)(2,1)S(1)}, bf16[144,576]{1,0:T(8,128)(2,1)S(1)}, u32[]{:S(2)}, u32[]{:S(2)}) collective-permute-start(bf16[144,576]{1,0:T(8,128)(2,1)S(1)} %get-tuple-element.127), channel_id=1, source_target_pairs={{0,16},{2,18},{4,20},{6,22},{8,24},{10,26},{12,28},{14,30},{16,0},... | collective-permute-start | bytes 497672 | tf_op jit(solution)/shard_map/ppermute | solution.py:362
  621.7 20.2 %collective-permute-start.49 = (bf16[144,576]{1,0:T(8,128)(2,1)S(1)}, bf16[144,576]{1,0:T(8,128)(2,1)S(1)}, u32[]{:S(2)}, u32[]{:S(2)}) collective-permute-start(bf16[144,576]{1,0:T(8,128)(2,1)S(1)} %get-tuple-element.128), channel_id=1, source_target_pairs={{0,24},{2,26},{4,28},{6,30},{8,0},{10,2},{12,4},{14,6},{16,8},{18,... | collective-permute-start | bytes 497672 | tf_op jit(solution)/shard_map/ppermute | solution.py:362
  (119 other events, 1469.5 us)
Sparse Core Ops, SparseCore 0:
  67.5 79.9 all-gather.4
  150.2 82.2 all-gather.6
  364.5 111.3 reduce-scatter.4
  479.8 90.5 reduce-scatter.6

commit v3 on v2

--- a/solution.py
+++ b/solution.py
@@ -612,14 +612,14 @@
         return jnp.concatenate([flat, grid.send(flat, step_twin=1)], axis=0)
 
     qkv_block = pair_up(by_kind(qkv_weight))
-    pair_block = qkv_block[:, :, own_width:]
     all_kinds = jnp.stack(grid.shards())
     order = order_matrix(grid.shards(), shard_rows)
     own_order = order_matrix(grid.members(), shard_rows)
     inputs = both(tokens).astype(f32)
     normal_one, scale_one = norm_parts(inputs)
     normed_one = (normal_one * attn_gain + attn_shift).astype(bf16)
-    up_weight, down_turned = after((up_weight, down_weight.T), qkv_block)
+    qkv_block, up_weight, down_turned = together(qkv_block, up_weight, down_weight.T)
+    pair_block, query_block = qkv_block[:, :, own_width:], qkv_block[:, :, :own_width]
     up_block = jnp.stack(grid.in_order(*pair_up(two_halves(up_weight))))
     down_block = jnp.stack(grid.in_order(*pair_up(two_halves(down_turned))))
     sizes = jnp.concatenate([lengths, grid.send(lengths, step_twin=1)])
@@ -633,12 +633,11 @@
         scatter_seq, seq_order = ScatterX, order
         pair_lines, pair_pieces = gather_all(grid, pair_block)
         pair_slots = all_kinds
-    query_lines, query_pieces = gather_all(
-        grid, after(qkv_block[:, :, :own_width], *pair_lines[1:])
-    )
-    out_lines, out_pieces = gather_all(grid, after(out_weight[None], *query_lines[1:]))
-
-    down_block = after(down_block, pair_pieces[1])
+    pair_pieces[1], query_block, down_block = together(pair_pieces[1], query_block, down_block)
+    query_lines, query_pieces = gather_all(grid, query_block)
+    query_pieces[1], out_block, up_block = together(query_pieces[1], out_weight[None], up_block)
+    out_lines, out_pieces = gather_all(grid, out_block)
+
     if groups == 2:
         kinds_by_seq = jnp.stack(grid.kinds_by_seq())
         own_down = lax.all_gather(
@@ -649,26 +648,28 @@
         own_down = [own_down, swap_seq(own_down)]
     else:
         own_down = grid.gather(down_block)
-    up_block = after(up_block, *query_lines[1:])
     own_up = grid.gather(up_block)
 
     back_low = both(cotangent)
 
-    own_pair = place(pair_pieces, pair_slots, query_lines[1:]).reshape(width, 2 * own_width)
+    own_pair = place(pair_pieces, pair_slots).reshape(width, 2 * own_width)
     pair_bias = jnp.concatenate([jnp.zeros((own_width,), f32), vector_kind(value_bias)])
     pairs = (jnp.dot(normed_one, own_pair, preferred_element_type=f32) + pair_bias).astype(bf16)
-    own_query = place(query_pieces, all_kinds, out_lines[1:])
+    pairs, row_source, back_source = together(pairs, normed_one, back_low)
+    own_query = place(query_pieces, all_kinds)
     own_query = own_query.reshape(width, own_width)
     queries = (
         jnp.dot(normed_one, own_query, preferred_element_type=f32) + vector_kind(query_bias)
     ).astype(bf16)
 
-    one_rows = reorder(normed_one, order)
-    seq_rows = reorder(normed_one, seq_order) if groups == 2 else one_rows
+    one_rows = reorder(row_source, order)
+    seq_rows = reorder(row_source, seq_order) if groups == 2 else one_rows
     kind_rows = []
     if groups == 2:
-        kind_rows = reorder(back_low, order_matrix(grid.kinds_by_seq(), shard_rows))
-    made = [*one_rows, *seq_rows, *kind_rows]
+        kind_rows = reorder(back_source, order_matrix(grid.kinds_by_seq(), shard_rows))
+    made = [[*one_rows, *seq_rows, *kind_rows]] + [[]] * (2 * images - 1)
+    if groups == 2:
+        made[images] = [own_down[0]]
 
     place_seq = lax.axis_index("seq") * local_len
     attended_parts, saved = [], []
@@ -686,7 +687,7 @@
             value_parts = (lax.all_gather(value, "seq", axis=1, tiled=True),)
             info = jnp.stack([sizes[image], jnp.zeros_like(sizes[image])])
         attended_part, lse = attend(
-            info, query, key_parts, value_parts, made if image == 0 else ()
+            info, query, key_parts, value_parts, made[image]
         )
         attended_parts.append(attended_part[0])
         saved.append((info, query, key_parts, value_parts, lse))
@@ -699,11 +700,11 @@
     normal_two, scale_two = norm_parts(resid)
     normed_two = (normal_two * mlp_gain + mlp_shift).astype(bf16)
     own_up_bias = grid.own_half([up_bias[:hidden_half], up_bias[hidden_half:]])
-    if groups == 2:
-        normed_two, own_down[1] = together(normed_two, own_down[1])
     hidden = jnp.dot(normed_two, own_up, preferred_element_type=f32) + own_up_bias
     active, slope = gelu_and_slope(hidden)
-    active, slope = lax.optimization_barrier((active.astype(bf16), slope.astype(bf16)))
+    active, slope = together(active.astype(bf16), slope.astype(bf16))
+    if groups == 2:
+        active, own_down[1] = together(active, own_down[1])
     if groups == 2:
         down_kept, down_going = halves_of(kind_rows, active)
         down_came = swap_seq(down_going)
@@ -776,10 +777,9 @@
     )
     came = grid.send(partial[rows:].astype(bf16), step_twin=1).astype(f32)
     outputs = (resid[:rows] + partial[:rows] + came + down_bias).astype(bf16)
-    grad_out.add()
     grad_query.add()
     if groups == 2:
-        last_far, grad_up, *grad_query.sums = together(last_far, grad_up, *grad_query.sums)
+        last_far, *grad_query.sums = together(last_far, *grad_query.sums)
         d_key[-1] = (d_key[-1][0], last_far[:, :, :own_width])
         d_value[-1] = (d_value[-1][0], last_far[:, :, own_width:])
 
@@ -811,12 +811,14 @@
         )
     )
     d_one = partial[:rows] + grid.send(partial[rows:].astype(bf16), step_twin=1).astype(f32)
+    d_one, grad_value.came, grad_up = together(d_one, grad_value.came, grad_up)
     grad_value.add()
     if groups == 2:
         grad_key.cross()
-        d_one, grad_key.going, *grad_value.sums = together(
-            d_one, grad_key.going, *grad_value.sums
-        )
+    (grad_out.came, grad_out.kept, *grad_value.sums) = together(
+        grad_out.came, grad_out.kept, *grad_value.sums
+    )
+    grad_out.add()
     grad_tokens = d_resid[:rows] + norm_back(d_one, normal_one[:rows], scale_one[:rows], attn_gain)
     grad_key.add()
     grad_out = grad_out.finish()

time: 675 us -> 647 us (0.959)
  starting transfers between devices: 87.8 us -> 71.4 us
  local copies, waits for them, and re-layouts: 38 us -> 51.3 us
  other arithmetic: 101 us -> 90.6 us
  waiting for transfers between devices: 205 us -> 197 us
    ppermute x4, waiting for transfers between devices: 29.6 us -> 2.99 us  [sum_seq(): lax.ppermute(value, 'seq', [(0, 1), (1, 0)]).astype(f32)]
    ppermute x11, waiting for transfers between devices: 91.5 us -> 70.6 us  [swap_seq(): return lax.ppermute(value, 'seq', [(0, 1), (1, 0)])]
    ppermute x41, waiting for transfers between devices: 71.8 us -> 91.8 us  [send(): return lax.ppermute(value, 'fsdp', self.pairs(**steps))]
    ppermute x5, waiting for transfers between devices: 11.8 us -> 23.5 us  [sum_all(): lax.ppermute(vector, axis, [(member, member ^ step) for member in range(c...]
    ppermute x41, starting transfers between devices: 61.3 us -> 52.3 us  [send(): return lax.ppermute(value, 'fsdp', self.pairs(**steps))]
    all_gather x1, waiting for transfers between devices: 0.01 us -> 7.7 us  [gather(): whole = lax.all_gather(block, 'fsdp', axis_index_groups=self.groups())]
    unnamed x211 -> x187, local copies, waits for them, and re-layouts: 11 us -> 16.9 us
  transfers between devices with their start and end apart: 65 -> 65, of which waited for: 28 -> 25; matrix products, arithmetic and copies ran while one was open for 29% -> 32% of each run, Pallas kernels for 16% -> 19%
where the time goes in v3:
time: 647 us; the launch traced here: 639 us
  waiting for transfers between devices  197 us (30%)
  Pallas kernels  128 us (20%)
  other arithmetic  90.6 us (14%)
  matrix products  84.5 us (13%)
  starting transfers between devices  71.4 us (11%)
  local copies, waits for them, and re-layouts  51.3 us (8%)
  between operations  16.7 us (3%)
    ppermute x41, waiting for transfers between devices, send(): return lax.ppermute(value, 'fsdp', self.pairs(**steps))  91.8 us
    ppermute x11, waiting for transfers between devices, swap_seq(): return lax.ppermute(value, 'seq', [(0, 1), (1, 0)])  70.6 us
    ppermute x41, starting transfers between devices, send(): return lax.ppermute(value, 'fsdp', self.pairs(**steps))  52.3 us
    pallas_call x2, Pallas kernels, attend_back(): pl.pallas_call(functools.partial(attend_back_kernel, parts, heads, min(bl...  49.5 us
    pallas_call x11, Pallas kernels, contract_rows(): pl.pallas_call(contract_kernel, grid=(pl.cdiv(columns, block),), in_specs...  37.3 us
    pallas_call x2, Pallas kernels, attend(): pl.pallas_call(functools.partial(attend_kernel, parts, heads, min(block,...  29.3 us
    dot_general x8, matrix products, reorder(): jnp.dot(rows, part, preferred_element_type=f32).astype(bf16)  24.5 us
    ppermute x5, waiting for transfers between devices, sum_all(): lax.ppermute(vector, axis, [(member, member ^ step) for member in range(c...  23.5 us
  transfers between devices with their start and end apart: 65, of which 25 were waited for; matrix products, arithmetic and copies ran while one was open for 32% of the time, Pallas kernels for 19%

profile of v3, /device:TPU:0, one launch (start us, length us, event | category | flops | bytes accessed | tf_op | source)
XLA Modules:
  0.0 638.8 jit_solution(5095698610441566570)
XLA Ops:
  7.7 4.5 reshape.784
  28.4 3.7 collective-permute-start.3
  36.7 4.1 collective-permute-done.3
  41.3 4.0 collective-permute-done.4
  48.2 3.9 fusion
  61.0 8.9 %collective-permute-done.8.refs_1_ = bf16[4,1,72,1152]{3,2,1,0:T(8,128)(2,1)} collective-permute-done((bf16[4,1,72,1152]{3,2,1,0:T(8,128)(2,1)S(1)}, bf16[4,1,72,1152]{3,2,1,0:T(8,128)(2,1)}, u32[]{:S(2)}, u32[]{:S(2)}) %collective-permute-start.8) | collective-permute-done | bytes 663584 | tf_op jit(solution)/shard_map/ppermute | solution.py:362
  69.9 4.8 collective-permute-start.11
  81.4 6.4 collective-permute-done.10
  89.5 4.0 collective-permute-done.14.refs_3_
  93.5 3.5 shard_map.272
  97.1 4.2 add_convert_fusion.3
  103.4 3.6 fusion.25.refs_6_.left
  109.3 3.6 fusion.37.refs_10_.left
  116.4 3.6 fusion.31.refs_8_.left
  120.0 3.6 fusion.28.refs_7_.left
  127.1 5.8 collective-permute-start.20
  132.8 3.7 collective-permute-start.19
  141.1 4.2 collective-permute-done.19
  150.9 17.3 %collective-permute-done.21.refs_1_ = bf16[4,1,72,1152]{3,2,1,0:T(8,128)(2,1)S(1)} collective-permute-done((bf16[4,1,72,1152]{3,2,1,0:T(8,128)(2,1)S(1)}, bf16[4,1,72,1152]{3,2,1,0:T(8,128)(2,1)S(1)}, u32[]{:S(2)}, u32[]{:S(2)}) %collective-permute-start.21) | collective-permute-done | bytes 663584 | tf_op jit(solution)/shard_map/ppermute | solution.py:362
  174.3 14.6 %shard_map.273 = (bf16[1,512,576]{2,1,0:T(8,128)(2,1)S(1)}, f32[8,1,512]{2,1,0:T(1,128)S(1)}) custom-call(s32[3]{0:T(128)S(1)} %copy-done.27, bf16[1,512,576]{2,1,0:T(8,128)(2,1)S(1)} %get-tuple-element.195.refs_0_, bf16[1,512,576]{2,1,0:T(8,128)(2,1)S(1)} %get-tuple-element.206.refs_1_.refs_3_, bf16[1,512,576]{2,1,0:T(8,128)(2,1)S(1)} %get-tuple-element.204.refs_2_.refs_4_, ...), custom_call_target="tpu_custom_call" | custom-call | flops 4294967296 | bytes 3538944 | tf_op jit(solution)/shard_map/pallas_call | solution.py:174
  194.0 14.7 %shard_map.274 = (bf16[1,512,576]{2,1,0:T(8,128)(2,1)S(1)}, f32[8,1,512]{2,1,0:T(1,128)S(1)}) custom-call(s32[3]{0:T(128)S(1)} %add_add_fusion.2.info, bf16[1,512,576]{2,1,0:T(8,128)(2,1)S(1)} %copy-done.20, bf16[1,512,576]{2,1,0:T(8,128)(2,1)S(1)} %copy-done.17, bf16[1,512,576]{2,1,0:T(8,128)(2,1)S(1)} %copy-done.22, ...), custom_call_target="tpu_custom_call" | custom-call | flops 4294967296 | bytes 3538944 | tf_op jit(solution)/shard_map/pallas_call | solution.py:174
  212.0 4.0 collective-permute-done.22
  219.2 3.8 add_convert_fusion.2
  223.0 7.7 %all-gather.7.cloned.1.call-done = bf16[16,72,2152]{2,1,0:T(8,128)(2,1)} async-done(((bf16[2,72,2152]{2,1,0:T(8,128)(2,1)}), bf16[16,72,2152]{2,1,0:T(8,128)(2,1)}) %all-gather.7.cloned.1.call-update) | async-done | bytes 4958224 | tf_op jit(solution)/shard_map/all_gather | solution.py:405
  230.7 11.9 %add_convert_fusion = (bf16[1024,2152]{1,0:T(8,128)(2,1)S(1)}, bf16[1024,2152]{1,0:T(8,128)(2,1)S(1)}) fusion(f32[2152]{0:T(1024)S(1)} %slice_select_fusion.4, bf16[1024,1152]{1,0:T(8,128)(2,1)} %get-tuple-element.160.left, bf16[1152,2152]{1,0:T(8,128)(2,1)} %bitcast.194), kind=kOutput, calls=%fused_computation.2 | convolution fusion | flops 5121277952 | bytes 16140704 | tf_op jit(solution)/shard_map/dot_general | solution.py:703
  242.7 26.0 %collective-permute-done.23.refs_1_ = bf16[8,1,72,2152]{3,2,1,0:T(8,128)(2,1)} collective-permute-done((bf16[8,1,72,2152]{3,2,1,0:T(8,128)(2,1)}, bf16[8,1,72,2152]{3,2,1,0:T(8,128)(2,1)}, u32[]{:S(2)}, u32[]{:S(2)}) %collective-permute-start.23) | collective-permute-done | bytes 2479136 | tf_op jit(solution)/shard_map/ppermute | solution.py:494
  268.7 5.1 shard_map.277.refs_3_
  274.2 5.1 shard_map.276.refs_2_
  282.4 10.0 %multiply_convert_fusion.right = bf16[1024,2152]{1,0:T(8,128)(2,1)} fusion(bf16[1024,2152]{1,0:T(8,128)(2,1)S(1)} %get-tuple-element.104, bf16[1152,2152]{1,0:T(8,128)(2,1)S(1)} %bitcast.157, bf16[512,1152]{1,0:T(8,128)(2,1)} %collective-permute-done.15, bf16[512,1152]{1,0:T(8,128)(2,1)S(1)} %bitcast.178), kind=kOutput, calls=%fused_computation.1 | convolution fusion | flops 5088534528 | bytes 16132096 | tf_op jit(solution)/shard_map/dot_general | solution.py:716
  292.5 37.0 %collective-permute-done.25 = bf16[576,2152]{1,0:T(8,128)(2,1)S(1)} collective-permute-done((bf16[576,2152]{1,0:T(8,128)(2,1)S(1)}, bf16[576,2152]{1,0:T(8,128)(2,1)S(1)}, u32[]{:S(2)}, u32[]{:S(2)}) %collective-permute-start.25) | collective-permute-done | bytes 2479136 | tf_op jit(solution)/shard_map/ppermute | solution.py:494
  335.5 8.9 %shard_map.279 = bf16[1152,2152]{1,0:T(8,128)(2,1)S(1)} custom-call(bf16[1024,1152]{1,0:T(8,128)(2,1)S(1)} %copy-done.8, bf16[1024,2152]{1,0:T(8,128)(2,1)S(1)} %copy-done.5), custom_call_target="tpu_custom_call" | custom-call | flops 5077204992 | bytes 11724800 | tf_op jit(solution)/shard_map/pallas_call | solution.py:244
  346.6 11.0 %fusion.70 = (bf16[1024,1152]{1,0:T(8,128)(2,1)S(1)}, f32[1024,1152]{1,0:T(8,128)}) fusion(bf16[1024,2152]{1,0:T(8,128)(2,1)} %multiply_convert_fusion.right, bf16[1152,2152]{1,0:T(8,128)(2,1)} %bitcast.195), kind=kOutput, calls=%fused_computation.222 | convolution fusion | flops 5078384640 | bytes 16443392 | tf_op jit(solution)/shard_map/dot_general | solution.py:721
  372.9 5.7 multiply_reduce_fusion.2
  381.5 5.7 fusion.57
  397.2 24.6 %shard_map.282 = (bf16[1,512,576]{2,1,0:T(8,128)(2,1)}, bf16[1,512,576]{2,1,0:T(8,128)(2,1)}, bf16[1,512,576]{2,1,0:T(8,128)(2,1)}, bf16[1,512,576]{2,1,0:T(8,128)(2,1)}, bf16[1,512,576]{2,1,0:T(8,128)(2,1)}) custom-call(s32[3]{0:T(128)} %add_add_fusion.1.info, bf16[1,512,576]{2,1,0:T(8,128)(2,1)} %copy-done.23, ...), custom_call_target="tpu_custom_call" | custom-call | flops 10737418240 | bytes 7077888 | tf_op jit(solution)/shard_map/pallas_call | solution.py:203
  425.2 24.9 %shard_map.283 = (bf16[1,512,576]{2,1,0:T(8,128)(2,1)}, bf16[1,512,576]{2,1,0:T(8,128)(2,1)}, bf16[1,512,576]{2,1,0:T(8,128)(2,1)}, bf16[1,512,576]{2,1,0:T(8,128)(2,1)}, bf16[1,512,576]{2,1,0:T(8,128)(2,1)}) custom-call(s32[3]{0:T(128)} %copy-done.26, bf16[1,512,576]{2,1,0:T(8,128)(2,1)} %get-tuple-element.196.refs_0_, ...), custom_call_target="tpu_custom_call" | custom-call | flops 10737418240 | bytes 7077888 | tf_op jit(solution)/shard_map/pallas_call | solution.py:203
  460.0 9.7 %fusion.71 = f32[1024,1152]{1,0:T(8,128)S(1)} fusion(bf16[1024,2152]{1,0:T(8,128)(2,1)} %copy-done.33, bf16[1152,2152]{1,0:T(8,128)(2,1)} %bitcast.158), kind=kOutput, calls=%fused_computation.223 | convolution fusion | flops 5077204992 | bytes 14084096 | tf_op jit(solution)/shard_map/dot_general | solution.py:775
  470.0 14.8 %collective-permute-done.29 = bf16[576,576]{1,0:T(8,128)(2,1)S(1)} collective-permute-done((bf16[576,576]{1,0:T(8,128)(2,1)S(1)}, bf16[576,576]{1,0:T(8,128)(2,1)S(1)}, u32[]{:S(2)}, u32[]{:S(2)}) %collective-permute-start.29) | collective-permute-done | bytes 663584 | tf_op jit(solution)/shard_map/ppermute | solution.py:362
  486.3 4.1 collective-permute-start.37
  513.5 4.0 fusion.43
  527.4 15.9 %collective-permute-done.42 = bf16[288,576]{1,0:T(8,128)(2,1)S(1)} collective-permute-done((bf16[288,576]{1,0:T(8,128)(2,1)S(1)}, bf16[288,576]{1,0:T(8,128)(2,1)S(1)}, u32[]{:S(2)}, u32[]{:S(2)}) %collective-permute-start.42) | collective-permute-done | bytes 331808 | tf_op jit(solution)/shard_map/ppermute | solution.py:362
  548.4 3.6 slice_add_fusion
  559.8 8.9 %collective-permute-done.31 = bf16[576,576]{1,0:T(8,128)(2,1)S(1)} collective-permute-done((bf16[576,576]{1,0:T(8,128)(2,1)S(1)}, bf16[576,576]{1,0:T(8,128)(2,1)S(1)}, u32[]{:S(2)}, u32[]{:S(2)}) %collective-permute-start.31) | collective-permute-done | bytes 663584 | tf_op jit(solution)/shard_map/ppermute | solution.py:362
  581.5 4.4 fusion.18
  586.0 7.4 %collective-permute-done.34 = f32[13520]{0:T(1024)S(1)} collective-permute-done((f32[13520]{0:T(1024)S(1)}, f32[13520]{0:T(1024)S(1)}, u32[]{:S(2)}, u32[]{:S(2)}) %collective-permute-start.34) | collective-permute-done | bytes 54112 | tf_op jit(solution)/shard_map/ppermute | solution.py:560
  599.7 9.6 %collective-permute-done.35 = f32[13520]{0:T(1024)S(1)} collective-permute-done((f32[13520]{0:T(1024)S(1)}, f32[13520]{0:T(1024)S(1)}, u32[]{:S(2)}, u32[]{:S(2)}) %collective-permute-start.35) | collective-permute-done | bytes 54112 | tf_op jit(solution)/shard_map/ppermute | solution.py:560
  614.0 4.1 collective-permute-done.36
  625.7 3.7 reshape.797
  (467 shorter events, 213.5 us)
Async XLA Ops:
  7.2 182.5 %all-gather.5.cloned.1.call-start = ((), (), s32[]{:S(2)}) async-start(), calls=%async_computation.3 | async-start | bytes 2820096 | tf_op jit(solution)/shard_map/all_gather | solution.py:643
  7.2 19.2 %collective-permute-start.7 = (s32[1]{0:T(128)}, s32[1]{0:T(128)}, u32[]{:S(2)}, u32[]{:S(2)}) collective-permute-start(s32[1]{0:T(128)} %param.17), channel_id=1, source_target_pairs={{0,2},{2,0},{4,6},{6,4},{8,10},{10,8},{12,14},{14,12},{16,18},{18,... | collective-permute-start | bytes 20 | tf_op jit(solution)/shard_map/ppermute | solution.py:362
  15.4 11.8 %collective-permute-start.1 = (bf16[72,1728]{1,0:T(8,128)(2,1)}, bf16[72,1728]{1,0:T(8,128)(2,1)}, u32[]{:S(2)}, u32[]{:S(2)}) collective-permute-start(bf16[72,1728]{1,0:T(8,128)(2,1)} %select_n.721), channel_id=1, source_target_pairs={{0,2},{2,0},{4,6},{6,4},{8,10},{10,8},{12,14},{14,12},{16,18},{18,... | collective-permute-start | bytes 746504 | tf_op jit(solution)/shard_map/ppermute | solution.py:362
  15.5 31.5 %collective-permute-start = (bf16[512,1152]{1,0:T(8,128)(2,1)S(1)}, bf16[512,1152]{1,0:T(8,128)(2,1)S(1)}, u32[]{:S(2)}, u32[]{:S(2)}) collective-permute-start(bf16[512,1152]{1,0:T(8,128)(2,1)S(1)} %bitcast.171), channel_id=1, source_target_pairs={{0,2},{2,0},{4,6},{6,4},{8,10},{10,8},{12,14},{14,12},{16,18},{18,... | collective-permute-start | bytes 3538952 | tf_op jit(solution)/shard_map/ppermute | solution.py:362
  28.4 12.4 %collective-permute-start.3 = (bf16[1,72,1152]{2,1,0:T(8,128)(2,1)S(1)}, bf16[1,72,1152]{2,1,0:T(8,128)(2,1)S(1)}, u32[]{:S(2)}, u32[]{:S(2)}) collective-permute-start(bf16[1,72,1152]{2,1,0:T(8,128)(2,1)S(1)} %slice_select_fusion.3), channel_id=1, source_target_pairs={{0,16},{2,18},{4,20},{6,22},{8,24},{10,26},{12,28},{14,30},{16,0},... | collective-permute-start | bytes 497672 | tf_op jit(solution)/shard_map/ppermute | solution.py:362
  33.5 11.8 %collective-permute-start.4 = (bf16[1,72,1152]{2,1,0:T(8,128)(2,1)S(1)}, bf16[1,72,1152]{2,1,0:T(8,128)(2,1)S(1)}, u32[]{:S(2)}, u32[]{:S(2)}) collective-permute-start(bf16[1,72,1152]{2,1,0:T(8,128)(2,1)S(1)} %slice_select_fusion.3), channel_id=1, source_target_pairs={{0,8},{2,10},{4,12},{6,14},{8,16},{10,18},{12,20},{14,22},{16,24},... | collective-permute-start | bytes 497672 | tf_op jit(solution)/shard_map/ppermute | solution.py:362
  35.7 9.7 %collective-permute-start.6 = (bf16[72,2152]{1,0:T(8,128)(2,1)S(1)}, bf16[72,2152]{1,0:T(8,128)(2,1)S(1)}, u32[]{:S(2)}, u32[]{:S(2)}) collective-permute-start(bf16[72,2152]{1,0:T(8,128)(2,1)S(1)} %broadcast_select_fusion.2), channel_id=1, source_target_pairs={{0,2},{2,0},{4,6},{6,4},{8,10},{10,8},{12,14},{14,12},{16,18},{18,... | collective-permute-start | bytes 929672 | tf_op jit(solution)/shard_map/ppermute | solution.py:362
  40.8 16.9 %collective-permute-start.15 = (bf16[512,1152]{1,0:T(8,128)(2,1)}, bf16[512,1152]{1,0:T(8,128)(2,1)}, u32[]{:S(2)}, u32[]{:S(2)}) collective-permute-start(bf16[512,1152]{1,0:T(8,128)(2,1)} %bitcast.176), channel_id=1, source_target_pairs={{0,2},{2,0},{4,6},{6,4},{8,10},{10,8},{12,14},{14,12},{16,18},{18,... | collective-permute-start | bytes 3538952 | tf_op jit(solution)/shard_map/ppermute | solution.py:362
  52.1 37.3 %collective-permute-start.13 = (bf16[4,1,72,1152]{3,2,1,0:T(8,128)(2,1)S(1)}, bf16[4,1,72,1152]{3,2,1,0:T(8,128)(2,1)S(1)}, u32[]{:S(2)}, u32[]{:S(2)}) collective-permute-start(bf16[4,1,72,1152]{3,2,1,0:T(8,128)(2,1)S(1)} %pad_maximum_fusion.12.refs_0_), channel_id=1, source_target_pairs={{0,1},{1,0},{2,3},{3,2},{4,5},{5,4},{6,7},{7,6},{8,9},{9,8},{10,11... | collective-permute-start | bytes 1990664 | tf_op jit(solution)/shard_map/ppermute | solution.py:494
  53.6 16.2 %collective-permute-start.8 = (bf16[4,1,72,1152]{3,2,1,0:T(8,128)(2,1)S(1)}, bf16[4,1,72,1152]{3,2,1,0:T(8,128)(2,1)}, u32[]{:S(2)}, u32[]{:S(2)}) collective-permute-start(bf16[4,1,72,1152]{3,2,1,0:T(8,128)(2,1)S(1)} %pad_maximum_fusion.12.refs_0_), channel_id=1, source_target_pairs={{0,4},{2,6},{4,0},{6,2},{8,12},{10,14},{12,8},{14,10},{16,20},{18,... | collective-permute-start | bytes 1990664 | tf_op jit(solution)/shard_map/ppermute | solution.py:362
  69.9 11.5 %collective-permute-start.11 = (bf16[2,72,576]{2,1,0:T(8,128)(2,1)S(1)}, bf16[2,72,576]{2,1,0:T(8,128)(2,1)S(1)}, u32[]{:S(2)}, u32[]{:S(2)}) collective-permute-start(bf16[2,72,576]{2,1,0:T(8,128)(2,1)S(1)} %copy-done.60), channel_id=1, source_target_pairs={{0,8},{2,10},{4,12},{6,14},{8,16},{10,18},{12,20},{14,22},{16,24},... | collective-permute-start | bytes 497672 | tf_op jit(solution)/shard_map/ppermute | solution.py:362
  74.7 13.0 %collective-permute-start.10 = (bf16[2,72,576]{2,1,0:T(8,128)(2,1)S(1)}, bf16[2,72,576]{2,1,0:T(8,128)(2,1)S(1)}, u32[]{:S(2)}, u32[]{:S(2)}) collective-permute-start(bf16[2,72,576]{2,1,0:T(8,128)(2,1)S(1)} %copy-done.60), channel_id=1, source_target_pairs={{0,16},{2,18},{4,20},{6,22},{8,24},{10,26},{12,28},{14,30},{16,0},... | collective-permute-start | bytes 497672 | tf_op jit(solution)/shard_map/ppermute | solution.py:362
  76.3 11.5 %collective-permute-start.9 = (bf16[2,72,576]{2,1,0:T(8,128)(2,1)S(1)}, bf16[2,72,576]{2,1,0:T(8,128)(2,1)S(1)}, u32[]{:S(2)}, u32[]{:S(2)}) collective-permute-start(bf16[2,72,576]{2,1,0:T(8,128)(2,1)S(1)} %copy-done.60), channel_id=1, source_target_pairs={{0,24},{2,26},{4,28},{6,30},{8,0},{10,2},{12,4},{14,6},{16,8},{18,... | collective-permute-start | bytes 497672 | tf_op jit(solution)/shard_map/ppermute | solution.py:362
  78.3 15.2 %collective-permute-start.14 = (bf16[4,1,72,1152]{3,2,1,0:T(8,128)(2,1)}, bf16[4,1,72,1152]{3,2,1,0:T(8,128)(2,1)}, u32[]{:S(2)}, u32[]{:S(2)}) collective-permute-start(bf16[4,1,72,1152]{3,2,1,0:T(8,128)(2,1)} %collective-permute-done.8.refs_1_), channel_id=1, source_target_pairs={{0,1},{1,0},{2,3},{3,2},{4,5},{5,4},{6,7},{7,6},{8,9},{9,8},{10,11... | collective-permute-start | bytes 1990664 | tf_op jit(solution)/shard_map/ppermute | solution.py:494
  79.6 151.1 %all-gather.7.cloned.1.call-start = ((), (), s32[]{:S(2)}) async-start(), calls=%async_computation.4 | async-start | bytes 5640192 | tf_op jit(solution)/shard_map/all_gather | solution.py:405
  87.9 35.7 %collective-permute-start.12 = (bf16[4,2,72,576]{3,2,1,0:T(8,128)(2,1)S(1)}, bf16[4,2,72,576]{3,2,1,0:T(8,128)(2,1)S(1)}, u32[]{:S(2)}, u32[]{:S(2)}) collective-permute-start(bf16[4,2,72,576]{3,2,1,0:T(8,128)(2,1)S(1)} %pad_maximum_fusion.11.refs_0_), channel_id=1, source_target_pairs={{0,4},{2,6},{4,0},{6,2},{8,12},{10,14},{12,8},{14,10},{16,20},{18,... | collective-permute-start | bytes 1990664 | tf_op jit(solution)/shard_map/ppermute | solution.py:362
  102.8 67.7 %collective-permute-start.16 = (bf16[1,512,1152]{2,1,0:T(8,128)(2,1)}, bf16[1,512,1152]{2,1,0:T(8,128)(2,1)}, u32[]{:S(2)}, u32[]{:S(2)}) collective-permute-start(bf16[1,512,1152]{2,1,0:T(8,128)(2,1)} %get-tuple-element.172), channel_id=1, source_target_pairs={{0,1},{1,0},{2,3},{3,2},{4,5},{5,4},{6,7},{7,6},{8,9},{9,8},{10,11... | collective-permute-start | bytes 3538952 | tf_op jit(solution)/shard_map/ppermute | solution.py:494
  123.6 420.4 %reduce-scatter.7.cloned.1.call-start = ((), (), s32[]{:S(2)}) async-start(), calls=%async_computation.5 | async-start | bytes 2820096
  125.5 47.2 %collective-permute-start.17 = (bf16[1,512,1152]{2,1,0:T(8,128)(2,1)S(1)}, bf16[1,512,1152]{2,1,0:T(8,128)(2,1)S(1)}, u32[]{:S(2)}, u32[]{:S(2)}) collective-permute-start(bf16[1,512,1152]{2,1,0:T(8,128)(2,1)S(1)} %copy-done.47), channel_id=1, source_target_pairs={{0,1},{1,0},{2,3},{3,2},{4,5},{5,4},{6,7},{7,6},{8,9},{9,8},{10,11... | collective-permute-start | bytes 3538952 | tf_op jit(solution)/shard_map/ppermute | solution.py:494
  127.1 14.0 %collective-permute-start.20 = (bf16[1,72,1152]{2,1,0:T(8,128)(2,1)}, bf16[1,72,1152]{2,1,0:T(8,128)(2,1)S(1)}, u32[]{:S(2)}, u32[]{:S(2)}) collective-permute-start(bf16[1,72,1152]{2,1,0:T(8,128)(2,1)} %bitcast.33), channel_id=1, source_target_pairs={{0,8},{2,10},{4,12},{6,14},{8,16},{10,18},{12,20},{14,22},{16,24},... | collective-permute-start | bytes 497672 | tf_op jit(solution)/shard_map/ppermute | solution.py:362
  132.8 12.4 %collective-permute-start.19 = (bf16[1,72,1152]{2,1,0:T(8,128)(2,1)}, bf16[1,72,1152]{2,1,0:T(8,128)(2,1)S(1)}, u32[]{:S(2)}, u32[]{:S(2)}) collective-permute-start(bf16[1,72,1152]{2,1,0:T(8,128)(2,1)} %bitcast.33), channel_id=1, source_target_pairs={{0,16},{2,18},{4,20},{6,22},{8,24},{10,26},{12,28},{14,30},{16,0},... | collective-permute-start | bytes 497672 | tf_op jit(solution)/shard_map/ppermute | solution.py:362
  146.3 21.9 %collective-permute-start.21 = (bf16[4,1,72,1152]{3,2,1,0:T(8,128)(2,1)S(1)}, bf16[4,1,72,1152]{3,2,1,0:T(8,128)(2,1)S(1)}, u32[]{:S(2)}, u32[]{:S(2)}) collective-permute-start(bf16[4,1,72,1152]{3,2,1,0:T(8,128)(2,1)S(1)} %pad_maximum_fusion.13.refs_0_), channel_id=1, source_target_pairs={{0,4},{2,6},{4,0},{6,2},{8,12},{10,14},{12,8},{14,10},{16,20},{18,... | collective-permute-start | bytes 1990664 | tf_op jit(solution)/shard_map/ppermute | solution.py:362
  212.0 56.7 %collective-permute-start.23 = (bf16[8,1,72,2152]{3,2,1,0:T(8,128)(2,1)}, bf16[8,1,72,2152]{3,2,1,0:T(8,128)(2,1)}, u32[]{:S(2)}, u32[]{:S(2)}) collective-permute-start(bf16[8,1,72,2152]{3,2,1,0:T(8,128)(2,1)} %bitcast.74.refs_5_.refs_0_), channel_id=1, source_target_pairs={{0,1},{1,0},{2,3},{3,2},{4,5},{5,4},{6,7},{7,6},{8,9},{9,8},{10,11... | collective-permute-start | bytes 7437320 | tf_op jit(solution)/shard_map/ppermute | solution.py:494
  273.8 55.6 %collective-permute-start.25 = (bf16[576,2152]{1,0:T(8,128)(2,1)S(1)}, bf16[576,2152]{1,0:T(8,128)(2,1)S(1)}, u32[]{:S(2)}, u32[]{:S(2)}) collective-permute-start(bf16[576,2152]{1,0:T(8,128)(2,1)S(1)} %shard_map.277.refs_3_), channel_id=1, source_target_pairs={{0,1},{1,0},{2,3},{3,2},{4,5},{5,4},{6,7},{7,6},{8,9},{9,8},{10,11... | collective-permute-start | bytes 7437320 | tf_op jit(solution)/shard_map/ppermute | solution.py:494
  331.5 237.3 %reduce-scatter.5.cloned.1.call-start = ((), (), s32[]{:S(2)}) async-start(), calls=%async_computation.2 | async-start | bytes 5640192 | tf_op jit(solution)/shard_map/reduce_scatter | solution.py:414
  359.4 13.5 %collective-permute-start.24 = (bf16[1024,1152]{1,0:T(8,128)(2,1)}, bf16[1024,1152]{1,0:T(8,128)(2,1)}, u32[]{:S(2)}, u32[]{:S(2)}) collective-permute-start(bf16[1024,1152]{1,0:T(8,128)(2,1)} %pad_maximum_fusion.3), channel_id=1, source_target_pairs={{0,2},{2,0},{4,6},{6,4},{8,10},{10,8},{12,14},{14,12},{16,18},{18,... | collective-permute-start | bytes 7077896 | tf_op jit(solution)/shard_map/ppermute | solution.py:362
  424.5 61.2 %collective-permute-start.27 = (bf16[1,512,1152]{2,1,0:T(8,128)(2,1)}, bf16[1,512,1152]{2,1,0:T(8,128)(2,1)S(1)}, u32[]{:S(2)}, u32[]{:S(2)}) collective-permute-start(bf16[1,512,1152]{2,1,0:T(8,128)(2,1)} %pad_maximum_fusion.9), channel_id=1, source_target_pairs={{0,1},{1,0},{2,3},{3,2},{4,5},{5,4},{6,7},{7,6},{8,9},{9,8},{10,11... | collective-permute-start | bytes 3538952 | tf_op jit(solution)/shard_map/ppermute | solution.py:494
  456.7 28.1 %collective-permute-start.29 = (bf16[576,576]{1,0:T(8,128)(2,1)S(1)}, bf16[576,576]{1,0:T(8,128)(2,1)S(1)}, u32[]{:S(2)}, u32[]{:S(2)}) collective-permute-start(bf16[576,576]{1,0:T(8,128)(2,1)S(1)} %shard_map.285), channel_id=1, source_target_pairs={{0,4},{2,6},{4,0},{6,2},{8,12},{10,14},{12,8},{14,10},{16,20},{18,... | collective-permute-start | bytes 1990664 | tf_op jit(solution)/shard_map/ppermute | solution.py:362
  458.7 27.6 %collective-permute-start.28 = (bf16[1,512,1152]{2,1,0:T(8,128)(2,1)S(1)}, bf16[1,512,1152]{2,1,0:T(8,128)(2,1)S(1)}, u32[]{:S(2)}, u32[]{:S(2)}) collective-permute-start(bf16[1,512,1152]{2,1,0:T(8,128)(2,1)S(1)} %pad_maximum_fusion.10), channel_id=1, source_target_pairs={{0,1},{1,0},{2,3},{3,2},{4,5},{5,4},{6,7},{7,6},{8,9},{9,8},{10,11... | collective-permute-start | bytes 3538952 | tf_op jit(solution)/shard_map/ppermute | solution.py:494
  469.9 43.5 %collective-permute-start.26 = (bf16[512,1152]{1,0:T(8,128)(2,1)S(1)}, bf16[512,1152]{1,0:T(8,128)(2,1)}, u32[]{:S(2)}, u32[]{:S(2)}) collective-permute-start(bf16[512,1152]{1,0:T(8,128)(2,1)S(1)} %slice.705), channel_id=1, source_target_pairs={{0,2},{2,0},{4,6},{6,4},{8,10},{10,8},{12,14},{14,12},{16,18},{18,... | collective-permute-start | bytes 3538952 | tf_op jit(solution)/shard_map/ppermute | solution.py:362
  486.3 31.9 %collective-permute-start.37 = (bf16[144,576]{1,0:T(8,128)(2,1)}, bf16[144,576]{1,0:T(8,128)(2,1)}, u32[]{:S(2)}, u32[]{:S(2)}) collective-permute-start(bf16[144,576]{1,0:T(8,128)(2,1)} %get-tuple-element.131), channel_id=1, source_target_pairs={{0,8},{2,10},{4,12},{6,14},{8,16},{10,18},{12,20},{14,22},{16,24},... | collective-permute-start | bytes 497672 | tf_op jit(solution)/shard_map/ppermute | solution.py:362
  490.3 28.3 %collective-permute-start.38 = (bf16[144,576]{1,0:T(8,128)(2,1)}, bf16[144,576]{1,0:T(8,128)(2,1)}, u32[]{:S(2)}, u32[]{:S(2)}) collective-permute-start(bf16[144,576]{1,0:T(8,128)(2,1)} %get-tuple-element.132), channel_id=1, source_target_pairs={{0,16},{2,18},{4,20},{6,22},{8,24},{10,26},{12,28},{14,30},{16,0},... | collective-permute-start | bytes 497672 | tf_op jit(solution)/shard_map/ppermute | solution.py:362
  492.0 26.7 %collective-permute-start.39 = (bf16[144,576]{1,0:T(8,128)(2,1)}, bf16[144,576]{1,0:T(8,128)(2,1)}, u32[]{:S(2)}, u32[]{:S(2)}) collective-permute-start(bf16[144,576]{1,0:T(8,128)(2,1)} %get-tuple-element.133), channel_id=1, source_target_pairs={{0,24},{2,26},{4,28},{6,30},{8,0},{10,2},{12,4},{14,6},{16,8},{18,... | collective-permute-start | bytes 497672 | tf_op jit(solution)/shard_map/ppermute | solution.py:362
  496.3 24.4 %collective-permute-start.41 = (bf16[576,576]{1,0:T(8,128)(2,1)S(1)}, bf16[576,576]{1,0:T(8,128)(2,1)}, u32[]{:S(2)}, u32[]{:S(2)}) collective-permute-start(bf16[576,576]{1,0:T(8,128)(2,1)S(1)} %shard_map.287), channel_id=1, source_target_pairs={{0,1},{1,0},{2,3},{3,2},{4,5},{5,4},{6,7},{7,6},{8,9},{9,8},{10,11... | collective-permute-start | bytes 1990664 | tf_op jit(solution)/shard_map/ppermute | solution.py:494
  513.4 34.5 %collective-permute-start.30 = (bf16[512,1152]{1,0:T(8,128)(2,1)}, bf16[512,1152]{1,0:T(8,128)(2,1)}, u32[]{:S(2)}, u32[]{:S(2)}) collective-permute-start(bf16[512,1152]{1,0:T(8,128)(2,1)} %slice.704), channel_id=1, source_target_pairs={{0,2},{2,0},{4,6},{6,4},{8,10},{10,8},{12,14},{14,12},{16,18},{18,... | collective-permute-start | bytes 3538952 | tf_op jit(solution)/shard_map/ppermute | solution.py:362
  518.2 54.3 %collective-permute-start.47 = (bf16[288,1152]{1,0:T(8,128)(2,1)}, bf16[288,1152]{1,0:T(8,128)(2,1)}, u32[]{:S(2)}, u32[]{:S(2)}) collective-permute-start(bf16[288,1152]{1,0:T(8,128)(2,1)} %copy-done.15), channel_id=1, source_target_pairs={{0,4},{2,6},{4,0},{6,2},{8,12},{10,14},{12,8},{14,10},{16,20},{18,... | collective-permute-start | bytes 1990664 | tf_op jit(solution)/shard_map/ppermute | solution.py:362
  522.0 21.3 %collective-permute-start.42 = (bf16[288,576]{1,0:T(8,128)(2,1)S(1)}, bf16[288,576]{1,0:T(8,128)(2,1)S(1)}, u32[]{:S(2)}, u32[]{:S(2)}) collective-permute-start(bf16[288,576]{1,0:T(8,128)(2,1)S(1)} %get-tuple-element.185), channel_id=1, source_target_pairs={{0,4},{2,6},{4,0},{6,2},{8,12},{10,14},{12,8},{14,10},{16,20},{18,... | collective-permute-start | bytes 995336 | tf_op jit(solution)/shard_map/ppermute | solution.py:362
  552.0 16.8 %collective-permute-start.31 = (bf16[576,576]{1,0:T(8,128)(2,1)S(1)}, bf16[576,576]{1,0:T(8,128)(2,1)S(1)}, u32[]{:S(2)}, u32[]{:S(2)}) collective-permute-start(bf16[576,576]{1,0:T(8,128)(2,1)S(1)} %shard_map.289), channel_id=1, source_target_pairs={{0,4},{2,6},{4,0},{6,2},{8,12},{10,14},{12,8},{14,10},{16,20},{18,... | collective-permute-start | bytes 1990664 | tf_op jit(solution)/shard_map/ppermute | solution.py:362
  572.5 22.6 %collective-permute-start.48 = (bf16[144,576]{1,0:T(8,128)(2,1)S(1)}, bf16[144,576]{1,0:T(8,128)(2,1)S(1)}, u32[]{:S(2)}, u32[]{:S(2)}) collective-permute-start(bf16[144,576]{1,0:T(8,128)(2,1)S(1)} %get-tuple-element.142), channel_id=1, source_target_pairs={{0,8},{2,10},{4,12},{6,14},{8,16},{10,18},{12,20},{14,22},{16,24},... | collective-permute-start | bytes 497672 | tf_op jit(solution)/shard_map/ppermute | solution.py:362
  573.1 22.1 %collective-permute-start.49 = (bf16[144,576]{1,0:T(8,128)(2,1)S(1)}, bf16[144,576]{1,0:T(8,128)(2,1)S(1)}, u32[]{:S(2)}, u32[]{:S(2)}) collective-permute-start(bf16[144,576]{1,0:T(8,128)(2,1)S(1)} %get-tuple-element.143), channel_id=1, source_target_pairs={{0,16},{2,18},{4,20},{6,22},{8,24},{10,26},{12,28},{14,30},{16,0},... | collective-permute-start | bytes 497672 | tf_op jit(solution)/shard_map/ppermute | solution.py:362
  574.9 21.9 %collective-permute-start.50 = (bf16[144,576]{1,0:T(8,128)(2,1)S(1)}, bf16[144,576]{1,0:T(8,128)(2,1)S(1)}, u32[]{:S(2)}, u32[]{:S(2)}) collective-permute-start(bf16[144,576]{1,0:T(8,128)(2,1)S(1)} %get-tuple-element.144), channel_id=1, source_target_pairs={{0,24},{2,26},{4,28},{6,30},{8,0},{10,2},{12,4},{14,6},{16,8},{18,... | collective-permute-start | bytes 497672 | tf_op jit(solution)/shard_map/ppermute | solution.py:362
  579.0 31.8 %collective-permute-start.53 = (bf16[72,1152]{1,0:T(8,128)(2,1)S(1)}, bf16[72,1152]{1,0:T(8,128)(2,1)S(1)}, u32[]{:S(2)}, u32[]{:S(2)}) collective-permute-start(bf16[72,1152]{1,0:T(8,128)(2,1)S(1)} %get-tuple-element.190), channel_id=1, source_target_pairs={{0,8},{2,10},{4,12},{6,14},{8,16},{10,18},{12,20},{14,22},{16,24},... | collective-permute-start | bytes 497672 | tf_op jit(solution)/shard_map/ppermute | solution.py:362
  581.4 12.0 %collective-permute-start.34 = (f32[13520]{0:T(1024)S(1)}, f32[13520]{0:T(1024)S(1)}, u32[]{:S(2)}, u32[]{:S(2)}) collective-permute-start(f32[13520]{0:T(1024)S(1)} %add.832), channel_id=1, source_target_pairs={{0,8},{2,10},{4,12},{6,14},{8,0},{10,2},{12,4},{14,6},{16,24},{18,... | collective-permute-start | bytes 162248 | tf_op jit(solution)/shard_map/ppermute | solution.py:560
  593.4 18.0 %collective-permute-start.55 = (bf16[72,1152]{1,0:T(8,128)(2,1)S(1)}, bf16[72,1152]{1,0:T(8,128)(2,1)S(1)}, u32[]{:S(2)}, u32[]{:S(2)}) collective-permute-start(bf16[72,1152]{1,0:T(8,128)(2,1)S(1)} %get-tuple-element.191), channel_id=1, source_target_pairs={{0,24},{2,26},{4,28},{6,30},{8,0},{10,2},{12,4},{14,6},{16,8},{18,... | collective-permute-start | bytes 497672 | tf_op jit(solution)/shard_map/ppermute | solution.py:362
  595.1 16.4 %collective-permute-start.54 = (bf16[72,1152]{1,0:T(8,128)(2,1)S(1)}, bf16[72,1152]{1,0:T(8,128)(2,1)S(1)}, u32[]{:S(2)}, u32[]{:S(2)}) collective-permute-start(bf16[72,1152]{1,0:T(8,128)(2,1)S(1)} %get-tuple-element.192), channel_id=1, source_target_pairs={{0,16},{2,18},{4,20},{6,22},{8,24},{10,26},{12,28},{14,30},{16,0},... | collective-permute-start | bytes 497672 | tf_op jit(solution)/shard_map/ppermute | solution.py:362
  595.2 25.8 %collective-permute-start.57 = (bf16[144,2152]{1,0:T(8,128)(2,1)S(1)}, bf16[144,2152]{1,0:T(8,128)(2,1)}, u32[]{:S(2)}, u32[]{:S(2)}) collective-permute-start(bf16[144,2152]{1,0:T(8,128)(2,1)S(1)} %copy-done.67), channel_id=1, source_target_pairs={{0,1},{1,0},{2,3},{3,2},{4,5},{5,4},{6,7},{7,6},{8,9},{9,8},{10,11... | collective-permute-start | bytes 1859336 | tf_op jit(solution)/shard_map/ppermute | solution.py:545
  596.8 12.6 %collective-permute-start.35 = (f32[13520]{0:T(1024)S(1)}, f32[13520]{0:T(1024)S(1)}, u32[]{:S(2)}, u32[]{:S(2)}) collective-permute-start(f32[13520]{0:T(1024)S(1)} %add.833), channel_id=1, source_target_pairs={{0,16},{2,18},{4,20},{6,22},{8,24},{10,26},{12,28},{14,30},{16,0},... | collective-permute-start | bytes 162248 | tf_op jit(solution)/shard_map/ppermute | solution.py:560
  609.3 10.1 %collective-permute-start.51 = (bf16[144,576]{1,0:T(8,128)(2,1)S(1)}, bf16[144,576]{1,0:T(8,128)(2,1)S(1)}, u32[]{:S(2)}, u32[]{:S(2)}) collective-permute-start(bf16[144,576]{1,0:T(8,128)(2,1)S(1)} %add_convert_fusion.12), channel_id=1, source_target_pairs={{0,1},{1,0},{2,3},{3,2},{4,5},{5,4},{6,7},{7,6},{8,9},{9,8},{10,11... | collective-permute-start | bytes 497672 | tf_op jit(solution)/shard_map/ppermute | solution.py:545
  (107 other events, 995.9 us)
Sparse Core Ops, SparseCore 0:
  79.7 62.3 all-gather.4
  144.2 86.4 all-gather.6
  331.6 72.7 reduce-scatter.6
  407.9 120.6 reduce-scatter.4

commit v4 on v3

--- a/solution.py
+++ b/solution.py
@@ -633,29 +633,21 @@
         scatter_seq, seq_order = ScatterX, order
         pair_lines, pair_pieces = gather_all(grid, pair_block)
         pair_slots = all_kinds
-    pair_pieces[1], query_block, down_block = together(pair_pieces[1], query_block, down_block)
+    pair_pieces[1], query_block, up_block = together(pair_pieces[1], query_block, up_block)
     query_lines, query_pieces = gather_all(grid, query_block)
-    query_pieces[1], out_block, up_block = together(query_pieces[1], out_weight[None], up_block)
+    query_pieces[1], out_block, down_block = together(
+        query_pieces[1], out_weight[None], down_block
+    )
     out_lines, out_pieces = gather_all(grid, out_block)
 
-    if groups == 2:
-        kinds_by_seq = jnp.stack(grid.kinds_by_seq())
-        own_down = lax.all_gather(
-            by_seq(down_block[0], down_block[1])[None],
-            "fsdp",
-            axis_index_groups=grid.groups(),
-        )
-        own_down = [own_down, swap_seq(own_down)]
-    else:
-        own_down = grid.gather(down_block)
-    own_up = grid.gather(up_block)
+    own_up, own_down = grid.gather(up_block), grid.gather(down_block)
 
     back_low = both(cotangent)
 
     own_pair = place(pair_pieces, pair_slots).reshape(width, 2 * own_width)
     pair_bias = jnp.concatenate([jnp.zeros((own_width,), f32), vector_kind(value_bias)])
     pairs = (jnp.dot(normed_one, own_pair, preferred_element_type=f32) + pair_bias).astype(bf16)
-    pairs, row_source, back_source = together(pairs, normed_one, back_low)
+    pairs, row_source = together(pairs, normed_one)
     own_query = place(query_pieces, all_kinds)
     own_query = own_query.reshape(width, own_width)
     queries = (
@@ -664,12 +656,7 @@
 
     one_rows = reorder(row_source, order)
     seq_rows = reorder(row_source, seq_order) if groups == 2 else one_rows
-    kind_rows = []
-    if groups == 2:
-        kind_rows = reorder(back_source, order_matrix(grid.kinds_by_seq(), shard_rows))
-    made = [[*one_rows, *seq_rows, *kind_rows]] + [[]] * (2 * images - 1)
-    if groups == 2:
-        made[images] = [own_down[0]]
+    made = [[*one_rows, *seq_rows]] + [[]] * (2 * images - 1)
 
     place_seq = lax.axis_index("seq") * local_len
     attended_parts, saved = [], []
@@ -693,7 +680,7 @@
         saved.append((info, query, key_parts, value_parts, lse))
     attended = jnp.concatenate(attended_parts, axis=0)
 
-    own_out = place(out_pieces, all_members)
+    own_out = place(out_pieces, all_members, attended_parts[-1:])
     own_out = own_out.reshape(own_width, width)
     partial = jnp.dot(attended, own_out, preferred_element_type=f32)
     resid = inputs + partial + grid.swap_rows(partial, rows) + out_bias
@@ -703,15 +690,9 @@
     hidden = jnp.dot(normed_two, own_up, preferred_element_type=f32) + own_up_bias
     active, slope = gelu_and_slope(hidden)
     active, slope = together(active.astype(bf16), slope.astype(bf16))
-    if groups == 2:
-        active, own_down[1] = together(active, own_down[1])
-    if groups == 2:
-        down_kept, down_going = halves_of(kind_rows, active)
-        down_came = swap_seq(down_going)
-        own_down = place(own_down, kinds_by_seq, [down_kept, down_going])
-        own_down = own_down.reshape(width, hidden_half)
-    else:
-        grad_down = grid.scatter(contract_rows(back_low, active))
+    grad_down = contract_rows(back_low, active)
+    back_low, grad_down = together(back_low, grad_down)
+    grad_down = grid.scatter(grad_down)
 
     d_active = jnp.dot(back_low, own_down, preferred_element_type=f32)
     d_hidden = (d_active * slope).astype(bf16)
@@ -735,9 +716,6 @@
         info, query, key_parts, value_parts, lse = saved[image]
         if image == 0:
             on_their_way = [grad_out.kept, grad_out.going]
-        elif image == images and groups == 2:
-            on_their_way = add_pieces(down_kept, down_came, 1)
-            down_total = on_their_way[0]
         else:
             on_their_way = []
         d_query_part, key_grads, value_grads = attend_back(
@@ -754,6 +732,8 @@
             near = jnp.concatenate([key_grads[1], value_grads[1]], axis=2)
             d_query[-1], near = together(d_query[-1], near)
             far = swap_seq(near)
+            if image == 0:
+                first_far = far
             if image == 2 * images - 1:
                 last_far = far
             d_key.append((key_grads[0], far[:, :, :own_width]))
@@ -768,6 +748,10 @@
                     )
                 )
     d_query = jnp.concatenate(d_query, axis=0)
+    if groups == 2:
+        d_query, first_far = together(d_query, first_far)
+        d_key[0] = (d_key[0][0], first_far[:, :, :own_width])
+        d_value[0] = (d_value[0][0], first_far[:, :, own_width:])
     grad_query = ScatterX(grid, one_rows, d_query)
     late_active, grad_query.kept, grad_query.going = together(
         active, grad_query.kept, grad_query.going
@@ -777,9 +761,8 @@
     )
     came = grid.send(partial[rows:].astype(bf16), step_twin=1).astype(f32)
     outputs = (resid[:rows] + partial[:rows] + came + down_bias).astype(bf16)
-    grad_query.add()
     if groups == 2:
-        last_far, *grad_query.sums = together(last_far, *grad_query.sums)
+        last_far, grad_down = together(last_far, grad_down)
         d_key[-1] = (d_key[-1][0], last_far[:, :, :own_width])
         d_value[-1] = (d_value[-1][0], last_far[:, :, own_width:])
 
@@ -811,42 +794,23 @@
         )
     )
     d_one = partial[:rows] + grid.send(partial[rows:].astype(bf16), step_twin=1).astype(f32)
-    d_one, grad_value.came, grad_up = together(d_one, grad_value.came, grad_up)
+    grad_down = sum_seq(grad_down)
+    grad_out.came, grad_query.came, grad_key.came, grad_value.came, grad_down = together(
+        grad_out.came, grad_query.came, grad_key.came, grad_value.came, grad_down
+    )
+    grad_out.add()
+    grad_query.add()
     grad_value.add()
     if groups == 2:
         grad_key.cross()
-    (grad_out.came, grad_out.kept, *grad_value.sums) = together(
-        grad_out.came, grad_out.kept, *grad_value.sums
-    )
-    grad_out.add()
     grad_tokens = d_resid[:rows] + norm_back(d_one, normal_one[:rows], scale_one[:rows], attn_gain)
     grad_key.add()
     grad_out = grad_out.finish()
     grad_up = sum_seq(grad_up)
-    if groups == 2:
-        grad_down = lax.psum_scatter(
-            down_total,
-            "fsdp",
-            scatter_dimension=0,
-            axis_index_groups=grid.groups(),
-            tiled=True,
-        )
-        grad_down, *grad_key.sums = together(grad_down, *grad_key.sums)
-        other = swap_seq(grad_down)
-        grad_down = by_seq(
-            jnp.concatenate([grad_down, other]), jnp.concatenate([other, grad_down])
-        ).astype(f32)
-    else:
-        grad_down = sum_seq(grad_down)
     grad_qkv = jnp.concatenate(
         [grad_query.finish(), grad_key.finish(), grad_value.finish()], axis=1
     )
 
-    grad_up, grad_down = (
-        jnp.concatenate(grid.swap_mine(total[:shard_rows], total[shard_rows:]), axis=1)
-        for total in (grad_up, grad_down)
-    )
-    grad_down = grad_down.T
     grad_qkv = jnp.stack(
         [member.reshape(shard_rows, 3, heads // 2, HD) for member in swap_twin(grid, grad_qkv)],
         axis=3,
@@ -857,8 +821,7 @@
         nothing = jnp.zeros_like(vector)
         return jnp.stack(grid.in_order(vector, nothing), axis=axis).reshape(-1)
 
-    vectors = sum_all(
-        jnp.concatenate(
+    vectors = jnp.concatenate(
             [
                 column_sum(d_one * normal_one[:rows]),
                 column_sum(d_one),
@@ -871,7 +834,13 @@
                 at_kind(column_sum(d_hidden), (-1,), 0),
             ]
         )
-    )
+    vectors, grad_up = together(vectors, grad_up)
+    vectors = sum_all(vectors)
+    grad_up, grad_down = (
+        jnp.concatenate(grid.swap_mine(total[:shard_rows], total[shard_rows:]), axis=1)
+        for total in (grad_up, grad_down)
+    )
+    grad_down = grad_down.T
     (
         grad_attn_gain,
         grad_attn_shift,

time: 647 us -> 616 us (0.952)
  waiting for transfers between devices: 197 us -> 171 us
  other arithmetic: 90.6 us -> 79.6 us
  local copies, waits for them, and re-layouts: 51.3 us -> 58.2 us
    ppermute x11 -> x8, waiting for transfers between devices: 70.6 us -> 29.9 us  [swap_seq(): return lax.ppermute(value, 'seq', [(0, 1), (1, 0)])]
    ppermute x41, waiting for transfers between devices: 91.8 us -> 118 us  [send(): return lax.ppermute(value, 'fsdp', self.pairs(**steps))]
    ppermute x5, waiting for transfers between devices: 23.5 us -> 5.02 us  [sum_all(): lax.ppermute(vector, axis, [(member, member ^ step) for member in range(c...]
    all_gather x1 -> x2, waiting for transfers between devices: 7.7 us -> 17.5 us  [gather(): whole = lax.all_gather(block, 'fsdp', axis_index_groups=self.groups())]
    dot_general x8 -> x6, matrix products: 24.5 us -> 19 us  [reorder(): jnp.dot(rows, part, preferred_element_type=f32).astype(bf16)]
    unnamed x187 -> x192, local copies, waits for them, and re-layouts: 16.9 us -> 19.6 us
    pallas_call x11 -> x10, Pallas kernels: 37.3 us -> 37.4 us  [contract_rows(): pl.pallas_call(contract_kernel, grid=(pl.cdiv(columns, block),), in_specs...]
  transfers between devices with their start and end apart: 65 -> 63, of which waited for: 25 -> 26; matrix products, arithmetic and copies ran while one was open for 32% -> 27% of each run, Pallas kernels for 19% -> 19%
where the time goes in v4:
time: 616 us; the launch traced here: 606 us
  waiting for transfers between devices  171 us (28%)
  Pallas kernels  125 us (20%)
  matrix products  82.1 us (13%)
  other arithmetic  79.6 us (13%)
  starting transfers between devices  73.5 us (12%)
  local copies, waits for them, and re-layouts  58.2 us (9%)
  between operations  17 us (3%)
    ppermute x41, waiting for transfers between devices, send(): return lax.ppermute(value, 'fsdp', self.pairs(**steps))  118 us
    ppermute x41, starting transfers between devices, send(): return lax.ppermute(value, 'fsdp', self.pairs(**steps))  58.8 us
    pallas_call x2, Pallas kernels, attend_back(): pl.pallas_call(functools.partial(attend_back_kernel, parts, heads, min(bl...  49.6 us
    pallas_call x10, Pallas kernels, contract_rows(): pl.pallas_call(contract_kernel, grid=(pl.cdiv(columns, block),), in_specs...  37.4 us
    ppermute x8, waiting for transfers between devices, swap_seq(): return lax.ppermute(value, 'seq', [(0, 1), (1, 0)])  29.9 us
    pallas_call x2, Pallas kernels, attend(): pl.pallas_call(functools.partial(attend_kernel, parts, heads, min(block,...  29.5 us
    unnamed x192, local copies, waits for them, and re-layouts  19.6 us
    dot_general x6, matrix products, reorder(): jnp.dot(rows, part, preferred_element_type=f32).astype(bf16)  19 us
  transfers between devices with their start and end apart: 63, of which 26 were waited for; matrix products, arithmetic and copies ran while one was open for 27% of the time, Pallas kernels for 19%

profile of v4, /device:TPU:0, one launch (start us, length us, event | category | flops | bytes accessed | tf_op | source)
XLA Modules:
  0.0 606.5 jit_solution(5309077385520590832)
XLA Ops:
  7.2 4.5 reshape.618
  18.9 3.7 collective-permute-start.3
  26.2 5.0 collective-permute-done.3
  31.3 4.5 collective-permute-done.4
  38.7 3.9 fusion
  44.1 15.0 %collective-permute-done.8.refs_1_ = bf16[4,1,72,1152]{3,2,1,0:T(8,128)(2,1)S(1)} collective-permute-done((bf16[4,1,72,1152]{3,2,1,0:T(8,128)(2,1)S(1)}, bf16[4,1,72,1152]{3,2,1,0:T(8,128)(2,1)S(1)}, u32[]{:S(2)}, u32[]{:S(2)}) %collective-permute-start.8) | collective-permute-done | bytes 663584 | tf_op jit(solution)/shard_map/ppermute | solution.py:362
  67.5 3.7 collective-permute-start.11
  79.7 12.2 %collective-permute-done.10 = bf16[2,72,576]{2,1,0:T(8,128)(2,1)S(1)} collective-permute-done((bf16[2,72,576]{2,1,0:T(8,128)(2,1)S(1)}, bf16[2,72,576]{2,1,0:T(8,128)(2,1)S(1)}, u32[]{:S(2)}, u32[]{:S(2)}) %collective-permute-start.10) | collective-permute-done | bytes 165920 | tf_op jit(solution)/shard_map/ppermute | solution.py:362
  95.3 4.1 shard_map.272
  99.5 3.7 add_convert_fusion.2
  109.6 3.5 fusion.21.refs_6_.left
  115.5 3.6 fusion.27.refs_8_.left
  119.1 3.5 fusion.24.refs_7_.left
  125.1 12.8 %collective-permute-start.19 = (bf16[1,72,1152]{2,1,0:T(8,128)(2,1)}, bf16[1,72,1152]{2,1,0:T(8,128)(2,1)}, u32[]{:S(2)}, u32[]{:S(2)}) collective-permute-start(bf16[1,72,1152]{2,1,0:T(8,128)(2,1)} %bitcast.33), channel_id=1, source_target_pairs={{0,8},{2,10},{4,12},{6,14},{8,16},{10,18},{12,20},{14,22},{16,24},... | collective-permute-start | bytes 497672 | tf_op jit(solution)/shard_map/ppermute | solution.py:362
  137.9 3.4 collective-permute-start.18
  144.2 4.1 add_convert_fusion.4
  149.0 9.4 %collective-permute-done.18 = bf16[1,72,1152]{2,1,0:T(8,128)(2,1)} collective-permute-done((bf16[1,72,1152]{2,1,0:T(8,128)(2,1)}, bf16[1,72,1152]{2,1,0:T(8,128)(2,1)}, u32[]{:S(2)}, u32[]{:S(2)}) %collective-permute-start.18) | collective-permute-done | bytes 165920 | tf_op jit(solution)/shard_map/ppermute | solution.py:362
  165.1 14.5 %shard_map.274 = (bf16[1,512,576]{2,1,0:T(8,128)(2,1)S(1)}, f32[8,1,512]{2,1,0:T(1,128)S(1)}) custom-call(s32[3]{0:T(128)S(1)} %add_add_fusion.2.info, bf16[1,512,576]{2,1,0:T(8,128)(2,1)S(1)} %get-tuple-element.176.refs_0_, bf16[1,512,576]{2,1,0:T(8,128)(2,1)S(1)} %copy-done.31, bf16[1,512,576]{2,1,0:T(8,128)(2,1)S(1)} %get-tuple-element.188.refs_2_.refs_4_, ...), custom_call_target="tpu_custom_call" | custom-call | flops 4294967296 | bytes 3538944 | tf_op jit(solution)/shard_map/pallas_call | solution.py:174
  183.0 14.9 %shard_map.273 = (bf16[1,512,576]{2,1,0:T(8,128)(2,1)S(1)}, f32[8,1,512]{2,1,0:T(1,128)S(1)}) custom-call(s32[3]{0:T(128)S(1)} %add_add_fusion.1.info, bf16[1,512,576]{2,1,0:T(8,128)(2,1)S(1)} %get-tuple-element.175.refs_0_, bf16[1,512,576]{2,1,0:T(8,128)(2,1)S(1)} %copy-done.33, bf16[1,512,576]{2,1,0:T(8,128)(2,1)S(1)} %get-tuple-element.184.refs_2_.refs_4_, ...), custom_call_target="tpu_custom_call" | custom-call | flops 4294967296 | bytes 3538944 | tf_op jit(solution)/shard_map/pallas_call | solution.py:174
  201.7 5.1 collective-permute-done.22
  210.3 3.8 add_convert_fusion.1
  214.2 12.9 %add_convert_fusion = (bf16[1024,2152]{1,0:T(8,128)(2,1)}, bf16[1024,2152]{1,0:T(8,128)(2,1)S(1)}) fusion(f32[2152]{0:T(1024)S(1)} %slice_select_fusion.3, bf16[1024,1152]{1,0:T(8,128)(2,1)} %get-tuple-element.142.left, bf16[1152,2152]{1,0:T(8,128)(2,1)} %bitcast.172), kind=kOutput, calls=%fused_computation.2 | convolution fusion | flops 5121277952 | bytes 16140704 | tf_op jit(solution)/shard_map/dot_general | solution.py:690
  227.0 8.7 %shard_map.276 = bf16[1152,2152]{1,0:T(8,128)(2,1)S(1)} custom-call(bf16[1024,1152]{1,0:T(8,128)(2,1)S(1)} %pad_maximum_fusion.2.left, bf16[1024,2152]{1,0:T(8,128)(2,1)S(1)} %get-tuple-element.107.right), custom_call_target="tpu_custom_call" | custom-call | flops 5077204992 | bytes 11724800 | tf_op jit(solution)/shard_map/pallas_call | solution.py:244
  240.0 17.5 %all-gather.7.cloned.1.call-done = bf16[16,72,2152]{2,1,0:T(8,128)(2,1)} async-done(((bf16[2,72,2152]{2,1,0:T(8,128)(2,1)}), bf16[16,72,2152]{2,1,0:T(8,128)(2,1)}) %all-gather.7.cloned.1.call-update) | async-done | bytes 4958224 | tf_op jit(solution)/shard_map/all_gather | solution.py:405
  257.5 9.9 %multiply_convert_fusion.right = bf16[1024,2152]{1,0:T(8,128)(2,1)S(1)} fusion(bf16[1024,2152]{1,0:T(8,128)(2,1)} %get-tuple-element.93, bf16[1024,1152]{1,0:T(8,128)(2,1)S(1)} %pad_maximum_fusion.2.left, bf16[1152,2152]{1,0:T(8,128)(2,1)} %bitcast.174), kind=kOutput, calls=%fused_computation.1 | convolution fusion | flops 5083815936 | bytes 16132096 | tf_op jit(solution)/shard_map/dot_general | solution.py:697
  267.4 8.7 %shard_map.277 = bf16[1152,2152]{1,0:T(8,128)(2,1)S(1)} custom-call(bf16[1024,1152]{1,0:T(8,128)(2,1)S(1)} %copy-done.23, bf16[1024,2152]{1,0:T(8,128)(2,1)S(1)} %multiply_convert_fusion.right), custom_call_target="tpu_custom_call" | custom-call | flops 5077204992 | bytes 11724800 | tf_op jit(solution)/shard_map/pallas_call | solution.py:244
  280.4 10.9 %fusion.60 = (bf16[1024,1152]{1,0:T(8,128)(2,1)S(1)}, f32[1024,1152]{1,0:T(8,128)}) fusion(bf16[1024,2152]{1,0:T(8,128)(2,1)} %copy-done.15, bf16[1152,2152]{1,0:T(8,128)(2,1)} %bitcast.173), kind=kOutput, calls=%fused_computation.210 | convolution fusion | flops 5078384640 | bytes 16443392 | tf_op jit(solution)/shard_map/dot_general | solution.py:702
  298.2 3.4 convolution_convert_fusion.1
  307.0 5.8 multiply_reduce_fusion.2
  325.3 24.7 %shard_map.280 = (bf16[1,512,576]{2,1,0:T(8,128)(2,1)}, bf16[1,512,576]{2,1,0:T(8,128)(2,1)}, bf16[1,512,576]{2,1,0:T(8,128)(2,1)}, bf16[1,512,576]{2,1,0:T(8,128)(2,1)}, bf16[1,512,576]{2,1,0:T(8,128)(2,1)}) custom-call(s32[3]{0:T(128)} %copy-done.43, bf16[1,512,576]{2,1,0:T(8,128)(2,1)} %copy-done.35, bf16[1,512,576]{2,1,0:T(8,128)(2,1)} %get-tuple-element.173.refs_1_, ...), custom_call_target="tpu_custom_call" | custom-call | flops 10737418240 | bytes 7077888 | tf_op jit(solution)/shard_map/pallas_call | solution.py:203
  354.3 24.9 %shard_map.281 = (bf16[1,512,576]{2,1,0:T(8,128)(2,1)}, bf16[1,512,576]{2,1,0:T(8,128)(2,1)}, bf16[1,512,576]{2,1,0:T(8,128)(2,1)}, bf16[1,512,576]{2,1,0:T(8,128)(2,1)}, bf16[1,512,576]{2,1,0:T(8,128)(2,1)}) custom-call(s32[3]{0:T(128)} %copy-done.42, bf16[1,512,576]{2,1,0:T(8,128)(2,1)} %copy-done.34, bf16[1,512,576]{2,1,0:T(8,128)(2,1)} %get-tuple-element.174.refs_1_, ...), custom_call_target="tpu_custom_call" | custom-call | flops 10737418240 | bytes 7077888 | tf_op jit(solution)/shard_map/pallas_call | solution.py:203
  388.5 8.7 %fusion.61 = f32[1024,1152]{1,0:T(8,128)S(1)} fusion(bf16[1024,2152]{1,0:T(8,128)(2,1)S(1)} %bitcast.149, bf16[1152,2152]{1,0:T(8,128)(2,1)} %bitcast.175), kind=kOutput, calls=%fused_computation.211 | convolution fusion | flops 5077204992 | bytes 14084096 | tf_op jit(solution)/shard_map/dot_general | solution.py:759
  406.6 4.2 fusion.33
  410.8 18.6 %collective-permute-done.26 = bf16[1,512,1152]{2,1,0:T(8,128)(2,1)} collective-permute-done((bf16[1,512,1152]{2,1,0:T(8,128)(2,1)}, bf16[1,512,1152]{2,1,0:T(8,128)(2,1)}, u32[]{:S(2)}, u32[]{:S(2)}) %collective-permute-start.26) | collective-permute-done | bytes 1179680 | tf_op jit(solution)/shard_map/ppermute | solution.py:494
  449.3 3.7 fusion.62
  461.3 10.0 %collective-permute-done.37 = bf16[576,576]{1,0:T(8,128)(2,1)} collective-permute-done((bf16[576,576]{1,0:T(8,128)(2,1)}, bf16[576,576]{1,0:T(8,128)(2,1)}, u32[]{:S(2)}, u32[]{:S(2)}) %collective-permute-start.37) | collective-permute-done | bytes 663584 | tf_op jit(solution)/shard_map/ppermute | solution.py:362
  472.9 3.8 collective-permute-start.55
  481.8 3.3 collective-permute-done.55
  485.7 12.9 %collective-permute-done.54 = bf16[72,1152]{1,0:T(8,128)(2,1)S(1)} collective-permute-done((bf16[72,1152]{1,0:T(8,128)(2,1)S(1)}, bf16[72,1152]{1,0:T(8,128)(2,1)S(1)}, u32[]{:S(2)}, u32[]{:S(2)}) %collective-permute-start.54) | collective-permute-done | bytes 165920 | tf_op jit(solution)/shard_map/ppermute | solution.py:362
  499.6 10.7 %collective-permute-start.48 = (bf16[144,576]{1,0:T(8,128)(2,1)S(1)}, bf16[144,576]{1,0:T(8,128)(2,1)S(1)}, u32[]{:S(2)}, u32[]{:S(2)}) collective-permute-start(bf16[144,576]{1,0:T(8,128)(2,1)S(1)} %get-tuple-element.162), channel_id=1, source_target_pairs={{0,8},{2,10},{4,12},{6,14},{8,16},{10,18},{12,20},{14,22},{16,24},... | collective-permute-start | bytes 497672 | tf_op jit(solution)/shard_map/ppermute | solution.py:362
  510.3 23.7 %collective-permute-done.40 = bf16[144,576]{1,0:T(8,128)(2,1)S(1)} collective-permute-done((bf16[144,576]{1,0:T(8,128)(2,1)S(1)}, bf16[144,576]{1,0:T(8,128)(2,1)S(1)}, u32[]{:S(2)}, u32[]{:S(2)}) %collective-permute-start.40) | collective-permute-done | bytes 165920 | tf_op jit(solution)/shard_map/ppermute | solution.py:362
  536.5 4.9 collective-permute-done.49
  546.2 3.8 collective-permute-start.46
  556.9 11.2 %collective-permute-done.47 = bf16[72,576]{1,0:T(8,128)(2,1)S(1)} collective-permute-done((bf16[72,576]{1,0:T(8,128)(2,1)S(1)}, bf16[72,576]{1,0:T(8,128)(2,1)S(1)}, u32[]{:S(2)}, u32[]{:S(2)}) %collective-permute-start.47) | collective-permute-done | bytes 82976 | tf_op jit(solution)/shard_map/ppermute | solution.py:494
  569.0 3.5 multiply_reduce_fusion.3
  575.5 4.5 fusion.14
  587.6 3.9 collective-permute-done.32
  593.1 3.7 reshape.630
  (458 shorter events, 187.9 us)
Async XLA Ops:
  7.2 207.0 %all-gather.5.cloned.1.call-start = ((), (), s32[]{:S(2)}) async-start(), calls=%async_computation.4 | async-start | bytes 5640192 | tf_op jit(solution)/shard_map/all_gather | solution.py:405
  14.7 22.8 %collective-permute-start = (bf16[512,1152]{1,0:T(8,128)(2,1)S(1)}, bf16[512,1152]{1,0:T(8,128)(2,1)S(1)}, u32[]{:S(2)}, u32[]{:S(2)}) collective-permute-start(bf16[512,1152]{1,0:T(8,128)(2,1)S(1)} %bitcast.154), channel_id=1, source_target_pairs={{0,2},{2,0},{4,6},{6,4},{8,10},{10,8},{12,14},{14,12},{16,18},{18,... | collective-permute-start | bytes 3538952 | tf_op jit(solution)/shard_map/ppermute | solution.py:362
  18.9 12.3 %collective-permute-start.3 = (bf16[1,72,1152]{2,1,0:T(8,128)(2,1)S(1)}, bf16[1,72,1152]{2,1,0:T(8,128)(2,1)S(1)}, u32[]{:S(2)}, u32[]{:S(2)}) collective-permute-start(bf16[1,72,1152]{2,1,0:T(8,128)(2,1)S(1)} %slice_select_fusion.2), channel_id=1, source_target_pairs={{0,16},{2,18},{4,20},{6,22},{8,24},{10,26},{12,28},{14,30},{16,0},... | collective-permute-start | bytes 497672 | tf_op jit(solution)/shard_map/ppermute | solution.py:362
  22.6 8.8 %collective-permute-start.2 = (bf16[1,72,1152]{2,1,0:T(8,128)(2,1)S(1)}, bf16[1,72,1152]{2,1,0:T(8,128)(2,1)S(1)}, u32[]{:S(2)}, u32[]{:S(2)}) collective-permute-start(bf16[1,72,1152]{2,1,0:T(8,128)(2,1)S(1)} %slice_select_fusion.2), channel_id=1, source_target_pairs={{0,24},{2,26},{4,28},{6,30},{8,0},{10,2},{12,4},{14,6},{16,8},{18,... | collective-permute-start | bytes 497672 | tf_op jit(solution)/shard_map/ppermute | solution.py:362
  23.9 11.9 %collective-permute-start.4 = (bf16[1,72,1152]{2,1,0:T(8,128)(2,1)S(1)}, bf16[1,72,1152]{2,1,0:T(8,128)(2,1)S(1)}, u32[]{:S(2)}, u32[]{:S(2)}) collective-permute-start(bf16[1,72,1152]{2,1,0:T(8,128)(2,1)S(1)} %slice_select_fusion.2), channel_id=1, source_target_pairs={{0,8},{2,10},{4,12},{6,14},{8,16},{10,18},{12,20},{14,22},{16,24},... | collective-permute-start | bytes 497672 | tf_op jit(solution)/shard_map/ppermute | solution.py:362
  26.0 9.9 %collective-permute-start.6 = (bf16[72,2152]{1,0:T(8,128)(2,1)S(1)}, bf16[72,2152]{1,0:T(8,128)(2,1)S(1)}, u32[]{:S(2)}, u32[]{:S(2)}) collective-permute-start(bf16[72,2152]{1,0:T(8,128)(2,1)S(1)} %broadcast_select_fusion.2), channel_id=1, source_target_pairs={{0,2},{2,0},{4,6},{6,4},{8,10},{10,8},{12,14},{14,12},{16,18},{18,... | collective-permute-start | bytes 929672 | tf_op jit(solution)/shard_map/ppermute | solution.py:362
  42.6 16.5 %collective-permute-start.8 = (bf16[4,1,72,1152]{3,2,1,0:T(8,128)(2,1)S(1)}, bf16[4,1,72,1152]{3,2,1,0:T(8,128)(2,1)S(1)}, u32[]{:S(2)}, u32[]{:S(2)}) collective-permute-start(bf16[4,1,72,1152]{3,2,1,0:T(8,128)(2,1)S(1)} %pad_maximum_fusion.13.refs_0_), channel_id=1, source_target_pairs={{0,4},{2,6},{4,0},{6,2},{8,12},{10,14},{12,8},{14,10},{16,20},{18,... | collective-permute-start | bytes 1990664 | tf_op jit(solution)/shard_map/ppermute | solution.py:362
  59.1 198.4 %all-gather.7.cloned.1.call-start = ((), (), s32[]{:S(2)}) async-start(), calls=%async_computation.5 | async-start | bytes 5640192 | tf_op jit(solution)/shard_map/all_gather | solution.py:405
  62.1 33.2 %collective-permute-start.13 = (bf16[4,1,72,1152]{3,2,1,0:T(8,128)(2,1)S(1)}, bf16[4,1,72,1152]{3,2,1,0:T(8,128)(2,1)S(1)}, u32[]{:S(2)}, u32[]{:S(2)}) collective-permute-start(bf16[4,1,72,1152]{3,2,1,0:T(8,128)(2,1)S(1)} %pad_maximum_fusion.13.refs_0_), channel_id=1, source_target_pairs={{0,1},{1,0},{2,3},{3,2},{4,5},{5,4},{6,7},{7,6},{8,9},{9,8},{10,11... | collective-permute-start | bytes 1990664 | tf_op jit(solution)/shard_map/ppermute | solution.py:494
  63.6 31.7 %collective-permute-start.14 = (bf16[4,1,72,1152]{3,2,1,0:T(8,128)(2,1)S(1)}, bf16[4,1,72,1152]{3,2,1,0:T(8,128)(2,1)S(1)}, u32[]{:S(2)}, u32[]{:S(2)}) collective-permute-start(bf16[4,1,72,1152]{3,2,1,0:T(8,128)(2,1)S(1)} %collective-permute-done.8.refs_1_), channel_id=1, source_target_pairs={{0,1},{1,0},{2,3},{3,2},{4,5},{5,4},{6,7},{7,6},{8,9},{9,8},{10,11... | collective-permute-start | bytes 1990664 | tf_op jit(solution)/shard_map/ppermute | solution.py:494
  67.5 12.2 %collective-permute-start.11 = (bf16[2,72,576]{2,1,0:T(8,128)(2,1)S(1)}, bf16[2,72,576]{2,1,0:T(8,128)(2,1)S(1)}, u32[]{:S(2)}, u32[]{:S(2)}) collective-permute-start(bf16[2,72,576]{2,1,0:T(8,128)(2,1)S(1)} %slice.352), channel_id=1, source_target_pairs={{0,8},{2,10},{4,12},{6,14},{8,16},{10,18},{12,20},{14,22},{16,24},... | collective-permute-start | bytes 497672 | tf_op jit(solution)/shard_map/ppermute | solution.py:362
  71.2 20.7 %collective-permute-start.10 = (bf16[2,72,576]{2,1,0:T(8,128)(2,1)S(1)}, bf16[2,72,576]{2,1,0:T(8,128)(2,1)S(1)}, u32[]{:S(2)}, u32[]{:S(2)}) collective-permute-start(bf16[2,72,576]{2,1,0:T(8,128)(2,1)S(1)} %slice.352), channel_id=1, source_target_pairs={{0,16},{2,18},{4,20},{6,22},{8,24},{10,26},{12,28},{14,30},{16,0},... | collective-permute-start | bytes 497672 | tf_op jit(solution)/shard_map/ppermute | solution.py:362
  73.2 20.7 %collective-permute-start.9 = (bf16[2,72,576]{2,1,0:T(8,128)(2,1)S(1)}, bf16[2,72,576]{2,1,0:T(8,128)(2,1)S(1)}, u32[]{:S(2)}, u32[]{:S(2)}) collective-permute-start(bf16[2,72,576]{2,1,0:T(8,128)(2,1)S(1)} %slice.352), channel_id=1, source_target_pairs={{0,24},{2,26},{4,28},{6,30},{8,0},{10,2},{12,4},{14,6},{16,8},{18,... | collective-permute-start | bytes 497672 | tf_op jit(solution)/shard_map/ppermute | solution.py:362
  94.0 31.1 %collective-permute-start.12 = (bf16[4,2,72,576]{3,2,1,0:T(8,128)(2,1)S(1)}, bf16[4,2,72,576]{3,2,1,0:T(8,128)(2,1)S(1)}, u32[]{:S(2)}, u32[]{:S(2)}) collective-permute-start(bf16[4,2,72,576]{3,2,1,0:T(8,128)(2,1)S(1)} %pad_maximum_fusion.12.refs_0_), channel_id=1, source_target_pairs={{0,4},{2,6},{4,0},{6,2},{8,12},{10,14},{12,8},{14,10},{16,20},{18,... | collective-permute-start | bytes 1990664 | tf_op jit(solution)/shard_map/ppermute | solution.py:362
  104.8 56.5 %collective-permute-start.15 = (bf16[1,512,1152]{2,1,0:T(8,128)(2,1)}, bf16[1,512,1152]{2,1,0:T(8,128)(2,1)}, u32[]{:S(2)}, u32[]{:S(2)}) collective-permute-start(bf16[1,512,1152]{2,1,0:T(8,128)(2,1)} %get-tuple-element.154), channel_id=1, source_target_pairs={{0,1},{1,0},{2,3},{3,2},{4,5},{5,4},{6,7},{7,6},{8,9},{9,8},{10,11... | collective-permute-start | bytes 3538952 | tf_op jit(solution)/shard_map/ppermute | solution.py:494
  106.4 56.6 %collective-permute-start.16 = (bf16[1,512,1152]{2,1,0:T(8,128)(2,1)}, bf16[1,512,1152]{2,1,0:T(8,128)(2,1)}, u32[]{:S(2)}, u32[]{:S(2)}) collective-permute-start(bf16[1,512,1152]{2,1,0:T(8,128)(2,1)} %get-tuple-element.155), channel_id=1, source_target_pairs={{0,1},{1,0},{2,3},{3,2},{4,5},{5,4},{6,7},{7,6},{8,9},{9,8},{10,11... | collective-permute-start | bytes 3538952 | tf_op jit(solution)/shard_map/ppermute | solution.py:494
  125.1 23.9 %collective-permute-start.19 = (bf16[1,72,1152]{2,1,0:T(8,128)(2,1)}, bf16[1,72,1152]{2,1,0:T(8,128)(2,1)}, u32[]{:S(2)}, u32[]{:S(2)}) collective-permute-start(bf16[1,72,1152]{2,1,0:T(8,128)(2,1)} %bitcast.33), channel_id=1, source_target_pairs={{0,8},{2,10},{4,12},{6,14},{8,16},{10,18},{12,20},{14,22},{16,24},... | collective-permute-start | bytes 497672 | tf_op jit(solution)/shard_map/ppermute | solution.py:362
  137.9 20.4 %collective-permute-start.18 = (bf16[1,72,1152]{2,1,0:T(8,128)(2,1)}, bf16[1,72,1152]{2,1,0:T(8,128)(2,1)}, u32[]{:S(2)}, u32[]{:S(2)}) collective-permute-start(bf16[1,72,1152]{2,1,0:T(8,128)(2,1)} %bitcast.33), channel_id=1, source_target_pairs={{0,16},{2,18},{4,20},{6,22},{8,24},{10,26},{12,28},{14,30},{16,0},... | collective-permute-start | bytes 497672 | tf_op jit(solution)/shard_map/ppermute | solution.py:362
  141.3 18.0 %collective-permute-start.17 = (bf16[1,72,1152]{2,1,0:T(8,128)(2,1)}, bf16[1,72,1152]{2,1,0:T(8,128)(2,1)}, u32[]{:S(2)}, u32[]{:S(2)}) collective-permute-start(bf16[1,72,1152]{2,1,0:T(8,128)(2,1)} %bitcast.33), channel_id=1, source_target_pairs={{0,24},{2,26},{4,28},{6,30},{8,0},{10,2},{12,4},{14,6},{16,8},{18,... | collective-permute-start | bytes 497672 | tf_op jit(solution)/shard_map/ppermute | solution.py:362
  143.9 285.5 %reduce-scatter.3.cloned.1.call-start = ((), (), s32[]{:S(2)}) async-start(), calls=%async_computation.2 | async-start | bytes 5640192 | tf_op jit(solution)/shard_map/reduce_scatter | solution.py:414
  160.5 20.0 %collective-permute-start.20 = (bf16[4,1,72,1152]{3,2,1,0:T(8,128)(2,1)S(1)}, bf16[4,1,72,1152]{3,2,1,0:T(8,128)(2,1)S(1)}, u32[]{:S(2)}, u32[]{:S(2)}) collective-permute-start(bf16[4,1,72,1152]{3,2,1,0:T(8,128)(2,1)S(1)} %pad_maximum_fusion.14.refs_0_), channel_id=1, source_target_pairs={{0,4},{2,6},{4,0},{6,2},{8,12},{10,14},{12,8},{14,10},{16,20},{18,... | collective-permute-start | bytes 1990664 | tf_op jit(solution)/shard_map/ppermute | solution.py:362
  293.1 13.9 %collective-permute-start.23 = (bf16[1024,1152]{1,0:T(8,128)(2,1)}, bf16[1024,1152]{1,0:T(8,128)(2,1)}, u32[]{:S(2)}, u32[]{:S(2)}) collective-permute-start(bf16[1024,1152]{1,0:T(8,128)(2,1)} %pad_maximum_fusion.3), channel_id=1, source_target_pairs={{0,2},{2,0},{4,6},{6,4},{8,10},{10,8},{12,14},{14,12},{16,18},{18,... | collective-permute-start | bytes 7077896 | tf_op jit(solution)/shard_map/ppermute | solution.py:362
  293.1 257.7 %reduce-scatter.5.cloned.1.call-start = ((), (), s32[]{:S(2)}) async-start(), calls=%async_computation.3 | async-start | bytes 5640192 | tf_op jit(solution)/shard_map/reduce_scatter | solution.py:414
  352.7 29.4 %collective-permute-start.24 = (bf16[1,512,1152]{2,1,0:T(8,128)(2,1)}, bf16[1,512,1152]{2,1,0:T(8,128)(2,1)S(1)}, u32[]{:S(2)}, u32[]{:S(2)}) collective-permute-start(bf16[1,512,1152]{2,1,0:T(8,128)(2,1)} %pad_maximum_fusion.10), channel_id=1, source_target_pairs={{0,1},{1,0},{2,3},{3,2},{4,5},{5,4},{6,7},{7,6},{8,9},{9,8},{10,11... | collective-permute-start | bytes 3538952 | tf_op jit(solution)/shard_map/ppermute | solution.py:494
  400.6 60.5 %collective-permute-start.34 = (bf16[288,1152]{1,0:T(8,128)(2,1)}, bf16[288,1152]{1,0:T(8,128)(2,1)}, u32[]{:S(2)}, u32[]{:S(2)}) collective-permute-start(bf16[288,1152]{1,0:T(8,128)(2,1)} %copy-done.29), channel_id=1, source_target_pairs={{0,4},{2,6},{4,0},{6,2},{8,12},{10,14},{12,8},{14,10},{16,20},{18,... | collective-permute-start | bytes 1990664 | tf_op jit(solution)/shard_map/ppermute | solution.py:362
  400.7 28.7 %collective-permute-start.26 = (bf16[1,512,1152]{2,1,0:T(8,128)(2,1)}, bf16[1,512,1152]{2,1,0:T(8,128)(2,1)}, u32[]{:S(2)}, u32[]{:S(2)}) collective-permute-start(bf16[1,512,1152]{2,1,0:T(8,128)(2,1)} %pad_maximum_fusion.11), channel_id=1, source_target_pairs={{0,1},{1,0},{2,3},{3,2},{4,5},{5,4},{6,7},{7,6},{8,9},{9,8},{10,11... | collective-permute-start | bytes 3538952 | tf_op jit(solution)/shard_map/ppermute | solution.py:494
  404.2 56.9 %collective-permute-start.35 = (bf16[576,576]{1,0:T(8,128)(2,1)}, bf16[576,576]{1,0:T(8,128)(2,1)}, u32[]{:S(2)}, u32[]{:S(2)}) collective-permute-start(bf16[576,576]{1,0:T(8,128)(2,1)} %shard_map.283), channel_id=1, source_target_pairs={{0,4},{2,6},{4,0},{6,2},{8,12},{10,14},{12,8},{14,10},{16,20},{18,... | collective-permute-start | bytes 1990664 | tf_op jit(solution)/shard_map/ppermute | solution.py:362
  429.4 29.7 %collective-permute-start.38 = (bf16[144,2152]{1,0:T(8,128)(2,1)}, bf16[144,2152]{1,0:T(8,128)(2,1)}, u32[]{:S(2)}, u32[]{:S(2)}) collective-permute-start(bf16[144,2152]{1,0:T(8,128)(2,1)} %reduce-scatter.3.cloned.1.call-done), channel_id=1, source_target_pairs={{0,1},{1,0},{2,3},{3,2},{4,5},{5,4},{6,7},{7,6},{8,9},{9,8},{10,11... | collective-permute-start | bytes 1859336 | tf_op jit(solution)/shard_map/ppermute | solution.py:545
  434.8 26.5 %collective-permute-start.36 = (bf16[576,576]{1,0:T(8,128)(2,1)}, bf16[576,576]{1,0:T(8,128)(2,1)}, u32[]{:S(2)}, u32[]{:S(2)}) collective-permute-start(bf16[576,576]{1,0:T(8,128)(2,1)} %shard_map.285), channel_id=1, source_target_pairs={{0,1},{1,0},{2,3},{3,2},{4,5},{5,4},{6,7},{7,6},{8,9},{9,8},{10,11... | collective-permute-start | bytes 1990664 | tf_op jit(solution)/shard_map/ppermute | solution.py:494
  439.4 31.9 %collective-permute-start.37 = (bf16[576,576]{1,0:T(8,128)(2,1)}, bf16[576,576]{1,0:T(8,128)(2,1)}, u32[]{:S(2)}, u32[]{:S(2)}) collective-permute-start(bf16[576,576]{1,0:T(8,128)(2,1)} %shard_map.287), channel_id=1, source_target_pairs={{0,4},{2,6},{4,0},{6,2},{8,12},{10,14},{12,8},{14,10},{16,20},{18,... | collective-permute-start | bytes 1990664 | tf_op jit(solution)/shard_map/ppermute | solution.py:362
  459.1 109.8 %collective-permute-start.27 = (bf16[512,1152]{1,0:T(8,128)(2,1)}, bf16[512,1152]{1,0:T(8,128)(2,1)S(1)}, u32[]{:S(2)}, u32[]{:S(2)}) collective-permute-start(bf16[512,1152]{1,0:T(8,128)(2,1)} %slice.683), channel_id=1, source_target_pairs={{0,2},{2,0},{4,6},{6,4},{8,10},{10,8},{12,14},{14,12},{16,18},{18,... | collective-permute-start | bytes 3538952 | tf_op jit(solution)/shard_map/ppermute | solution.py:362
  471.4 71.7 %collective-permute-start.58 = (bf16[72,2152]{1,0:T(8,128)(2,1)S(1)}, bf16[72,2152]{1,0:T(8,128)(2,1)S(1)}, u32[]{:S(2)}, u32[]{:S(2)}) collective-permute-start(bf16[72,2152]{1,0:T(8,128)(2,1)S(1)} %select_convert_fusion), channel_id=1, source_target_pairs={{0,2},{2,0},{4,6},{6,4},{8,10},{10,8},{12,14},{14,12},{16,18},{18,... | collective-permute-start | bytes 929672 | tf_op jit(solution)/shard_map/ppermute | solution.py:362
  472.8 9.0 %collective-permute-start.53 = (bf16[72,1152]{1,0:T(8,128)(2,1)S(1)}, bf16[72,1152]{1,0:T(8,128)(2,1)S(1)}, u32[]{:S(2)}, u32[]{:S(2)}) collective-permute-start(bf16[72,1152]{1,0:T(8,128)(2,1)S(1)} %get-tuple-element.170), channel_id=1, source_target_pairs={{0,8},{2,10},{4,12},{6,14},{8,16},{10,18},{12,20},{14,22},{16,24},... | collective-permute-start | bytes 497672 | tf_op jit(solution)/shard_map/ppermute | solution.py:362
  472.9 12.3 %collective-permute-start.55 = (bf16[72,1152]{1,0:T(8,128)(2,1)S(1)}, bf16[72,1152]{1,0:T(8,128)(2,1)S(1)}, u32[]{:S(2)}, u32[]{:S(2)}) collective-permute-start(bf16[72,1152]{1,0:T(8,128)(2,1)S(1)} %get-tuple-element.171), channel_id=1, source_target_pairs={{0,24},{2,26},{4,28},{6,30},{8,0},{10,2},{12,4},{14,6},{16,8},{18,... | collective-permute-start | bytes 497672 | tf_op jit(solution)/shard_map/ppermute | solution.py:362
  476.7 21.9 %collective-permute-start.54 = (bf16[72,1152]{1,0:T(8,128)(2,1)S(1)}, bf16[72,1152]{1,0:T(8,128)(2,1)S(1)}, u32[]{:S(2)}, u32[]{:S(2)}) collective-permute-start(bf16[72,1152]{1,0:T(8,128)(2,1)S(1)} %get-tuple-element.172), channel_id=1, source_target_pairs={{0,16},{2,18},{4,20},{6,22},{8,24},{10,26},{12,28},{14,30},{16,0},... | collective-permute-start | bytes 497672 | tf_op jit(solution)/shard_map/ppermute | solution.py:362
  481.8 17.8 %collective-permute-start.39 = (bf16[144,576]{1,0:T(8,128)(2,1)S(1)}, bf16[144,576]{1,0:T(8,128)(2,1)S(1)}, u32[]{:S(2)}, u32[]{:S(2)}) collective-permute-start(bf16[144,576]{1,0:T(8,128)(2,1)S(1)} %get-tuple-element.167), channel_id=1, source_target_pairs={{0,8},{2,10},{4,12},{6,14},{8,16},{10,18},{12,20},{14,22},{16,24},... | collective-permute-start | bytes 497672 | tf_op jit(solution)/shard_map/ppermute | solution.py:362
  485.1 25.2 %collective-permute-start.41 = (bf16[144,576]{1,0:T(8,128)(2,1)S(1)}, bf16[144,576]{1,0:T(8,128)(2,1)S(1)}, u32[]{:S(2)}, u32[]{:S(2)}) collective-permute-start(bf16[144,576]{1,0:T(8,128)(2,1)S(1)} %get-tuple-element.168), channel_id=1, source_target_pairs={{0,24},{2,26},{4,28},{6,30},{8,0},{10,2},{12,4},{14,6},{16,8},{18,... | collective-permute-start | bytes 497672 | tf_op jit(solution)/shard_map/ppermute | solution.py:362
  498.6 35.5 %collective-permute-start.40 = (bf16[144,576]{1,0:T(8,128)(2,1)S(1)}, bf16[144,576]{1,0:T(8,128)(2,1)S(1)}, u32[]{:S(2)}, u32[]{:S(2)}) collective-permute-start(bf16[144,576]{1,0:T(8,128)(2,1)S(1)} %get-tuple-element.169), channel_id=1, source_target_pairs={{0,16},{2,18},{4,20},{6,22},{8,24},{10,26},{12,28},{14,30},{16,0},... | collective-permute-start | bytes 497672 | tf_op jit(solution)/shard_map/ppermute | solution.py:362
  499.6 35.5 %collective-permute-start.48 = (bf16[144,576]{1,0:T(8,128)(2,1)S(1)}, bf16[144,576]{1,0:T(8,128)(2,1)S(1)}, u32[]{:S(2)}, u32[]{:S(2)}) collective-permute-start(bf16[144,576]{1,0:T(8,128)(2,1)S(1)} %get-tuple-element.162), channel_id=1, source_target_pairs={{0,8},{2,10},{4,12},{6,14},{8,16},{10,18},{12,20},{14,22},{16,24},... | collective-permute-start | bytes 497672 | tf_op jit(solution)/shard_map/ppermute | solution.py:362
  510.3 25.7 %collective-permute-start.50 = (bf16[144,576]{1,0:T(8,128)(2,1)S(1)}, bf16[144,576]{1,0:T(8,128)(2,1)S(1)}, u32[]{:S(2)}, u32[]{:S(2)}) collective-permute-start(bf16[144,576]{1,0:T(8,128)(2,1)S(1)} %get-tuple-element.163), channel_id=1, source_target_pairs={{0,24},{2,26},{4,28},{6,30},{8,0},{10,2},{12,4},{14,6},{16,8},{18,... | collective-permute-start | bytes 497672 | tf_op jit(solution)/shard_map/ppermute | solution.py:362
  535.1 10.9 %collective-permute-start.43 = (bf16[288,576]{1,0:T(8,128)(2,1)S(1)}, bf16[288,576]{1,0:T(8,128)(2,1)S(1)}, u32[]{:S(2)}, u32[]{:S(2)}) collective-permute-start(bf16[288,576]{1,0:T(8,128)(2,1)S(1)} %get-tuple-element.166), channel_id=1, source_target_pairs={{0,4},{2,6},{4,0},{6,2},{8,12},{10,14},{12,8},{14,10},{16,20},{18,... | collective-permute-start | bytes 995336 | tf_op jit(solution)/shard_map/ppermute | solution.py:362
  536.0 10.2 %collective-permute-start.56 = (bf16[72,1152]{1,0:T(8,128)(2,1)S(1)}, bf16[72,1152]{1,0:T(8,128)(2,1)S(1)}, u32[]{:S(2)}, u32[]{:S(2)}) collective-permute-start(bf16[72,1152]{1,0:T(8,128)(2,1)S(1)} %add_convert_fusion.21), channel_id=1, source_target_pairs={{0,1},{1,0},{2,3},{3,2},{4,5},{5,4},{6,7},{7,6},{8,9},{9,8},{10,11... | collective-permute-start | bytes 497672 | tf_op jit(solution)/shard_map/ppermute | solution.py:545
  541.5 9.3 %collective-permute-start.42 = (bf16[144,576]{1,0:T(8,128)(2,1)S(1)}, bf16[144,576]{1,0:T(8,128)(2,1)S(1)}, u32[]{:S(2)}, u32[]{:S(2)}) collective-permute-start(bf16[144,576]{1,0:T(8,128)(2,1)S(1)} %add_convert_fusion.16), channel_id=1, source_target_pairs={{0,1},{1,0},{2,3},{3,2},{4,5},{5,4},{6,7},{7,6},{8,9},{9,8},{10,11... | collective-permute-start | bytes 497672 | tf_op jit(solution)/shard_map/ppermute | solution.py:545
  543.1 13.8 %collective-permute-start.51 = (bf16[144,576]{1,0:T(8,128)(2,1)S(1)}, bf16[144,576]{1,0:T(8,128)(2,1)S(1)}, u32[]{:S(2)}, u32[]{:S(2)}) collective-permute-start(bf16[144,576]{1,0:T(8,128)(2,1)S(1)} %add_convert_fusion.11), channel_id=1, source_target_pairs={{0,1},{1,0},{2,3},{3,2},{4,5},{5,4},{6,7},{7,6},{8,9},{9,8},{10,11... | collective-permute-start | bytes 497672 | tf_op jit(solution)/shard_map/ppermute | solution.py:545
  553.0 19.6 %collective-permute-start.28 = (bf16[144,2152]{1,0:T(8,128)(2,1)}, bf16[144,2152]{1,0:T(8,128)(2,1)}, u32[]{:S(2)}, u32[]{:S(2)}) collective-permute-start(bf16[144,2152]{1,0:T(8,128)(2,1)} %reduce-scatter.5.cloned.1.call-done), channel_id=1, source_target_pairs={{0,1},{1,0},{2,3},{3,2},{4,5},{5,4},{6,7},{7,6},{8,9},{9,8},{10,11... | collective-permute-start | bytes 1859336 | tf_op jit(solution)/shard_map/ppermute | solution.py:545
  556.3 11.8 %collective-permute-start.47 = (bf16[72,576]{1,0:T(8,128)(2,1)S(1)}, bf16[72,576]{1,0:T(8,128)(2,1)S(1)}, u32[]{:S(2)}, u32[]{:S(2)}) collective-permute-start(bf16[72,576]{1,0:T(8,128)(2,1)S(1)} %add_convert_fusion.26), channel_id=1, source_target_pairs={{0,1},{1,0},{2,3},{3,2},{4,5},{5,4},{6,7},{7,6},{8,9},{9,8},{10,11... | collective-permute-start | bytes 248840 | tf_op jit(solution)/shard_map/ppermute | solution.py:494
  568.8 11.3 %collective-permute-start.52 = (bf16[72,1728]{1,0:T(8,128)(2,1)S(1)}, bf16[72,1728]{1,0:T(8,128)(2,1)S(1)}, u32[]{:S(2)}, u32[]{:S(2)}) collective-permute-start(bf16[72,1728]{1,0:T(8,128)(2,1)S(1)} %slice.685), channel_id=1, source_target_pairs={{0,2},{2,0},{4,6},{6,4},{8,10},{10,8},{12,14},{14,12},{16,18},{18,... | collective-permute-start | bytes 746504 | tf_op jit(solution)/shard_map/ppermute | solution.py:362
  587.6 10.4 %collective-permute-start.57 = (bf16[72,2152]{1,0:T(8,128)(2,1)}, bf16[72,2152]{1,0:T(8,128)(2,1)S(1)}, u32[]{:S(2)}, u32[]{:S(2)}) collective-permute-start(bf16[72,2152]{1,0:T(8,128)(2,1)} %select_convert_fusion.1), channel_id=1, source_target_pairs={{0,2},{2,0},{4,6},{6,4},{8,10},{10,8},{12,14},{14,12},{16,18},{18,... | collective-permute-start | bytes 929672 | tf_op jit(solution)/shard_map/ppermute | solution.py:362
  (108 other events, 1405.5 us)
Sparse Core Ops, SparseCore 0:
  59.3 113.5 all-gather.4
  175.0 82.4 all-gather.6
  293.3 98.2 reduce-scatter.2
  400.7 135.0 reduce-scatter.4
